TPU v7x, 32 devices: a whole 2x2x4 slice. The times are simulated.
32 devices in a mesh: region: 4 (over z), col: 8 (over y, x, core).
Axes of the slice: x: 2, y: 2, z: 4, core: 2. Of those that a mesh axis runs over, the one named last changes fastest.
Arguments:
- forcing: float32 [3, 256, 1024], P(None, 'region', 'col'), may hold values from 0.05 to 3
- river_storage: float32 [256, 1024], P('region', 'col'), may hold values from 0.1 to 4
- river_rate: float32 [256, 1024], P('region', 'col'), may hold values from 0.2 to 0.9
- flow_code: int32 [256, 1024], P('region', 'col'), may hold values from 1 to 128
- home_slot: int32 [32, 1024], P(('region', 'col')), may hold values from -1 to 1023, as said below
- home_offset: int32 [32, 1024], P(('region', 'col')), may hold values from 0 to 8184, as said below
- worker_list: int32 [15360], P(('region', 'col')), may hold values from 0 to 1023, as said below
- patch_cell: int32 [15360, 128], P(('region', 'col')), may hold values from 0 to 63, as said below
- patch_area: float32 [15360, 128], P(('region', 'col')), may hold values from 0.02 to 0.3
- canopy_water: float32 [15360, 128], P(('region', 'col')), may hold values from 0 to 1
- canopy_cap: float32 [15360, 128], P(('region', 'col')), may hold values from 0.1 to 2
- soil_water: float32 [15, 15360, 128], P(None, ('region', 'col')), may hold values from 0.05 to 0.5
- porosity: float32 [15, 15360, 128], P(None, ('region', 'col')), may hold values from 0.3 to 0.55
- drainage: float32 [15, 15360, 128], P(None, ('region', 'col')), may hold values from 0.02 to 0.8
Outputs:
- soil_new: float32 [15, 15360, 128], P(None, ('region', 'col'))
- canopy_new: float32 [15360, 128], P(('region', 'col'))
- cell_runoff: float32 [256, 1024], P('region', 'col')
- cell_evap: float32 [256, 1024], P('region', 'col')
- river_new: float32 [256, 1024], P('region', 'col')
Inputs may be any that keep to these rules, and one draw needn't show every extreme that they name: `home_slot`: A home's live block slots come first and hold w * 32 + k (worker w, position k), distinct within the home; -1 marks unused slots. A home has 1024, 512, 256 or 128 live blocks, each for a quarter of the homes; at most 32 of one home's blocks go to one worker, and the busiest homes send exactly 32 to every worker. `worker_list`: every slot of every worker holds a live block; h * 32 + k at block b of worker w means home_slot[h, j] = w * 32 + k for exactly one j. `home_offset`: the first home cell of a live block, row-major over the home's cells; 0 for unused slots. Offset plus patch_cell stays below 8192. `patch_cell`: never falling along a block.
All inputs are finite; a program needn't handle non-finite values.
Results may differ from a plain program's by a relative error of at most 0.000073.
Values sent between devices are 32-bit elements; how exact they have to be, the bound alone decides.
No kernel may reach another device: no remote copies, remote signals or barrier semaphores. Data moves between devices by JAX's collectives and lax.ppermute only.
A program may use at most 64 MiB of HBM per device.

v0:
```python
import functools

import jax
import jax.numpy as jnp
from jax import lax
from jax.experimental import pallas as pl
from jax.experimental.pallas import tpu as pltpu
from jax.sharding import PartitionSpec as P

ITERS = 4
WINDOW = 64
LANES = 128
MIB = 1024 * 1024
VMEM_LIMIT = 24 * MIB

directions = ((0, 1), (1, 1), (1, 0), (1, -1), (0, -1), (-1, -1), (-1, 0), (-1, 1))
axes = ("region", "col")


def iota(shape, dim):
    return lax.broadcasted_iota(jnp.int32, shape, dim)


def onehot(mask):
    return jnp.where(mask, jnp.float32(1.0), jnp.float32(0.0)).astype(jnp.bfloat16)


def lane_pick(values, index):
    return jnp.take_along_axis(values, index, axis=1, mode="promise_in_bounds")


def in_hbm(value):
    return pltpu.with_memory_space_constraint(value, pltpu.HBM)


def thirds(value):
    high = value.astype(jnp.bfloat16)
    rest = value - high.astype(jnp.float32)
    middle = rest.astype(jnp.bfloat16)
    low = (rest - middle.astype(jnp.float32)).astype(jnp.bfloat16)
    return high, middle, low


def halves(value):
    high = value.astype(jnp.bfloat16)
    return high, (value - high.astype(jnp.float32)).astype(jnp.bfloat16)


def matmul(a, b, a_dim=1, b_dim=0):
    return lax.dot_general(
        a, b, (((a_dim,), (b_dim,)), ((), ())), preferred_element_type=jnp.float32
    )


def slot_factors(slot, offset, homes, capacity):
    slots = slot.shape[1]
    worker = slot // capacity if capacity & (capacity - 1) else slot >> (capacity.bit_length() - 1)
    position = slot - worker * capacity
    by_worker = onehot(iota((homes, slots), 0) == worker)
    at_position = iota((capacity, slots), 0) == position
    row = jnp.where(at_position, ((offset >> 7) + 1).astype(jnp.float32), 0.0)
    lane = jnp.where(at_position, (offset & 127).astype(jnp.float32), 0.0)
    return by_worker, row.astype(jnp.bfloat16), lane.astype(jnp.bfloat16)


def slot_columns(slot, offset, homes, capacity, split=False):
    slots = slot.shape[1]
    by_worker, row, lane = slot_factors(slot, offset, homes, capacity)
    table = matmul(by_worker, jnp.concatenate([row, lane], axis=0), 1, 1)
    groups = 2 if split else 1
    spread = jnp.broadcast_to(
        table[:, None, :], (homes, capacity // groups, 2 * capacity)
    ).reshape(slots // groups, 2 * capacity)
    spread = jnp.concatenate([spread] * groups, axis=0)
    number = iota(spread.shape, 0)
    position = number % (capacity // groups) * groups + number // (slots // groups)
    place = position == iota(spread.shape, 1) % capacity
    kept = jnp.where(place, spread, 0.0).astype(jnp.bfloat16)
    shape = (2 * capacity, 2 * LANES)
    gather = onehot((iota(shape, 0) >= capacity) == (iota(shape, 1) >= LANES))
    columns = matmul(kept, gather).astype(jnp.int32)
    return columns[:, :LANES] - 1, columns[:, LANES:]


def slot_rows(slot, offset, homes, capacity):
    slots = slot.shape[1]
    by_worker, row, lane = slot_factors(slot, offset, homes, capacity)
    table = matmul(jnp.concatenate([row, lane], axis=0), by_worker, 1, 1).astype(jnp.bfloat16)
    number = iota((1, slots), 1)
    worker = number // capacity
    position = number - worker * capacity
    spread = matmul(table, onehot(iota((homes, slots), 0) == worker))
    at_position = iota((capacity, slots), 0) == position
    rows = jnp.sum(jnp.where(at_position, spread[:capacity], 0.0), axis=0, keepdims=True)
    lanes = jnp.sum(jnp.where(at_position, spread[capacity:], 0.0), axis=0, keepdims=True)
    return rows.astype(jnp.int32) - 1, lanes.astype(jnp.int32)


def pack_kernel(
    homes, capacity, slot_in, offset_in, forcing_in, out, slot, offset, forcing, row_of, lane_of,
    rain, ready,
):
    copies = [
        pltpu.make_async_copy(source, target, ready.at[i])
        for i, (source, target) in enumerate(
            ((slot_in, slot), (offset_in, offset), (forcing_in, forcing))
        )
    ]
    for copy in copies:
        copy.start()
    slots = slot.shape[1]
    pairs = capacity // 2
    lane_rows = forcing.shape[1]
    copies[0].wait()
    copies[1].wait()
    row_of[...], lane_of[...] = slot_columns(slot[...], offset[...], homes, capacity, True)
    copies[2].wait()
    parts = []
    for var in range(3):
        here = forcing[var]
        following = jnp.concatenate([here[1:], here[:1]], axis=0)
        parts += [here, following]
    table = jnp.concatenate(thirds(jnp.concatenate(parts, axis=1)), axis=0)
    chunk = 128
    here = iota((chunk, LANES), 1)
    for start in range(0, slots, chunk):
        odd = start >= slots // 2
        row = row_of[pl.ds(start, chunk), :]
        lane = lane_of[pl.ds(start, chunk), :]
        shape = (chunk, 3 * lane_rows)
        wide = jnp.concatenate([row, row], axis=1)[:, : 3 * lane_rows]
        pick = onehot(wide == iota(shape, 1) % lane_rows)
        rows = matmul(pick, table)
        after = here >= lane
        joined = [
            jnp.where(
                after,
                rows[:, 2 * var * LANES : (2 * var + 1) * LANES],
                rows[:, (2 * var + 1) * LANES : (2 * var + 2) * LANES],
            )
            for var in range(3)
        ]
        first = (here + lane) & 127
        second = (first + WINDOW) & 127
        losses = jnp.where(
            here < WINDOW, lane_pick(joined[1], first), lane_pick(joined[2], second)
        )
        base = start - slots // 2 if odd else start
        if odd:
            rains = jnp.where(
                here < WINDOW, rain[pl.ds(base, chunk), :], lane_pick(joined[0], second)
            )
        else:
            rain[pl.ds(base, chunk), :] = lane_pick(joined[0], first)
        for part in range(0, chunk, pairs):
            place = (base + part) * 3
            if odd:
                out[pl.ds(place + pairs, pairs), :] = rains[part : part + pairs]
                out[pl.ds(place + 2 * pairs, pairs), :] = losses[part : part + pairs]
            else:
                out[pl.ds(place, pairs), :] = losses[part : part + pairs]


def pack(homes, capacity, slot, offset, forcing):
    slots = slot.shape[1]
    return pl.pallas_call(
        functools.partial(pack_kernel, homes, capacity),
        in_specs=[pl.BlockSpec(memory_space=pltpu.HBM)] * 3,
        out_shape=jax.ShapeDtypeStruct((slots + slots // 2, LANES), jnp.float32),
        scratch_shapes=[
            pltpu.VMEM(slot.shape, jnp.int32),
            pltpu.VMEM(offset.shape, jnp.int32),
            pltpu.VMEM(forcing.shape, jnp.float32),
            pltpu.VMEM((slots, LANES), jnp.int32),
            pltpu.VMEM((slots, LANES), jnp.int32),
            pltpu.VMEM((slots // 2, LANES), jnp.float32),
            pltpu.SemaphoreType.DMA((3,)),
        ],
        compiler_params=pltpu.CompilerParams(vmem_limit_bytes=VMEM_LIMIT),
        cost_estimate=pl.CostEstimate(flops=10**9, bytes_accessed=2 * MIB, transcendentals=0),
        name="pack_forcing",
    )(in_hbm(slot), in_hbm(offset), in_hbm(forcing))


def unpack_plan_kernel(homes, capacity, lane_rows, slot, offset, code, place):
    slots = slot.shape[1]
    row, lane = slot_columns(slot[...], offset[...], homes, capacity)
    here = iota((slots, LANES), 1)
    index = (here - lane) & 127
    inside = (index < WINDOW) & (row >= 0)
    code[...] = jnp.where(inside, index + jnp.where(here >= lane, 0, LANES), -1)
    row_lane, _ = slot_rows(slot[...], offset[...], homes, capacity)
    place[...] = onehot(iota((lane_rows, slots), 0) == row_lane)


def unpack_plan(homes, capacity, lane_rows, slot, offset):
    slots = slot.shape[1]
    return pl.pallas_call(
        functools.partial(unpack_plan_kernel, homes, capacity, lane_rows),
        out_shape=(
            jax.ShapeDtypeStruct((slots, LANES), jnp.int32),
            jax.ShapeDtypeStruct((lane_rows, slots), jnp.bfloat16),
        ),
        compiler_params=pltpu.CompilerParams(vmem_limit_bytes=VMEM_LIMIT),
        cost_estimate=pl.CostEstimate(flops=10**9, bytes_accessed=2 * MIB, transcendentals=0),
        name="unpack_plan",
    )(slot, offset)


def strips_for_neighbours(state, rows):
    device = iota((rows, LANES), 0) // ITERS
    down = device // lax.axis_size("col") - lax.axis_index("region")
    right = device % lax.axis_size("col") - lax.axis_index("col")
    height, width = state.shape
    columns = jnp.transpose(state)
    empty = jnp.zeros((ITERS, LANES - height), jnp.float32)

    def repeated(strip):
        if strip.shape[1] < LANES:
            strip = jnp.concatenate([strip, empty], axis=1)
        return jnp.concatenate([strip] * (rows // ITERS), axis=0)

    near = (jnp.abs(down) <= 1).astype(jnp.int32)
    strips = jnp.zeros((rows, LANES), jnp.float32)
    strips = jnp.where((right == 0) & (down == 1), repeated(state[height - ITERS :]), strips)
    strips = jnp.where((right == 0) & (down == -1), repeated(state[:ITERS]), strips)
    strips = jnp.where((right == 1) & (near == 1), repeated(columns[width - ITERS :]), strips)
    return jnp.where((right == -1) & (near == 1), repeated(columns[:ITERS]), strips)


def cell_totals(arrived, code, place, first):
    lane_rows = place.shape[0]
    marks = code[...]
    window = lane_pick(arrived[...], (marks + first) & 127)
    placed = jnp.concatenate(
        [
            jnp.where((marks >= 0) & (marks < LANES), window, 0.0),
            jnp.where(marks >= LANES, window, 0.0),
        ],
        axis=1,
    )
    totals = matmul(place[...], jnp.concatenate(halves(placed), axis=1))
    totals = totals[:, :256] + totals[:, 256:]
    over = totals[:, LANES:]
    over = jnp.concatenate([over[lane_rows - 1 :], over[: lane_rows - 1]], axis=0)
    over = jnp.where(iota(over.shape, 0) == 0, 0.0, over)
    return totals[:, :LANES] + over


def unpack_runoff_kernel(arrived, code, place, river, _, __, runoff, storage, strips):
    total = cell_totals(arrived, code, place, 0)
    state = river[...] + total
    runoff[...] = total
    storage[...] = state
    strips[...] = strips_for_neighbours(state, strips.shape[0])


def unpack_runoff(homes, arrived, code, place, river, *after):
    shape = jax.ShapeDtypeStruct((place.shape[0], LANES), jnp.float32)
    strips = jax.ShapeDtypeStruct((homes * ITERS, LANES), jnp.float32)
    return pl.pallas_call(
        unpack_runoff_kernel,
        in_specs=[pl.BlockSpec(memory_space=pltpu.VMEM)] * 4
        + [pl.BlockSpec(memory_space=pl.ANY)] * 2,
        out_shape=(shape, shape, strips),
        compiler_params=pltpu.CompilerParams(vmem_limit_bytes=VMEM_LIMIT),
        cost_estimate=pl.CostEstimate(flops=10**9, bytes_accessed=1 * MIB, transcendentals=0),
        name="unpack_runoff",
    )(arrived, code, place, river, *after)


def unpack_evap_kernel(arrived, code, place, evap):
    evap[...] = cell_totals(arrived, code, place, WINDOW)


def unpack_evap(arrived, code, place):
    return pl.pallas_call(
        unpack_evap_kernel,
        out_shape=jax.ShapeDtypeStruct((place.shape[0], LANES), jnp.float32),
        compiler_params=pltpu.CompilerParams(vmem_limit_bytes=VMEM_LIMIT),
        cost_estimate=pl.CostEstimate(flops=10**9, bytes_accessed=1 * MIB, transcendentals=0),
        name="unpack_evap",
    )(arrived, code, place)


def segment_plan_kernel(cell, worker, meta):
    chunk = 96
    for start in range(0, cell.shape[0], chunk):
        values = cell[pl.ds(start, chunk), :]
        target = iota(values.shape, 1) & (WINDOW - 1)
        count = jnp.zeros_like(values)
        for step in (64, 32, 16, 8, 4, 2, 1):
            probe = lane_pick(values, count + (step - 1))
            count = jnp.where(probe <= target, count + step, count)
        count = jnp.where(lane_pick(values, count) <= target, count + 1, count)
        odd = worker[pl.ds(start, chunk), :] & 1
        meta[pl.ds(start, chunk), :] = count + (odd << 8)


def segment_plan(cell, worker):
    return pl.pallas_call(
        segment_plan_kernel,
        out_shape=jax.ShapeDtypeStruct(cell.shape, jnp.int32),
        compiler_params=pltpu.CompilerParams(vmem_limit_bytes=VMEM_LIMIT),
        cost_estimate=pl.CostEstimate(flops=10**8, bytes_accessed=1 * MIB, transcendentals=0),
        name="segment_plan",
    )(cell, worker)


def land_sums_kernel(
    pairs, slots, first_rows, arrived, cell, meta, area, water, cap, soil_in, porosity_in,
    drainage_in, _, __, through, lost, canopy_new, sums_out, soil, porosity, drainage, fetched,
    runoffs, evaps, sums, ready,
):
    layers, rows = soil.shape[:2]
    steps = ready.shape[0]
    block = rows // steps
    ahead = 4
    arrays = ((soil_in, soil), (porosity_in, porosity), (drainage_in, drainage))

    def part_of(step):
        return pl.ds(pl.multiple_of(step * block, block), block)

    def reads(step):
        return [
            pltpu.make_async_copy(
                source.at[:, part_of(step), :], target.at[:, part_of(step), :], ready.at[step, i]
            )
            for i, (source, target) in enumerate(arrays)
        ]

    def start_reads(step):
        for copy in reads(step):
            copy.start()

    def fetch(step):
        base = pl.multiple_of(step % 2 * (2 * block), 2 * block)
        for i in range(block):
            row = first_rows[step * block + i]
            fetched[pl.ds(base + 2 * i, 2), :] = arrived[pl.ds(row, 2, stride=pairs), :]

    def cascade(step):
        part = part_of(step)
        base = pl.multiple_of(step % 2 * (2 * block), 2 * block)
        index = cell[part, :]
        one = fetched[pl.ds(base, block, stride=2), :]
        two = fetched[pl.ds(base + 1, block, stride=2), :]
        odd = meta[part, :] >> 8
        loss = jnp.where(odd == 1, two, one)
        rain = lane_pick(jnp.where(odd == 1, one, two), index + odd * WINDOW)
        demand = lane_pick(loss, index)
        limit = lane_pick(loss, index + WINDOW)
        wetted = water[part, :] + rain
        flowing = jnp.maximum(wetted - cap[part, :], 0.0)
        retained = jnp.minimum(wetted, cap[part, :])
        canopy_loss = jnp.minimum(demand, retained)
        canopy_new[part, :] = retained - canopy_loss
        through[part, :] = flowing
        surface = jnp.zeros_like(flowing)
        for layer in range(layers):
            filled = soil[layer, part, :] + flowing
            excess = jnp.maximum(filled - porosity[layer, part, :], 0.0)
            surface = surface + excess
            filled = filled - excess
            flowing = drainage[layer, part, :] * filled
            if layer == 0:
                half = 0.5 * (filled - flowing)
                soil_loss = jnp.minimum(jnp.minimum(limit, demand - canopy_loss), half)
                lost[part, :] = soil_loss
                evaps[part, :] = area[part, :] * (canopy_loss + soil_loss)
        runoffs[part, :] = area[part, :] * (surface + flowing)

    def hand_back(step):
        part = part_of(step)
        shape = (2 * LANES, LANES)
        upto = onehot((iota(shape, 0) & 127) <= iota(shape, 1))
        count = meta[part, :] & 255
        last = jnp.maximum(count - 1, 0)
        here = iota((block, LANES), 1)
        picked = [
            lane_pick(matmul(jnp.concatenate(halves(value[part, :]), axis=1), upto), last)
            for value in (runoffs, evaps)
        ]
        reached = jnp.where(count > 0, jnp.where(here < WINDOW, *picked), 0.0)
        before = jnp.where((here & (WINDOW - 1)) == 0, 0.0, pltpu.roll(reached, 1, 1))
        sums[...] = reached - before
        for i in range(block):
            sums_out[pl.ds(slots[step * block + i], 1), :] = sums[pl.ds(i, 1), :]

    start_reads(0)
    fetch(0)
    start_reads(1)
    sums_out[...] = jnp.zeros_like(sums_out)
    runoffs[pl.ds(0, block), :] = jnp.zeros((block, LANES), jnp.float32)
    evaps[pl.ds(0, block), :] = jnp.zeros((block, LANES), jnp.float32)
    start_reads(2)
    start_reads(3)

    def round_of(step, carry):
        for copy in reads(step):
            copy.wait()

        @pl.when(step + ahead < steps)
        def _():
            start_reads(step + ahead)

        hand_back(jnp.maximum(step - 1, 0))
        cascade(step)
        fetch(jnp.minimum(step + 1, steps - 1))
        return carry

    lax.fori_loop(0, steps, round_of, 0)
    hand_back(steps - 1)


def land_sums(
    sums_shape, pairs, slots, first_rows, arrived, cell, meta, area, water, cap, soil, porosity,
    drainage, after,
):
    layers, rows = soil.shape[:2]
    steps = 10
    block = rows // steps
    near = pl.BlockSpec(memory_space=pltpu.VMEM)
    far = pl.BlockSpec(memory_space=pltpu.HBM)
    return pl.pallas_call(
        functools.partial(land_sums_kernel, pairs),
        in_specs=[pl.BlockSpec(memory_space=pltpu.SMEM)] * 2 + [near] * 6 + [far] * 3
        + [pl.BlockSpec(memory_space=pl.ANY)] * 2,
        out_specs=[near] * 4,
        scratch_shapes=[pltpu.VMEM(soil.shape, jnp.float32)] * 3
        + [pltpu.VMEM((4 * block, LANES), jnp.float32)]
        + [pltpu.VMEM((rows, LANES), jnp.float32)] * 2
        + [pltpu.VMEM((block, LANES), jnp.float32), pltpu.SemaphoreType.DMA((steps, 3))],
        out_shape=[jax.ShapeDtypeStruct((rows, LANES), jnp.float32)] * 3
        + [jax.ShapeDtypeStruct(sums_shape, jnp.float32)],
        compiler_params=pltpu.CompilerParams(vmem_limit_bytes=VMEM_LIMIT),
        cost_estimate=pl.CostEstimate(flops=10**8, bytes_accessed=20 * MIB, transcendentals=0),
        name="land_sums",
    )(
        slots, first_rows, arrived, cell, meta, area, water, cap,
        in_hbm(soil), in_hbm(porosity), in_hbm(drainage), *after,
    )


def new_soil_kernel(through, lost, canopy, soil, porosity, drainage, soil_new, canopy_new):
    layers, block = soil.shape[:2]
    chunk = 48
    canopy_new[...] = canopy[...]
    for start in range(0, block, chunk):
        part = pl.ds(start, chunk)
        flowing = through[part, :]
        for layer in range(layers):
            filled = soil[layer, part, :] + flowing
            filled = filled - jnp.maximum(filled - porosity[layer, part, :], 0.0)
            flowing = drainage[layer, part, :] * filled
            middle = filled - flowing
            soil_new[layer, part, :] = middle - lost[part, :] if layer == 0 else middle


def new_soil(through, lost, canopy, soil, porosity, drainage):
    layers, rows = soil.shape[:2]
    block = 96
    flat = pl.BlockSpec((block, LANES), lambda i: (i, 0))
    deep = pl.BlockSpec((layers, block, LANES), lambda i: (0, i, 0))
    return pl.pallas_call(
        new_soil_kernel,
        grid=(rows // block,),
        in_specs=[flat, flat, flat, deep, deep, deep],
        out_specs=[deep, flat],
        out_shape=(
            jax.ShapeDtypeStruct(soil.shape, jnp.float32),
            jax.ShapeDtypeStruct((rows, LANES), jnp.float32),
        ),
        compiler_params=pltpu.CompilerParams(vmem_limit_bytes=VMEM_LIMIT),
        cost_estimate=pl.CostEstimate(flops=10**8, bytes_accessed=16 * MIB, transcendentals=0),
        name="new_soil",
    )(through, lost, canopy, in_hbm(soil), in_hbm(porosity), in_hbm(drainage))


def halo_parts(value, axis, dim, width):
    count, length = (lax.axis_size(axis), value.shape[dim])
    up = [(i, i + 1) for i in range(count - 1)]
    down = [(j, i) for i, j in up]
    last = lax.slice_in_dim(value, length - width, length, axis=dim)
    initial = lax.slice_in_dim(value, 0, width, axis=dim)
    return lax.ppermute(last, axis, up), lax.ppermute(initial, axis, down)


def edge_columns_kernel(tall, _, first, last):
    arrays, height, width = tall.shape
    for number in range(arrays):
        values = tall[number]
        values = jnp.concatenate([values, jnp.zeros((LANES - height, width), jnp.float32)], axis=0)
        columns = jnp.transpose(values)
        part = pl.ds(number * ITERS, ITERS)
        first[part, :] = columns[:ITERS]
        last[part, :] = columns[width - ITERS :]


def edge_columns(tall, after):
    shape = jax.ShapeDtypeStruct((2 * ITERS, LANES), jnp.float32)
    return pl.pallas_call(
        edge_columns_kernel,
        in_specs=[pl.BlockSpec(memory_space=pltpu.VMEM), pl.BlockSpec(memory_space=pl.ANY)],
        out_shape=(shape, shape),
        compiler_params=pltpu.CompilerParams(vmem_limit_bytes=VMEM_LIMIT),
        cost_estimate=pl.CostEstimate(flops=10**6, bytes_accessed=10**5, transcendentals=0),
        name="edge_columns",
    )(tall, after)


def extended(own, strip):
    height = own.shape[0]

    def column_strip(right):
        middle, above, below = strip(0, right), strip(-1, right), strip(1, right)
        return jnp.concatenate(
            [
                middle[:, :height],
                below[:, :ITERS],
                above[:, height - ITERS : height],
                jnp.zeros((ITERS, LANES - height - 2 * ITERS), jnp.float32),
            ],
            axis=1,
        )

    gap = jnp.zeros((LANES - 2 * ITERS, LANES), jnp.float32)
    sides = jnp.concatenate([column_strip(1), gap, column_strip(-1)], axis=0)
    sides = jnp.transpose(sides)[: height + 2 * ITERS]
    tall = jnp.concatenate([own, strip(1, 0), strip(-1, 0)], axis=0)
    return jnp.concatenate([tall, sides], axis=1)


def neighbour(down, right):
    row, column = lax.axis_index("region") + down, lax.axis_index("col") + right
    there = (row >= 0) & (row < lax.axis_size("region"))
    there &= (column >= 0) & (column < lax.axis_size("col"))
    return jnp.where(there, row * lax.axis_size("col") + column, 0), jnp.where(there, 1.0, 0.0)


def static_halo_kernel(tall, before, after, out):
    height, width = tall.shape[1:]
    gap = jnp.zeros((LANES - 2 * ITERS, LANES), jnp.float32)
    for number in range(2):
        part = pl.ds(number * ITERS, ITERS)
        sides = jnp.transpose(jnp.concatenate([after[part, :], gap, before[part, :]], axis=0))
        out[number, :, :width] = tall[number]
        out[number, :, width:] = sides[:height]


def static_halo(tall, before, after):
    arrays, height, width = tall.shape
    return pl.pallas_call(
        static_halo_kernel,
        out_shape=jax.ShapeDtypeStruct((arrays, height, width + LANES), jnp.float32),
        compiler_params=pltpu.CompilerParams(vmem_limit_bytes=VMEM_LIMIT),
        cost_estimate=pl.CostEstimate(flops=10**6, bytes_accessed=10**6, transcendentals=0),
        name="static_halo",
    )(tall, before, after)


def river_kernel(state, strips, fixed, out):
    height, width = state.shape

    def strip(down, right):
        device, there = neighbour(down, right)
        return strips[pl.ds(device * ITERS, ITERS), :] * there

    storage = extended(state[...], strip)
    rate = fixed[0]
    code = fixed[1]
    rows, cols = storage.shape
    for _ in range(ITERS):
        outflow = rate * storage
        inflow = jnp.zeros_like(storage)
        for col_step in (-1, 0, 1):
            column = jnp.zeros_like(storage)
            for bit, (row_step, step) in enumerate(directions):
                if step != col_step:
                    continue
                leaving = jnp.where(code == float(1 << bit), outflow, 0.0)
                if row_step:
                    leaving = pltpu.roll(leaving, row_step % rows, 0)
                column = column + leaving
            if col_step:
                column = pltpu.roll(column, col_step % cols, 1)
            inflow = inflow + column
        storage = storage - outflow + inflow
    out[...] = storage[:height, :width]


def river(state, strips, fixed):
    return pl.pallas_call(
        river_kernel,
        out_shape=jax.ShapeDtypeStruct(state.shape, jnp.float32),
        compiler_params=pltpu.CompilerParams(vmem_limit_bytes=VMEM_LIMIT),
        cost_estimate=pl.CostEstimate(flops=10**7, bytes_accessed=1 * MIB, transcendentals=0),
        name="river_steps",
    )(state, strips, fixed)


def exchange(value):
    return lax.all_to_all(value, axes, split_axis=0, concat_axis=0, tiled=True)


def shards(
    forcing,
    river_storage,
    river_rate,
    flow_code,
    home_slot,
    home_offset,
    worker_list,
    patch_cell,
    patch_area,
    canopy_water,
    canopy_cap,
    soil_water,
    porosity,
    drainage,
):
    homes = lax.axis_size("region") * lax.axis_size("col")
    capacity = home_slot.shape[1] // homes
    grid_rows, grid_cols = river_storage.shape
    lane_rows = grid_rows * grid_cols // LANES
    outgoing = pack(
        homes, capacity, home_slot, home_offset, forcing.reshape(3, lane_rows, LANES)
    )
    arrived = exchange(outgoing)
    home = worker_list // capacity
    position = worker_list - home * capacity
    pairs = capacity // 2
    first_rows = home * (3 * pairs) + position // 2 + position % 2 * pairs
    meta = segment_plan(patch_cell, worker_list[:, None])
    fixed = jnp.stack([river_rate, flow_code.astype(jnp.float32)])
    above, below = halo_parts(fixed, "region", 1, ITERS)
    through, lost, canopy, sums = land_sums(
        (homes * capacity, LANES), pairs, worker_list, first_rows, arrived, patch_cell, meta,
        patch_area, canopy_water, canopy_cap, soil_water, porosity, drainage, (above, below),
    )
    returned = exchange(sums)
    soil_new, canopy_new = new_soil(through, lost, canopy, soil_water, porosity, drainage)
    code, place = unpack_plan(homes, capacity, lane_rows, home_slot, home_offset)
    fixed = jnp.concatenate([fixed, below, above], axis=1)
    initial, last = edge_columns(fixed, sums)
    count = lax.axis_size("col")
    before = lax.ppermute(last, "col", [(i, i + 1) for i in range(count - 1)])
    after = lax.ppermute(initial, "col", [(i + 1, i) for i in range(count - 1)])
    fixed = static_halo(fixed, before, after)
    cell_runoff, storage, strips = unpack_runoff(
        homes, returned, code, place, river_storage.reshape(lane_rows, LANES), fixed, in_hbm(canopy_new)
    )
    cell_evap = unpack_evap(returned, code, place)
    river_new = river(storage.reshape(river_storage.shape), exchange(strips), fixed)
    return (
        soil_new,
        canopy_new,
        cell_runoff.reshape(river_storage.shape),
        cell_evap.reshape(river_storage.shape),
        river_new,
    )


def solution(mesh):
    placed = (
        P(None, "region", "col"),
        P("region", "col"),
        P("region", "col"),
        P("region", "col"),
        P(("region", "col"), None),
        P(("region", "col"), None),
        P(("region", "col")),
        P(("region", "col"), None),
        P(("region", "col"), None),
        P(("region", "col"), None),
        P(("region", "col"), None),
        P(None, ("region", "col"), None),
        P(None, ("region", "col"), None),
        P(None, ("region", "col"), None),
    )
    return jax.shard_map(
        shards,
        mesh=mesh,
        in_specs=placed,
        out_specs=(
            P(None, ("region", "col"), None),
            P(("region", "col"), None),
            P("region", "col"),
            P("region", "col"),
            P("region", "col"),
        ),
        check_vma=False,
    )
```

profile of v0, /device:TPU:0, one launch (start us, length us, event | category | flops | bytes accessed | tf_op | source)
XLA Modules:
  0.0 72.6 jit_solution(2180717380776961131)
XLA Ops:
  0.6 0.0 copy-start.9
  0.6 0.0 copy-start.8
  0.7 0.0 copy-start.4
  0.7 0.0 copy-start
  0.7 0.0 copy-start.1
  0.7 0.0 copy-start.2
  0.7 0.0 copy-start.3
  0.7 3.6 %pack_forcing.1 = f32[1536,128]{1,0:T(8,128)} custom-call(s32[1,1024]{1,0:T(1,128)} %slot.1, s32[1,1024]{1,0:T(1,128)} %offset.1, f32[3,64,128]{2,1,0:T(8,128)} %forcing_in.1), custom_call_target="tpu_custom_call" | custom-call | flops 1000000000 | bytes 2097152 | tf_op jit(solution)/shard_map/pack_forcing/pallas_call | solution.py:166
  4.3 7.3 %all-to-all-start = ((f32[32,48,128]{2,1,0:T(8,128)}), f32[32,48,128]{2,1,0:T(8,128)S(1)}, u32[]{:S(2)}, u32[]{:S(2)}) async-start(f32[32,48,128]{2,1,0:T(8,128)} %bitcast), calls=%async_computation | async-start | bytes 1572864 | tf_op jit(solution)/shard_map/all_to_all | solution.py:603
  11.6 0.0 copy-done.9
  11.7 0.0 copy-done.8
  11.7 3.7 %collective-permute-start = (f32[2,4,128]{2,1,0:T(4,128)S(1)}, f32[2,4,128]{2,1,0:T(4,128)S(1)}, u32[]{:S(2)}, u32[]{:S(2)}) collective-permute-start(f32[2,4,128]{2,1,0:T(4,128)S(1)} %get-tuple-element.32), channel_id=1, source_target_pairs={{0,8},{8,16},{16,24},{1,9},{9,17},{17,25},{2,10},{10,18},{18,26},{... | collective-permute-start | bytes 12296 | tf_op jit(solution)/shard_map/ppermute | solution.py:486
  15.4 1.3 %collective-permute-start.1 = (f32[2,4,128]{2,1,0:T(4,128)S(1)}, f32[2,4,128]{2,1,0:T(4,128)S(1)}, u32[]{:S(2)}, u32[]{:S(2)}) collective-permute-start(f32[2,4,128]{2,1,0:T(4,128)S(1)} %get-tuple-element.31), channel_id=1, source_target_pairs={{8,0},{16,8},{24,16},{9,1},{17,9},{25,17},{10,2},{18,10},{26,18},{... | collective-permute-start | bytes 12296 | tf_op jit(solution)/shard_map/ppermute | solution.py:486
  16.7 0.0 copy-done.4
  16.7 0.1 copy.19.worker
  16.8 0.0 copy-done
  16.9 1.9 %segment_plan.1.meta = s32[480,128]{1,0:T(8,128)S(1)} custom-call(s32[480,128]{1,0:T(8,128)S(1)} %copy-done, s32[480,1]{1,0:T(8,128)S(1)} %copy.19.worker), custom_call_target="tpu_custom_call" | custom-call | flops 100000000 | bytes 1048576 | tf_op jit(solution)/shard_map/segment_plan/pallas_call | solution.py:301
  18.8 6.3 %collective-permute-done._ = f32[2,4,128]{2,1,0:T(4,128)S(1)} collective-permute-done((f32[2,4,128]{2,1,0:T(4,128)S(1)}, f32[2,4,128]{2,1,0:T(4,128)S(1)}, u32[]{:S(2)}, u32[]{:S(2)}) %collective-permute-start) | collective-permute-done | bytes 4128 | tf_op jit(solution)/shard_map/ppermute | solution.py:486
  25.1 0.0 collective-permute-done.1.__
  25.1 7.2 %all-to-all-done = f32[32,48,128]{2,1,0:T(8,128)S(1)} async-done(((f32[32,48,128]{2,1,0:T(8,128)}), f32[32,48,128]{2,1,0:T(8,128)S(1)}, u32[]{:S(2)}, u32[]{:S(2)}) %all-to-all-start) | async-done | bytes 786464 | tf_op jit(solution)/shard_map/all_to_all | solution.py:603
  32.3 0.0 copy-done.1
  32.3 0.0 copy-done.2
  32.3 0.0 copy-done.3
  32.3 0.0 copy-start.6
  32.3 0.0 copy-start.7
  32.3 6.9 %land_sums.1 = (f32[480,128]{1,0:T(8,128)S(1)}, f32[480,128]{1,0:T(8,128)S(1)}, f32[480,128]{1,0:T(8,128)S(1)}, f32[1024,128]{1,0:T(8,128)}) custom-call(s32[480]{0:T(512)S(1)} %copy-done.4, s32[480]{0:T(512)S(1)} %fusion.2.first_rows, f32[1536,128]{1,0:T(8,128)S(1)} %bitcast.10, s32[480,128]{1,0:T(8,128)S(1)} %copy-done, s32[480,128]{1,0:T(8,128)S(1)} %segment_plan.1.meta, ...), custom_call_target="tpu_custom_call" | custom-call | flops 100000000 | bytes 20971520 | tf_op jit(solution)/shard_map/land_sums/pallas_call | solution.py:425
  39.2 3.6 %all-to-all-start.1 = ((f32[32,32,128]{2,1,0:T(8,128)}), f32[32,32,128]{2,1,0:T(8,128)S(1)}, u32[]{:S(2)}, u32[]{:S(2)}) async-start(f32[32,32,128]{2,1,0:T(8,128)} %bitcast.5), calls=%async_computation.1 | async-start | bytes 1048576 | tf_op jit(solution)/shard_map/all_to_all | solution.py:603
  42.9 0.0 copy-done.6
  42.9 0.0 copy-done.7
  42.9 0.7 unpack_plan.1
  43.6 0.1 edge_columns.1
  43.6 2.2 %collective-permute-start.2 = (f32[8,128]{1,0:T(8,128)S(1)}, f32[8,128]{1,0:T(8,128)S(1)}, u32[]{:S(2)}, u32[]{:S(2)}) collective-permute-start(f32[8,128]{1,0:T(8,128)S(1)} %get-tuple-element.26), channel_id=1, source_target_pairs={{0,1},{1,2},{2,3},{3,4},{4,5},{5,6},{6,7},{8,9},{9,10},{10,11},{11... | collective-permute-start | bytes 12296 | tf_op jit(solution)/shard_map/ppermute | solution.py:647
  45.8 1.3 %collective-permute-start.3 = (f32[8,128]{1,0:T(8,128)S(1)}, f32[8,128]{1,0:T(8,128)S(1)}, u32[]{:S(2)}, u32[]{:S(2)}) collective-permute-start(f32[8,128]{1,0:T(8,128)S(1)} %get-tuple-element.27), channel_id=1, source_target_pairs={{1,0},{2,1},{3,2},{4,3},{5,4},{6,5},{7,6},{9,8},{10,9},{11,10},{12... | collective-permute-start | bytes 12296 | tf_op jit(solution)/shard_map/ppermute | solution.py:648
  47.1 0.0 copy-start.5
  47.1 7.5 %new_soil.1 = (f32[15,480,128]{2,1,0:T(8,128)}, f32[480,128]{1,0:T(8,128)}) custom-call(f32[480,128]{1,0:T(8,128)S(1)} %get-tuple-element.18.through, f32[480,128]{1,0:T(8,128)S(1)} %get-tuple-element.19.lost, f32[480,128]{1,0:T(8,128)S(1)} %get-tuple-element.20.canopy, f32[15,480,128]{2,1,0:T(8,128)} %soil.1, f32[15,480,128]{2,1,0:T(8,128)} %porosity.1, ...), custom_call_target="tpu_custom_call" | custom-call | flops 100000000 | bytes 16777216 | tf_op jit(solution)/shard_map/new_soil/pallas_call | solution.py:465
  54.6 0.0 collective-permute-done.2.before
  54.6 0.0 collective-permute-done.3.after
  54.6 0.1 static_halo.1._.fixed
  54.7 3.7 %all-to-all-done.1 = f32[32,32,128]{2,1,0:T(8,128)S(1)} async-done(((f32[32,32,128]{2,1,0:T(8,128)}), f32[32,32,128]{2,1,0:T(8,128)S(1)}, u32[]{:S(2)}, u32[]{:S(2)}) %all-to-all-start.1) | async-done | bytes 524320 | tf_op jit(solution)/shard_map/all_to_all | solution.py:603
  58.4 0.0 copy-done.5
  58.4 1.3 %unpack_runoff.1 = (f32[64,128]{1,0:T(8,128)}, f32[64,128]{1,0:T(8,128)S(1)}, f32[128,128]{1,0:T(8,128)}) custom-call(f32[1024,128]{1,0:T(8,128)S(1)} %bitcast.11, s32[1024,128]{1,0:T(8,128)S(1)} %get-tuple-element.24.code, bf16[64,1024]{1,0:T(8,128)(2,1)S(1)} %get-tuple-element.25.place, f32[64,128]{1,0:T(8,128)S(1)} %copy-done.5, ...), custom_call_target="tpu_custom_call" | custom-call | flops 1000000000 | bytes 1048576 | tf_op jit(solution)/shard_map/unpack_runoff/pallas_call | solution.py:261
  59.8 4.2 %all-to-all-start.2 = ((f32[32,4,128]{2,1,0:T(4,128)}), f32[32,4,128]{2,1,0:T(4,128)S(1)}, u32[]{:S(2)}, u32[]{:S(2)}) async-start(f32[32,4,128]{2,1,0:T(4,128)} %bitcast.7), calls=%async_computation.2 | async-start | bytes 131072 | tf_op jit(solution)/shard_map/all_to_all | solution.py:603
  64.0 1.2 %unpack_evap.1 = f32[64,128]{1,0:T(8,128)} custom-call(f32[1024,128]{1,0:T(8,128)S(1)} %bitcast.12, s32[1024,128]{1,0:T(8,128)S(1)} %get-tuple-element.24.code, bf16[64,1024]{1,0:T(8,128)(2,1)S(1)} %get-tuple-element.25.place), custom_call_target="tpu_custom_call" | custom-call | flops 1000000000 | bytes 1048576 | tf_op jit(solution)/shard_map/unpack_evap/pallas_call | solution.py:277
  65.2 6.2 %all-to-all-done.2 = f32[32,4,128]{2,1,0:T(4,128)S(1)} async-done(((f32[32,4,128]{2,1,0:T(4,128)}), f32[32,4,128]{2,1,0:T(4,128)S(1)}, u32[]{:S(2)}, u32[]{:S(2)}) %all-to-all-start.2) | async-done | bytes 65568 | tf_op jit(solution)/shard_map/all_to_all | solution.py:603
  71.4 1.2 %river_steps.1 = f32[64,128]{1,0:T(8,128)} custom-call(f32[64,128]{1,0:T(8,128)S(1)} %get-tuple-element.29.state, f32[128,128]{1,0:T(8,128)S(1)} %bitcast.13, f32[2,72,256]{2,1,0:T(8,128)S(1)} %static_halo.1._.fixed), custom_call_target="tpu_custom_call" | custom-call | flops 10000000 | bytes 1048576 | tf_op jit(solution)/shard_map/river_steps/pallas_call | solution.py:593
  (4 shorter events, 0.0 us)
Async XLA Ops:
  0.6 11.0 %copy-start.9 = (s32[64,128]{1,0:T(8,128)S(1)}, s32[64,128]{1,0:T(8,128)}, u32[]{:S(2)}) copy-start(s32[64,128]{1,0:T(8,128)} %param.17) | copy-start | bytes 98308
  0.6 11.0 %copy-start.8 = (f32[64,128]{1,0:T(8,128)S(1)}, f32[64,128]{1,0:T(8,128)}, u32[]{:S(2)}) copy-start(f32[64,128]{1,0:T(8,128)} %param.16) | copy-start | bytes 98308
  0.7 16.0 %copy-start.4 = (s32[480]{0:T(512)S(1)}, s32[480]{0:T(512)}, u32[]{:S(2)}) copy-start(s32[480]{0:T(512)} %slots.1) | copy-start | bytes 5764
  0.7 16.2 %copy-start = (s32[480,128]{1,0:T(8,128)S(1)}, s32[480,128]{1,0:T(8,128)}, u32[]{:S(2)}) copy-start(s32[480,128]{1,0:T(8,128)} %cell.3) | copy-start | bytes 737284
  0.7 31.6 %copy-start.1 = (f32[480,128]{1,0:T(8,128)S(1)}, f32[480,128]{1,0:T(8,128)}, u32[]{:S(2)}) copy-start(f32[480,128]{1,0:T(8,128)} %area.1) | copy-start | bytes 737284
  0.7 31.6 %copy-start.2 = (f32[480,128]{1,0:T(8,128)S(1)}, f32[480,128]{1,0:T(8,128)}, u32[]{:S(2)}) copy-start(f32[480,128]{1,0:T(8,128)} %water.1) | copy-start | bytes 737284
  0.7 31.6 %copy-start.3 = (f32[480,128]{1,0:T(8,128)S(1)}, f32[480,128]{1,0:T(8,128)}, u32[]{:S(2)}) copy-start(f32[480,128]{1,0:T(8,128)} %cap.1) | copy-start | bytes 737284
  4.3 28.0 %all-to-all-start = ((f32[32,48,128]{2,1,0:T(8,128)}), f32[32,48,128]{2,1,0:T(8,128)S(1)}, u32[]{:S(2)}, u32[]{:S(2)}) async-start(f32[32,48,128]{2,1,0:T(8,128)} %bitcast), calls=%async_computation | async-start | bytes 1572864 | tf_op jit(solution)/shard_map/all_to_all | solution.py:603
  11.7 13.4 %collective-permute-start = (f32[2,4,128]{2,1,0:T(4,128)S(1)}, f32[2,4,128]{2,1,0:T(4,128)S(1)}, u32[]{:S(2)}, u32[]{:S(2)}) collective-permute-start(f32[2,4,128]{2,1,0:T(4,128)S(1)} %get-tuple-element.32), channel_id=1, source_target_pairs={{0,8},{8,16},{16,24},{1,9},{9,17},{17,25},{2,10},{10,18},{18,26},{... | collective-permute-start | bytes 12296 | tf_op jit(solution)/shard_map/ppermute | solution.py:486
  15.4 9.7 %collective-permute-start.1 = (f32[2,4,128]{2,1,0:T(4,128)S(1)}, f32[2,4,128]{2,1,0:T(4,128)S(1)}, u32[]{:S(2)}, u32[]{:S(2)}) collective-permute-start(f32[2,4,128]{2,1,0:T(4,128)S(1)} %get-tuple-element.31), channel_id=1, source_target_pairs={{8,0},{16,8},{24,16},{9,1},{17,9},{25,17},{10,2},{18,10},{26,18},{... | collective-permute-start | bytes 12296 | tf_op jit(solution)/shard_map/ppermute | solution.py:486
  32.3 10.6 %copy-start.6 = (s32[1,1024]{1,0:T(1,128)S(1)}, s32[1,1024]{1,0:T(1,128)}, u32[]{:S(2)}) copy-start(s32[1,1024]{1,0:T(1,128)} %slot.1) | copy-start | bytes 12292
  32.3 10.6 %copy-start.7 = (s32[1,1024]{1,0:T(1,128)S(1)}, s32[1,1024]{1,0:T(1,128)}, u32[]{:S(2)}) copy-start(s32[1,1024]{1,0:T(1,128)} %offset.1) | copy-start | bytes 12292
  39.2 19.2 %all-to-all-start.1 = ((f32[32,32,128]{2,1,0:T(8,128)}), f32[32,32,128]{2,1,0:T(8,128)S(1)}, u32[]{:S(2)}, u32[]{:S(2)}) async-start(f32[32,32,128]{2,1,0:T(8,128)} %bitcast.5), calls=%async_computation.1 | async-start | bytes 1048576 | tf_op jit(solution)/shard_map/all_to_all | solution.py:603
  43.6 11.0 %collective-permute-start.2 = (f32[8,128]{1,0:T(8,128)S(1)}, f32[8,128]{1,0:T(8,128)S(1)}, u32[]{:S(2)}, u32[]{:S(2)}) collective-permute-start(f32[8,128]{1,0:T(8,128)S(1)} %get-tuple-element.26), channel_id=1, source_target_pairs={{0,1},{1,2},{2,3},{3,4},{4,5},{5,6},{6,7},{8,9},{9,10},{10,11},{11... | collective-permute-start | bytes 12296 | tf_op jit(solution)/shard_map/ppermute | solution.py:647
  45.8 8.8 %collective-permute-start.3 = (f32[8,128]{1,0:T(8,128)S(1)}, f32[8,128]{1,0:T(8,128)S(1)}, u32[]{:S(2)}, u32[]{:S(2)}) collective-permute-start(f32[8,128]{1,0:T(8,128)S(1)} %get-tuple-element.27), channel_id=1, source_target_pairs={{1,0},{2,1},{3,2},{4,3},{5,4},{6,5},{7,6},{9,8},{10,9},{11,10},{12... | collective-permute-start | bytes 12296 | tf_op jit(solution)/shard_map/ppermute | solution.py:648
  47.1 11.3 %copy-start.5 = (f32[64,128]{1,0:T(8,128)S(1)}, f32[64,128]{1,0:T(8,128)}, u32[]{:S(2)}) copy-start(f32[64,128]{1,0:T(8,128)} %river.1) | copy-start | bytes 98308
  59.8 11.7 %all-to-all-start.2 = ((f32[32,4,128]{2,1,0:T(4,128)}), f32[32,4,128]{2,1,0:T(4,128)S(1)}, u32[]{:S(2)}, u32[]{:S(2)}) async-start(f32[32,4,128]{2,1,0:T(4,128)} %bitcast.7), calls=%async_computation.2 | async-start | bytes 131072 | tf_op jit(solution)/shard_map/all_to_all | solution.py:603
where the time goes:
time: 73.1 us; the launch traced here: 72.6 us
  Pallas kernels  24.5 us (34%)
  starting transfers between devices  23.6 us (32%)
  waiting for transfers between devices  23.4 us (32%)
  between operations  0.91 us (1%)
    all_to_all x3, waiting for transfers between devices, exchange(): return lax.all_to_all(value, axes, split_axis=0, concat_axis=0, tiled=True)  17.1 us
    all_to_all x3, starting transfers between devices, exchange(): return lax.all_to_all(value, axes, split_axis=0, concat_axis=0, tiled=True)  15.2 us
    pallas_call x1, Pallas kernels, new_soil(): pl.pallas_call(new_soil_kernel, grid=(rows // block,), in_specs=[flat, fl...  7.48 us
    pallas_call x1, Pallas kernels, land_sums(): pl.pallas_call(functools.partial(land_sums_kernel, pairs), in_specs=[pl.B...  6.9 us
    ppermute x2, waiting for transfers between devices, halo_parts(): return (lax.ppermute(last, axis, up), lax.ppermute(initial, axis, down))  6.33 us
    ppermute x2, starting transfers between devices, halo_parts(): return (lax.ppermute(last, axis, up), lax.ppermute(initial, axis, down))  4.97 us
    pallas_call x1, Pallas kernels, pack(): pl.pallas_call(functools.partial(pack_kernel, homes, capacity), in_specs=...  3.61 us
    ppermute x1, starting transfers between devices, shards(): before = lax.ppermute(last, 'col', [(i, i + 1) for i in range(count - 1)])  2.18 us
  transfers between devices with their start and end apart: 7, of which 4 were waited for; matrix products, arithmetic and copies ran while one was open for 0% of the time, Pallas kernels for 16%

commit v1 on v0

--- a/solution.py
+++ b/solution.py
@@ -370,29 +370,27 @@
                 evaps[part, :] = area[part, :] * (canopy_loss + soil_loss)
         runoffs[part, :] = area[part, :] * (surface + flowing)
 
-    def hand_back(step):
-        part = part_of(step)
+    def hand_back(start, count):
+        part = pl.ds(start, count)
         shape = (2 * LANES, LANES)
         upto = onehot((iota(shape, 0) & 127) <= iota(shape, 1))
-        count = meta[part, :] & 255
-        last = jnp.maximum(count - 1, 0)
-        here = iota((block, LANES), 1)
+        patches = meta[part, :] & 255
+        last = jnp.maximum(patches - 1, 0)
+        here = iota((count, LANES), 1)
         picked = [
             lane_pick(matmul(jnp.concatenate(halves(value[part, :]), axis=1), upto), last)
             for value in (runoffs, evaps)
         ]
-        reached = jnp.where(count > 0, jnp.where(here < WINDOW, *picked), 0.0)
+        reached = jnp.where(patches > 0, jnp.where(here < WINDOW, *picked), 0.0)
         before = jnp.where((here & (WINDOW - 1)) == 0, 0.0, pltpu.roll(reached, 1, 1))
         sums[...] = reached - before
-        for i in range(block):
-            sums_out[pl.ds(slots[step * block + i], 1), :] = sums[pl.ds(i, 1), :]
+        for i in range(count):
+            sums_out[pl.ds(slots[start + i], 1), :] = sums[pl.ds(i, 1), :]
 
     start_reads(0)
     fetch(0)
     start_reads(1)
     sums_out[...] = jnp.zeros_like(sums_out)
-    runoffs[pl.ds(0, block), :] = jnp.zeros((block, LANES), jnp.float32)
-    evaps[pl.ds(0, block), :] = jnp.zeros((block, LANES), jnp.float32)
     start_reads(2)
     start_reads(3)
 
@@ -404,13 +402,13 @@
         def _():
             start_reads(step + ahead)
 
-        hand_back(jnp.maximum(step - 1, 0))
         cascade(step)
         fetch(jnp.minimum(step + 1, steps - 1))
         return carry
 
-    lax.fori_loop(0, steps, round_of, 0)
-    hand_back(steps - 1)
+    for half in range(2):
+        lax.fori_loop(half * steps // 2, (half + 1) * steps // 2, round_of, 0)
+        hand_back(half * rows // 2, rows // 2)
 
 
 def land_sums(
@@ -430,7 +428,7 @@
         scratch_shapes=[pltpu.VMEM(soil.shape, jnp.float32)] * 3
         + [pltpu.VMEM((4 * block, LANES), jnp.float32)]
         + [pltpu.VMEM((rows, LANES), jnp.float32)] * 2
-        + [pltpu.VMEM((block, LANES), jnp.float32), pltpu.SemaphoreType.DMA((steps, 3))],
+        + [pltpu.VMEM((rows // 2, LANES), jnp.float32), pltpu.SemaphoreType.DMA((steps, 3))],
         out_shape=[jax.ShapeDtypeStruct((rows, LANES), jnp.float32)] * 3
         + [jax.ShapeDtypeStruct(sums_shape, jnp.float32)],
         compiler_params=pltpu.CompilerParams(vmem_limit_bytes=VMEM_LIMIT),
@@ -442,7 +440,8 @@
     )
 
 
-def new_soil_kernel(through, lost, canopy, soil, porosity, drainage, soil_new, canopy_new):
+def new_soil_kernel(through, lost, canopy, soil, porosity, drainage, *rest):
+    soil_new, canopy_new = rest[-2:]
     layers, block = soil.shape[:2]
     chunk = 48
     canopy_new[...] = canopy[...]
@@ -457,24 +456,29 @@
             soil_new[layer, part, :] = middle - lost[part, :] if layer == 0 else middle
 
 
-def new_soil(through, lost, canopy, soil, porosity, drainage):
+def new_soil(first, last, through, lost, canopy, soil, porosity, drainage, made=(), after=None):
     layers, rows = soil.shape[:2]
     block = 96
-    flat = pl.BlockSpec((block, LANES), lambda i: (i, 0))
-    deep = pl.BlockSpec((layers, block, LANES), lambda i: (0, i, 0))
+    flat = pl.BlockSpec((block, LANES), lambda i: (first + i, 0))
+    deep = pl.BlockSpec((layers, block, LANES), lambda i: (0, first + i, 0))
+    anywhere = pl.BlockSpec(memory_space=pl.ANY)
+    more = [in_hbm(value) for value in made] + ([] if after is None else [after])
     return pl.pallas_call(
         new_soil_kernel,
-        grid=(rows // block,),
-        in_specs=[flat, flat, flat, deep, deep, deep],
+        grid=(last - first,),
+        in_specs=[flat, flat, flat, deep, deep, deep] + [anywhere] * len(more),
         out_specs=[deep, flat],
         out_shape=(
             jax.ShapeDtypeStruct(soil.shape, jnp.float32),
             jax.ShapeDtypeStruct((rows, LANES), jnp.float32),
         ),
-        compiler_params=pltpu.CompilerParams(vmem_limit_bytes=VMEM_LIMIT),
-        cost_estimate=pl.CostEstimate(flops=10**8, bytes_accessed=16 * MIB, transcendentals=0),
+        input_output_aliases={6: 0, 7: 1} if made else {},
+        compiler_params=pltpu.CompilerParams(vmem_limit_bytes=VMEM_LIMIT),
+        cost_estimate=pl.CostEstimate(
+            flops=10**8, bytes_accessed=3 * MIB * (last - first), transcendentals=0
+        ),
         name="new_soil",
-    )(through, lost, canopy, in_hbm(soil), in_hbm(porosity), in_hbm(drainage))
+    )(through, lost, canopy, in_hbm(soil), in_hbm(porosity), in_hbm(drainage), *more)
 
 
 def halo_parts(value, axis, dim, width):
@@ -559,7 +563,7 @@
     )(tall, before, after)
 
 
-def river_kernel(state, strips, fixed, out):
+def river_kernel(state, strips, fixed, _, out):
     height, width = state.shape
 
     def strip(down, right):
@@ -589,14 +593,15 @@
     out[...] = storage[:height, :width]
 
 
-def river(state, strips, fixed):
+def river(state, strips, fixed, after):
     return pl.pallas_call(
         river_kernel,
+        in_specs=[pl.BlockSpec(memory_space=pltpu.VMEM)] * 3 + [pl.BlockSpec(memory_space=pl.ANY)],
         out_shape=jax.ShapeDtypeStruct(state.shape, jnp.float32),
         compiler_params=pltpu.CompilerParams(vmem_limit_bytes=VMEM_LIMIT),
         cost_estimate=pl.CostEstimate(flops=10**7, bytes_accessed=1 * MIB, transcendentals=0),
         name="river_steps",
-    )(state, strips, fixed)
+    )(state, strips, fixed, in_hbm(after))
 
 
 def exchange(value):
@@ -639,7 +644,10 @@
         patch_area, canopy_water, canopy_cap, soil_water, porosity, drainage, (above, below),
     )
     returned = exchange(sums)
-    soil_new, canopy_new = new_soil(through, lost, canopy, soil_water, porosity, drainage)
+    layers_of = (through, lost, canopy, soil_water, porosity, drainage)
+    blocks = worker_list.shape[0] // 96
+    early = blocks * 3 // 5
+    made = new_soil(0, early, *layers_of)
     code, place = unpack_plan(homes, capacity, lane_rows, home_slot, home_offset)
     fixed = jnp.concatenate([fixed, below, above], axis=1)
     initial, last = edge_columns(fixed, sums)
@@ -648,10 +656,14 @@
     after = lax.ppermute(initial, "col", [(i + 1, i) for i in range(count - 1)])
     fixed = static_halo(fixed, before, after)
     cell_runoff, storage, strips = unpack_runoff(
-        homes, returned, code, place, river_storage.reshape(lane_rows, LANES), fixed, in_hbm(canopy_new)
-    )
+        homes, returned, code, place, river_storage.reshape(lane_rows, LANES), fixed,
+        in_hbm(made[1]),
+    )
+    soil_new, canopy_new = new_soil(early, blocks, *layers_of, made, strips)
     cell_evap = unpack_evap(returned, code, place)
-    river_new = river(storage.reshape(river_storage.shape), exchange(strips), fixed)
+    river_new = river(
+        storage.reshape(river_storage.shape), exchange(strips), fixed, canopy_new
+    )
     return (
         soil_new,
         canopy_new,

time: 73.1 us -> 72.3 us (0.989)
  waiting for transfers between devices: 23.4 us -> 21.7 us
  Pallas kernels: 24.5 us -> 25.7 us
    all_to_all x3, starting transfers between devices: 15.2 us -> 14 us  [exchange(): return lax.all_to_all(value, axes, split_axis=0, concat_axis=0, tiled=True)]
    pallas_call x2 -> x3, Pallas kernels: 8.68 us -> 9.57 us  [the longest x2 8.36 us: new_soil(): pl.pallas_call(new_soil_kernel, grid=(last - first,), in_specs=[flat, fla...]
    ppermute x2, waiting for transfers between devices: 6.33 us -> 5.45 us  [halo_parts(): return (lax.ppermute(last, axis, up), lax.ppermute(initial, axis, down))]
    ppermute x2, starting transfers between devices: 4.97 us -> 5.84 us  [halo_parts(): return (lax.ppermute(last, axis, up), lax.ppermute(initial, axis, down))]
    all_to_all x3, waiting for transfers between devices: 17.1 us -> 16.2 us  [exchange(): return lax.all_to_all(value, axes, split_axis=0, concat_axis=0, tiled=True)]
  transfers between devices with their start and end apart: 7 -> 7, of which waited for: 4 -> 5; matrix products, arithmetic and copies ran while one was open for 0% -> 0% of each run, Pallas kernels for 16% -> 17%
where the time goes in v1:
time: 72.3 us; the launch traced here: 71.8 us
  Pallas kernels  25.7 us (36%)
  starting transfers between devices  23.3 us (32%)
  waiting for transfers between devices  21.7 us (30%)
  between operations  0.91 us (1%)
    all_to_all x3, waiting for transfers between devices, exchange(): return lax.all_to_all(value, axes, split_axis=0, concat_axis=0, tiled=True)  16.2 us
    all_to_all x3, starting transfers between devices, exchange(): return lax.all_to_all(value, axes, split_axis=0, concat_axis=0, tiled=True)  14 us
    pallas_call x2, Pallas kernels, new_soil(): pl.pallas_call(new_soil_kernel, grid=(last - first,), in_specs=[flat, fla...  8.36 us
    pallas_call x1, Pallas kernels, land_sums(): pl.pallas_call(functools.partial(land_sums_kernel, pairs), in_specs=[pl.B...  7.25 us
    ppermute x2, starting transfers between devices, halo_parts(): return (lax.ppermute(last, axis, up), lax.ppermute(initial, axis, down))  5.84 us
    ppermute x2, waiting for transfers between devices, halo_parts(): return (lax.ppermute(last, axis, up), lax.ppermute(initial, axis, down))  5.45 us
    pallas_call x1, Pallas kernels, pack(): pl.pallas_call(functools.partial(pack_kernel, homes, capacity), in_specs=...  3.61 us
    ppermute x1, starting transfers between devices, shards(): before = lax.ppermute(last, 'col', [(i, i + 1) for i in range(count - 1)])  2.17 us
  transfers between devices with their start and end apart: 7, of which 5 were waited for; matrix products, arithmetic and copies ran while one was open for 0% of the time, Pallas kernels for 17%

profile of v1, /device:TPU:0, one launch (start us, length us, event | category | flops | bytes accessed | tf_op | source)
XLA Modules:
  0.0 71.8 jit_solution(11602547016002790123)
XLA Ops:
  0.6 0.0 copy-start.9
  0.6 0.0 copy-start.8
  0.7 0.0 copy-start.4
  0.7 0.0 copy-start
  0.7 0.0 copy-start.3
  0.7 0.0 copy-start.2
  0.7 0.0 copy-start.1
  0.7 3.6 %pack_forcing.1 = f32[1536,128]{1,0:T(8,128)} custom-call(s32[1,1024]{1,0:T(1,128)} %slot.1, s32[1,1024]{1,0:T(1,128)} %offset.1, f32[3,64,128]{2,1,0:T(8,128)} %forcing_in.1), custom_call_target="tpu_custom_call" | custom-call | flops 1000000000 | bytes 2097152 | tf_op jit(solution)/shard_map/pack_forcing/pallas_call | solution.py:166
  4.3 7.3 %all-to-all-start = ((f32[32,48,128]{2,1,0:T(8,128)}), f32[32,48,128]{2,1,0:T(8,128)S(1)}, u32[]{:S(2)}, u32[]{:S(2)}) async-start(f32[32,48,128]{2,1,0:T(8,128)} %bitcast), calls=%async_computation | async-start | bytes 1572864 | tf_op jit(solution)/shard_map/all_to_all | solution.py:608
  11.6 0.0 copy-done.9
  11.7 0.0 copy-done.8
  11.7 1.3 %collective-permute-start.1 = (f32[2,4,128]{2,1,0:T(4,128)S(1)}, f32[2,4,128]{2,1,0:T(4,128)S(1)}, u32[]{:S(2)}, u32[]{:S(2)}) collective-permute-start(f32[2,4,128]{2,1,0:T(4,128)S(1)} %get-tuple-element.35), channel_id=1, source_target_pairs={{8,0},{16,8},{24,16},{9,1},{17,9},{25,17},{10,2},{18,10},{26,18},{... | collective-permute-start | bytes 12296 | tf_op jit(solution)/shard_map/ppermute | solution.py:490
  13.0 4.5 %collective-permute-start = (f32[2,4,128]{2,1,0:T(4,128)S(1)}, f32[2,4,128]{2,1,0:T(4,128)S(1)}, u32[]{:S(2)}, u32[]{:S(2)}) collective-permute-start(f32[2,4,128]{2,1,0:T(4,128)S(1)} %get-tuple-element.36), channel_id=1, source_target_pairs={{0,8},{8,16},{16,24},{1,9},{9,17},{17,25},{2,10},{10,18},{18,26},{... | collective-permute-start | bytes 12296 | tf_op jit(solution)/shard_map/ppermute | solution.py:490
  17.5 0.0 copy-done.4
  17.5 0.1 copy.21.worker
  17.7 0.0 copy-done
  17.7 1.9 %segment_plan.1.meta = s32[480,128]{1,0:T(8,128)S(1)} custom-call(s32[480,128]{1,0:T(8,128)S(1)} %copy-done, s32[480,1]{1,0:T(8,128)S(1)} %copy.21.worker), custom_call_target="tpu_custom_call" | custom-call | flops 100000000 | bytes 1048576 | tf_op jit(solution)/shard_map/segment_plan/pallas_call | solution.py:301
  19.6 2.3 %collective-permute-done.1.__ = f32[2,4,128]{2,1,0:T(4,128)S(1)} collective-permute-done((f32[2,4,128]{2,1,0:T(4,128)S(1)}, f32[2,4,128]{2,1,0:T(4,128)S(1)}, u32[]{:S(2)}, u32[]{:S(2)}) %collective-permute-start.1) | collective-permute-done | bytes 4128 | tf_op jit(solution)/shard_map/ppermute | solution.py:490
  22.0 3.1 %collective-permute-done._ = f32[2,4,128]{2,1,0:T(4,128)S(1)} collective-permute-done((f32[2,4,128]{2,1,0:T(4,128)S(1)}, f32[2,4,128]{2,1,0:T(4,128)S(1)}, u32[]{:S(2)}, u32[]{:S(2)}) %collective-permute-start) | collective-permute-done | bytes 4128 | tf_op jit(solution)/shard_map/ppermute | solution.py:490
  25.1 7.2 %all-to-all-done = f32[32,48,128]{2,1,0:T(8,128)S(1)} async-done(((f32[32,48,128]{2,1,0:T(8,128)}), f32[32,48,128]{2,1,0:T(8,128)S(1)}, u32[]{:S(2)}, u32[]{:S(2)}) %all-to-all-start) | async-done | bytes 786464 | tf_op jit(solution)/shard_map/all_to_all | solution.py:608
  32.3 0.0 copy-done.3
  32.3 0.0 copy-done.2
  32.3 0.0 copy-done.1
  32.3 0.0 copy-start.6
  32.3 0.0 copy-start.7
  32.3 7.3 %land_sums.1 = (f32[480,128]{1,0:T(8,128)S(1)}, f32[480,128]{1,0:T(8,128)S(1)}, f32[480,128]{1,0:T(8,128)S(1)}, f32[1024,128]{1,0:T(8,128)}) custom-call(s32[480]{0:T(512)S(1)} %copy-done.4, s32[480]{0:T(512)S(1)} %fusion.2.first_rows, f32[1536,128]{1,0:T(8,128)S(1)} %bitcast.10, s32[480,128]{1,0:T(8,128)S(1)} %copy-done, s32[480,128]{1,0:T(8,128)S(1)} %segment_plan.1.meta, ...), custom_call_target="tpu_custom_call" | custom-call | flops 100000000 | bytes 20971520 | tf_op jit(solution)/shard_map/land_sums/pallas_call | solution.py:423
  39.6 3.6 %all-to-all-start.1 = ((f32[32,32,128]{2,1,0:T(8,128)}), f32[32,32,128]{2,1,0:T(8,128)S(1)}, u32[]{:S(2)}, u32[]{:S(2)}) async-start(f32[32,32,128]{2,1,0:T(8,128)} %bitcast.5), calls=%async_computation.1 | async-start | bytes 1048576 | tf_op jit(solution)/shard_map/all_to_all | solution.py:608
  43.2 0.0 copy-done.6
  43.2 0.0 copy-done.7
  43.2 0.7 unpack_plan.1
  43.9 0.1 edge_columns.1
  44.0 2.2 %collective-permute-start.2 = (f32[8,128]{1,0:T(8,128)S(1)}, f32[8,128]{1,0:T(8,128)S(1)}, u32[]{:S(2)}, u32[]{:S(2)}) collective-permute-start(f32[8,128]{1,0:T(8,128)S(1)} %get-tuple-element.28), channel_id=1, source_target_pairs={{0,1},{1,2},{2,3},{3,4},{4,5},{5,6},{6,7},{8,9},{9,10},{10,11},{11... | collective-permute-start | bytes 12296 | tf_op jit(solution)/shard_map/ppermute | solution.py:655
  46.2 1.3 %collective-permute-start.3 = (f32[8,128]{1,0:T(8,128)S(1)}, f32[8,128]{1,0:T(8,128)S(1)}, u32[]{:S(2)}, u32[]{:S(2)}) collective-permute-start(f32[8,128]{1,0:T(8,128)S(1)} %get-tuple-element.29), channel_id=1, source_target_pairs={{1,0},{2,1},{3,2},{4,3},{5,4},{6,5},{7,6},{9,8},{10,9},{11,10},{12... | collective-permute-start | bytes 12296 | tf_op jit(solution)/shard_map/ppermute | solution.py:656
  47.5 0.0 copy-start.5
  47.5 5.1 %new_soil.2 = (f32[15,480,128]{2,1,0:T(8,128)}, f32[480,128]{1,0:T(8,128)}) custom-call(f32[480,128]{1,0:T(8,128)S(1)} %get-tuple-element.20.through, f32[480,128]{1,0:T(8,128)S(1)} %get-tuple-element.21.lost, f32[480,128]{1,0:T(8,128)S(1)} %get-tuple-element.22.canopy, f32[15,480,128]{2,1,0:T(8,128)} %soil.3, f32[15,480,128]{2,1,0:T(8,128)} %porosity.3, ...), custom_call_target="tpu_custom_call" | custom-call | flops 100000000 | bytes 9437184 | tf_op jit(solution)/shard_map/new_soil/pallas_call | solution.py:466
  52.5 0.0 collective-permute-done.2.before
  52.6 0.0 collective-permute-done.3.after
  52.6 0.1 static_halo.1._.fixed
  52.6 6.1 %all-to-all-done.1 = f32[32,32,128]{2,1,0:T(8,128)S(1)} async-done(((f32[32,32,128]{2,1,0:T(8,128)}), f32[32,32,128]{2,1,0:T(8,128)S(1)}, u32[]{:S(2)}, u32[]{:S(2)}) %all-to-all-start.1) | async-done | bytes 524320 | tf_op jit(solution)/shard_map/all_to_all | solution.py:608
  58.8 0.0 copy-done.5
  58.8 1.4 %unpack_runoff.1 = (f32[64,128]{1,0:T(8,128)}, f32[64,128]{1,0:T(8,128)S(1)}, f32[128,128]{1,0:T(8,128)}) custom-call(f32[1024,128]{1,0:T(8,128)S(1)} %bitcast.11, s32[1024,128]{1,0:T(8,128)S(1)} %get-tuple-element.26.code, bf16[64,1024]{1,0:T(8,128)(2,1)S(1)} %get-tuple-element.27.place, f32[64,128]{1,0:T(8,128)S(1)} %copy-done.5, ...), custom_call_target="tpu_custom_call" | custom-call | flops 1000000000 | bytes 1048576 | tf_op jit(solution)/shard_map/unpack_runoff/pallas_call | solution.py:261
  60.1 3.1 %all-to-all-start.2 = ((f32[32,4,128]{2,1,0:T(4,128)}), f32[32,4,128]{2,1,0:T(4,128)S(1)}, u32[]{:S(2)}, u32[]{:S(2)}) async-start(f32[32,4,128]{2,1,0:T(4,128)} %bitcast.7), calls=%async_computation.2 | async-start | bytes 131072 | tf_op jit(solution)/shard_map/all_to_all | solution.py:608
  63.2 3.3 %new_soil.3 = (f32[15,480,128]{2,1,0:T(8,128)}, f32[480,128]{1,0:T(8,128)}) custom-call(f32[480,128]{1,0:T(8,128)S(1)} %get-tuple-element.20.through, f32[480,128]{1,0:T(8,128)S(1)} %get-tuple-element.21.lost, f32[480,128]{1,0:T(8,128)S(1)} %get-tuple-element.22.canopy, f32[15,480,128]{2,1,0:T(8,128)} %soil.3, ...), custom_call_target="tpu_custom_call", output_to_operand_aliasing={{0}: (6, {}), {1}: (7, {})} | custom-call | flops 100000000 | bytes 6291456 | tf_op jit(solution)/shard_map/new_soil/pallas_call | solution.py:466
  66.5 1.2 %unpack_evap.1 = f32[64,128]{1,0:T(8,128)} custom-call(f32[1024,128]{1,0:T(8,128)S(1)} %bitcast.12, s32[1024,128]{1,0:T(8,128)S(1)} %get-tuple-element.26.code, bf16[64,1024]{1,0:T(8,128)(2,1)S(1)} %get-tuple-element.27.place), custom_call_target="tpu_custom_call" | custom-call | flops 1000000000 | bytes 1048576 | tf_op jit(solution)/shard_map/unpack_evap/pallas_call | solution.py:277
  67.7 2.9 %all-to-all-done.2 = f32[32,4,128]{2,1,0:T(4,128)S(1)} async-done(((f32[32,4,128]{2,1,0:T(4,128)}), f32[32,4,128]{2,1,0:T(4,128)S(1)}, u32[]{:S(2)}, u32[]{:S(2)}) %all-to-all-start.2) | async-done | bytes 65568 | tf_op jit(solution)/shard_map/all_to_all | solution.py:608
  70.6 1.2 %river_steps.1 = f32[64,128]{1,0:T(8,128)} custom-call(f32[64,128]{1,0:T(8,128)S(1)} %get-tuple-element.34.state, f32[128,128]{1,0:T(8,128)S(1)} %bitcast.13, f32[2,72,256]{2,1,0:T(8,128)S(1)} %static_halo.1._.fixed, f32[480,128]{1,0:T(8,128)} %get-tuple-element.16._), custom_call_target="tpu_custom_call" | custom-call | flops 10000000 | bytes 1048576 | tf_op jit(solution)/shard_map/river_steps/pallas_call | solution.py:597
  (4 shorter events, 0.0 us)
Async XLA Ops:
  0.6 11.0 %copy-start.9 = (s32[64,128]{1,0:T(8,128)S(1)}, s32[64,128]{1,0:T(8,128)}, u32[]{:S(2)}) copy-start(s32[64,128]{1,0:T(8,128)} %param.17) | copy-start | bytes 98308
  0.6 11.0 %copy-start.8 = (f32[64,128]{1,0:T(8,128)S(1)}, f32[64,128]{1,0:T(8,128)}, u32[]{:S(2)}) copy-start(f32[64,128]{1,0:T(8,128)} %param.16) | copy-start | bytes 98308
  0.7 16.9 %copy-start.4 = (s32[480]{0:T(512)S(1)}, s32[480]{0:T(512)}, u32[]{:S(2)}) copy-start(s32[480]{0:T(512)} %slots.1) | copy-start | bytes 5764
  0.7 17.1 %copy-start = (s32[480,128]{1,0:T(8,128)S(1)}, s32[480,128]{1,0:T(8,128)}, u32[]{:S(2)}) copy-start(s32[480,128]{1,0:T(8,128)} %cell.3) | copy-start | bytes 737284
  0.7 31.6 %copy-start.3 = (f32[480,128]{1,0:T(8,128)S(1)}, f32[480,128]{1,0:T(8,128)}, u32[]{:S(2)}) copy-start(f32[480,128]{1,0:T(8,128)} %cap.1) | copy-start | bytes 737284
  0.7 31.6 %copy-start.2 = (f32[480,128]{1,0:T(8,128)S(1)}, f32[480,128]{1,0:T(8,128)}, u32[]{:S(2)}) copy-start(f32[480,128]{1,0:T(8,128)} %water.1) | copy-start | bytes 737284
  0.7 31.6 %copy-start.1 = (f32[480,128]{1,0:T(8,128)S(1)}, f32[480,128]{1,0:T(8,128)}, u32[]{:S(2)}) copy-start(f32[480,128]{1,0:T(8,128)} %area.1) | copy-start | bytes 737284
  4.3 28.0 %all-to-all-start = ((f32[32,48,128]{2,1,0:T(8,128)}), f32[32,48,128]{2,1,0:T(8,128)S(1)}, u32[]{:S(2)}, u32[]{:S(2)}) async-start(f32[32,48,128]{2,1,0:T(8,128)} %bitcast), calls=%async_computation | async-start | bytes 1572864 | tf_op jit(solution)/shard_map/all_to_all | solution.py:608
  11.7 10.3 %collective-permute-start.1 = (f32[2,4,128]{2,1,0:T(4,128)S(1)}, f32[2,4,128]{2,1,0:T(4,128)S(1)}, u32[]{:S(2)}, u32[]{:S(2)}) collective-permute-start(f32[2,4,128]{2,1,0:T(4,128)S(1)} %get-tuple-element.35), channel_id=1, source_target_pairs={{8,0},{16,8},{24,16},{9,1},{17,9},{25,17},{10,2},{18,10},{26,18},{... | collective-permute-start | bytes 12296 | tf_op jit(solution)/shard_map/ppermute | solution.py:490
  13.0 12.1 %collective-permute-start = (f32[2,4,128]{2,1,0:T(4,128)S(1)}, f32[2,4,128]{2,1,0:T(4,128)S(1)}, u32[]{:S(2)}, u32[]{:S(2)}) collective-permute-start(f32[2,4,128]{2,1,0:T(4,128)S(1)} %get-tuple-element.36), channel_id=1, source_target_pairs={{0,8},{8,16},{16,24},{1,9},{9,17},{17,25},{2,10},{10,18},{18,26},{... | collective-permute-start | bytes 12296 | tf_op jit(solution)/shard_map/ppermute | solution.py:490
  32.3 10.9 %copy-start.6 = (s32[1,1024]{1,0:T(1,128)S(1)}, s32[1,1024]{1,0:T(1,128)}, u32[]{:S(2)}) copy-start(s32[1,1024]{1,0:T(1,128)} %slot.1) | copy-start | bytes 12292
  32.3 10.9 %copy-start.7 = (s32[1,1024]{1,0:T(1,128)S(1)}, s32[1,1024]{1,0:T(1,128)}, u32[]{:S(2)}) copy-start(s32[1,1024]{1,0:T(1,128)} %offset.1) | copy-start | bytes 12292
  39.6 19.2 %all-to-all-start.1 = ((f32[32,32,128]{2,1,0:T(8,128)}), f32[32,32,128]{2,1,0:T(8,128)S(1)}, u32[]{:S(2)}, u32[]{:S(2)}) async-start(f32[32,32,128]{2,1,0:T(8,128)} %bitcast.5), calls=%async_computation.1 | async-start | bytes 1048576 | tf_op jit(solution)/shard_map/all_to_all | solution.py:608
  44.0 8.5 %collective-permute-start.2 = (f32[8,128]{1,0:T(8,128)S(1)}, f32[8,128]{1,0:T(8,128)S(1)}, u32[]{:S(2)}, u32[]{:S(2)}) collective-permute-start(f32[8,128]{1,0:T(8,128)S(1)} %get-tuple-element.28), channel_id=1, source_target_pairs={{0,1},{1,2},{2,3},{3,4},{4,5},{5,6},{6,7},{8,9},{9,10},{10,11},{11... | collective-permute-start | bytes 12296 | tf_op jit(solution)/shard_map/ppermute | solution.py:655
  46.2 6.4 %collective-permute-start.3 = (f32[8,128]{1,0:T(8,128)S(1)}, f32[8,128]{1,0:T(8,128)S(1)}, u32[]{:S(2)}, u32[]{:S(2)}) collective-permute-start(f32[8,128]{1,0:T(8,128)S(1)} %get-tuple-element.29), channel_id=1, source_target_pairs={{1,0},{2,1},{3,2},{4,3},{5,4},{6,5},{7,6},{9,8},{10,9},{11,10},{12... | collective-permute-start | bytes 12296 | tf_op jit(solution)/shard_map/ppermute | solution.py:656
  47.5 11.3 %copy-start.5 = (f32[64,128]{1,0:T(8,128)S(1)}, f32[64,128]{1,0:T(8,128)}, u32[]{:S(2)}) copy-start(f32[64,128]{1,0:T(8,128)} %river.1) | copy-start | bytes 98308
  60.1 10.5 %all-to-all-start.2 = ((f32[32,4,128]{2,1,0:T(4,128)}), f32[32,4,128]{2,1,0:T(4,128)S(1)}, u32[]{:S(2)}, u32[]{:S(2)}) async-start(f32[32,4,128]{2,1,0:T(4,128)} %bitcast.7), calls=%async_computation.2 | async-start | bytes 131072 | tf_op jit(solution)/shard_map/all_to_all | solution.py:608

commit v2 on v1

--- a/solution.py
+++ b/solution.py
@@ -63,7 +63,7 @@
     return by_worker, row.astype(jnp.bfloat16), lane.astype(jnp.bfloat16)
 
 
-def slot_columns(slot, offset, homes, capacity, split=False):
+def slot_table(slot, offset, homes, capacity, split=False):
     slots = slot.shape[1]
     by_worker, row, lane = slot_factors(slot, offset, homes, capacity)
     table = matmul(by_worker, jnp.concatenate([row, lane], axis=0), 1, 1)
@@ -75,10 +75,14 @@
     number = iota(spread.shape, 0)
     position = number % (capacity // groups) * groups + number // (slots // groups)
     place = position == iota(spread.shape, 1) % capacity
-    kept = jnp.where(place, spread, 0.0).astype(jnp.bfloat16)
-    shape = (2 * capacity, 2 * LANES)
-    gather = onehot((iota(shape, 0) >= capacity) == (iota(shape, 1) >= LANES))
-    columns = matmul(kept, gather).astype(jnp.int32)
+    return jnp.where(place, spread, 0.0).astype(jnp.bfloat16)
+
+
+def slot_columns(table):
+    width = table.shape[1]
+    shape = (width, 2 * LANES)
+    gather = onehot((iota(shape, 0) >= width // 2) == (iota(shape, 1) >= LANES))
+    columns = matmul(table, gather).astype(jnp.int32)
     return columns[:, :LANES] - 1, columns[:, LANES:]
 
 
@@ -97,8 +101,7 @@
 
 
 def pack_kernel(
-    homes, capacity, slot_in, offset_in, forcing_in, out, slot, offset, forcing, row_of, lane_of,
-    rain, ready,
+    homes, capacity, slot_in, offset_in, forcing_in, out, slot, offset, forcing, rain, ready
 ):
     copies = [
         pltpu.make_async_copy(source, target, ready.at[i])
@@ -113,7 +116,7 @@
     lane_rows = forcing.shape[1]
     copies[0].wait()
     copies[1].wait()
-    row_of[...], lane_of[...] = slot_columns(slot[...], offset[...], homes, capacity, True)
+    places = slot_table(slot[...], offset[...], homes, capacity, True)
     copies[2].wait()
     parts = []
     for var in range(3):
@@ -125,8 +128,7 @@
     here = iota((chunk, LANES), 1)
     for start in range(0, slots, chunk):
         odd = start >= slots // 2
-        row = row_of[pl.ds(start, chunk), :]
-        lane = lane_of[pl.ds(start, chunk), :]
+        row, lane = slot_columns(places[start : start + chunk])
         shape = (chunk, 3 * lane_rows)
         wide = jnp.concatenate([row, row], axis=1)[:, : 3 * lane_rows]
         pick = onehot(wide == iota(shape, 1) % lane_rows)
@@ -171,8 +173,6 @@
             pltpu.VMEM(slot.shape, jnp.int32),
             pltpu.VMEM(offset.shape, jnp.int32),
             pltpu.VMEM(forcing.shape, jnp.float32),
-            pltpu.VMEM((slots, LANES), jnp.int32),
-            pltpu.VMEM((slots, LANES), jnp.int32),
             pltpu.VMEM((slots // 2, LANES), jnp.float32),
             pltpu.SemaphoreType.DMA((3,)),
         ],
@@ -184,7 +184,7 @@
 
 def unpack_plan_kernel(homes, capacity, lane_rows, slot, offset, code, place):
     slots = slot.shape[1]
-    row, lane = slot_columns(slot[...], offset[...], homes, capacity)
+    row, lane = slot_columns(slot_table(slot[...], offset[...], homes, capacity))
     here = iota((slots, LANES), 1)
     index = (here - lane) & 127
     inside = (index < WINDOW) & (row >= 0)
@@ -310,16 +310,16 @@
 def land_sums_kernel(
     pairs, slots, first_rows, arrived, cell, meta, area, water, cap, soil_in, porosity_in,
     drainage_in, _, __, through, lost, canopy_new, sums_out, soil, porosity, drainage, fetched,
-    runoffs, evaps, sums, ready,
+    runoffs, evaps, ready,
 ):
     layers, rows = soil.shape[:2]
     steps = ready.shape[0]
     block = rows // steps
-    ahead = 4
+    chunk = block // 2
     arrays = ((soil_in, soil), (porosity_in, porosity), (drainage_in, drainage))
 
     def part_of(step):
-        return pl.ds(pl.multiple_of(step * block, block), block)
+        return pl.ds(step * block, block)
 
     def reads(step):
         return [
@@ -329,22 +329,15 @@
             for i, (source, target) in enumerate(arrays)
         ]
 
-    def start_reads(step):
-        for copy in reads(step):
-            copy.start()
-
     def fetch(step):
-        base = pl.multiple_of(step % 2 * (2 * block), 2 * block)
-        for i in range(block):
-            row = first_rows[step * block + i]
-            fetched[pl.ds(base + 2 * i, 2), :] = arrived[pl.ds(row, 2, stride=pairs), :]
-
-    def cascade(step):
-        part = part_of(step)
-        base = pl.multiple_of(step % 2 * (2 * block), 2 * block)
+        for i in range(step * block, (step + 1) * block):
+            fetched[pl.ds(2 * i, 2), :] = arrived[pl.ds(first_rows[i], 2, stride=pairs), :]
+
+    def cascade(start):
+        part = pl.ds(start, chunk)
         index = cell[part, :]
-        one = fetched[pl.ds(base, block, stride=2), :]
-        two = fetched[pl.ds(base + 1, block, stride=2), :]
+        one = fetched[pl.ds(2 * start, chunk, stride=2), :]
+        two = fetched[pl.ds(2 * start + 1, chunk, stride=2), :]
         odd = meta[part, :] >> 8
         loss = jnp.where(odd == 1, two, one)
         rain = lane_pick(jnp.where(odd == 1, one, two), index + odd * WINDOW)
@@ -370,45 +363,41 @@
                 evaps[part, :] = area[part, :] * (canopy_loss + soil_loss)
         runoffs[part, :] = area[part, :] * (surface + flowing)
 
-    def hand_back(start, count):
-        part = pl.ds(start, count)
+    def scan(step):
+        part = part_of(step)
         shape = (2 * LANES, LANES)
         upto = onehot((iota(shape, 0) & 127) <= iota(shape, 1))
         patches = meta[part, :] & 255
         last = jnp.maximum(patches - 1, 0)
-        here = iota((count, LANES), 1)
+        here = iota((block, LANES), 1)
         picked = [
             lane_pick(matmul(jnp.concatenate(halves(value[part, :]), axis=1), upto), last)
             for value in (runoffs, evaps)
         ]
         reached = jnp.where(patches > 0, jnp.where(here < WINDOW, *picked), 0.0)
         before = jnp.where((here & (WINDOW - 1)) == 0, 0.0, pltpu.roll(reached, 1, 1))
-        sums[...] = reached - before
-        for i in range(count):
-            sums_out[pl.ds(slots[start + i], 1), :] = sums[pl.ds(i, 1), :]
-
-    start_reads(0)
-    fetch(0)
-    start_reads(1)
+        runoffs[part, :] = reached - before
+
+    def hand_back(step):
+        for i in range(step * block, (step + 1) * block):
+            sums_out[pl.ds(slots[i], 1), :] = runoffs[pl.ds(i, 1), :]
+
+    for step in range(steps):
+        for copy in reads(step):
+            copy.start()
     sums_out[...] = jnp.zeros_like(sums_out)
-    start_reads(2)
-    start_reads(3)
-
-    def round_of(step, carry):
-        for copy in reads(step):
-            copy.wait()
-
-        @pl.when(step + ahead < steps)
-        def _():
-            start_reads(step + ahead)
-
-        cascade(step)
-        fetch(jnp.minimum(step + 1, steps - 1))
-        return carry
-
-    for half in range(2):
-        lax.fori_loop(half * steps // 2, (half + 1) * steps // 2, round_of, 0)
-        hand_back(half * rows // 2, rows // 2)
+    for step in range(steps):
+        fetch(step)
+    for step in range(steps + 2):
+        if step < steps:
+            for copy in reads(step):
+                copy.wait()
+            for start in range(step * block, (step + 1) * block, chunk):
+                cascade(start)
+        if 1 <= step <= steps:
+            scan(step - 1)
+        if step >= 2:
+            hand_back(step - 2)
 
 
 def land_sums(
@@ -416,8 +405,7 @@
     drainage, after,
 ):
     layers, rows = soil.shape[:2]
-    steps = 10
-    block = rows // steps
+    steps = 5
     near = pl.BlockSpec(memory_space=pltpu.VMEM)
     far = pl.BlockSpec(memory_space=pltpu.HBM)
     return pl.pallas_call(
@@ -426,9 +414,9 @@
         + [pl.BlockSpec(memory_space=pl.ANY)] * 2,
         out_specs=[near] * 4,
         scratch_shapes=[pltpu.VMEM(soil.shape, jnp.float32)] * 3
-        + [pltpu.VMEM((4 * block, LANES), jnp.float32)]
+        + [pltpu.VMEM((2 * rows, LANES), jnp.float32)]
         + [pltpu.VMEM((rows, LANES), jnp.float32)] * 2
-        + [pltpu.VMEM((rows // 2, LANES), jnp.float32), pltpu.SemaphoreType.DMA((steps, 3))],
+        + [pltpu.SemaphoreType.DMA((steps, 3))],
         out_shape=[jax.ShapeDtypeStruct((rows, LANES), jnp.float32)] * 3
         + [jax.ShapeDtypeStruct(sums_shape, jnp.float32)],
         compiler_params=pltpu.CompilerParams(vmem_limit_bytes=VMEM_LIMIT),

time: 72.3 us -> 71.4 us (0.988)
  Pallas kernels: 25.7 us -> 24.8 us
    pallas_call x1, Pallas kernels: 7.25 us -> 6.27 us  [land_sums(): pl.pallas_call(functools.partial(land_sums_kernel, pairs), in_specs=[pl.B...]
where the time goes in v2:
time: 71.4 us; the launch traced here: 70.9 us
  Pallas kernels  24.8 us (35%)
  starting transfers between devices  23.3 us (33%)
  waiting for transfers between devices  21.7 us (30%)
  between operations  0.91 us (1%)
    all_to_all x3, waiting for transfers between devices, exchange(): return lax.all_to_all(value, axes, split_axis=0, concat_axis=0, tiled=True)  16.2 us
    all_to_all x3, starting transfers between devices, exchange(): return lax.all_to_all(value, axes, split_axis=0, concat_axis=0, tiled=True)  14 us
    pallas_call x2, Pallas kernels, new_soil(): pl.pallas_call(new_soil_kernel, grid=(last - first,), in_specs=[flat, fla...  8.36 us
    pallas_call x1, Pallas kernels, land_sums(): pl.pallas_call(functools.partial(land_sums_kernel, pairs), in_specs=[pl.B...  6.27 us
    ppermute x2, starting transfers between devices, halo_parts(): return (lax.ppermute(last, axis, up), lax.ppermute(initial, axis, down))  5.84 us
    ppermute x2, waiting for transfers between devices, halo_parts(): return (lax.ppermute(last, axis, up), lax.ppermute(initial, axis, down))  5.45 us
    pallas_call x1, Pallas kernels, pack(): pl.pallas_call(functools.partial(pack_kernel, homes, capacity), in_specs=...  3.7 us
    ppermute x1, starting transfers between devices, shards(): before = lax.ppermute(last, 'col', [(i, i + 1) for i in range(count - 1)])  2.17 us
  transfers between devices with their start and end apart: 7, of which 5 were waited for; matrix products, arithmetic and copies ran while one was open for 0% of the time, Pallas kernels for 17%

profile of v2, /device:TPU:0, one launch (start us, length us, event | category | flops | bytes accessed | tf_op | source)
XLA Modules:
  0.0 70.9 jit_solution(7088299129354683637)
XLA Ops:
  0.6 0.0 copy-start.9
  0.6 0.0 copy-start.8
  0.7 0.0 copy-start.4
  0.7 0.0 copy-start
  0.7 0.0 copy-start.3
  0.7 0.0 copy-start.2
  0.7 0.0 copy-start.1
  0.7 3.7 %pack_forcing.1 = f32[1536,128]{1,0:T(8,128)} custom-call(s32[1,1024]{1,0:T(1,128)} %slot.1, s32[1,1024]{1,0:T(1,128)} %offset.1, f32[3,64,128]{2,1,0:T(8,128)} %forcing_in.1), custom_call_target="tpu_custom_call" | custom-call | flops 1000000000 | bytes 2097152 | tf_op jit(solution)/shard_map/pack_forcing/pallas_call | solution.py:168
  4.4 7.3 %all-to-all-start = ((f32[32,48,128]{2,1,0:T(8,128)}), f32[32,48,128]{2,1,0:T(8,128)S(1)}, u32[]{:S(2)}, u32[]{:S(2)}) async-start(f32[32,48,128]{2,1,0:T(8,128)} %bitcast), calls=%async_computation | async-start | bytes 1572864 | tf_op jit(solution)/shard_map/all_to_all | solution.py:596
  11.7 0.0 copy-done.9
  11.7 0.0 copy-done.8
  11.8 1.3 %collective-permute-start.1 = (f32[2,4,128]{2,1,0:T(4,128)S(1)}, f32[2,4,128]{2,1,0:T(4,128)S(1)}, u32[]{:S(2)}, u32[]{:S(2)}) collective-permute-start(f32[2,4,128]{2,1,0:T(4,128)S(1)} %get-tuple-element.35), channel_id=1, source_target_pairs={{8,0},{16,8},{24,16},{9,1},{17,9},{25,17},{10,2},{18,10},{26,18},{... | collective-permute-start | bytes 12296 | tf_op jit(solution)/shard_map/ppermute | solution.py:478
  13.1 4.5 %collective-permute-start = (f32[2,4,128]{2,1,0:T(4,128)S(1)}, f32[2,4,128]{2,1,0:T(4,128)S(1)}, u32[]{:S(2)}, u32[]{:S(2)}) collective-permute-start(f32[2,4,128]{2,1,0:T(4,128)S(1)} %get-tuple-element.36), channel_id=1, source_target_pairs={{0,8},{8,16},{16,24},{1,9},{9,17},{17,25},{2,10},{10,18},{18,26},{... | collective-permute-start | bytes 12296 | tf_op jit(solution)/shard_map/ppermute | solution.py:478
  17.6 0.0 copy-done.4
  17.6 0.1 copy.21.worker
  17.8 0.0 copy-done
  17.8 1.9 %segment_plan.1.meta = s32[480,128]{1,0:T(8,128)S(1)} custom-call(s32[480,128]{1,0:T(8,128)S(1)} %copy-done, s32[480,1]{1,0:T(8,128)S(1)} %copy.21.worker), custom_call_target="tpu_custom_call" | custom-call | flops 100000000 | bytes 1048576 | tf_op jit(solution)/shard_map/segment_plan/pallas_call | solution.py:301
  19.7 2.3 %collective-permute-done.1.__ = f32[2,4,128]{2,1,0:T(4,128)S(1)} collective-permute-done((f32[2,4,128]{2,1,0:T(4,128)S(1)}, f32[2,4,128]{2,1,0:T(4,128)S(1)}, u32[]{:S(2)}, u32[]{:S(2)}) %collective-permute-start.1) | collective-permute-done | bytes 4128 | tf_op jit(solution)/shard_map/ppermute | solution.py:478
  22.1 3.1 %collective-permute-done._ = f32[2,4,128]{2,1,0:T(4,128)S(1)} collective-permute-done((f32[2,4,128]{2,1,0:T(4,128)S(1)}, f32[2,4,128]{2,1,0:T(4,128)S(1)}, u32[]{:S(2)}, u32[]{:S(2)}) %collective-permute-start) | collective-permute-done | bytes 4128 | tf_op jit(solution)/shard_map/ppermute | solution.py:478
  25.2 7.2 %all-to-all-done = f32[32,48,128]{2,1,0:T(8,128)S(1)} async-done(((f32[32,48,128]{2,1,0:T(8,128)}), f32[32,48,128]{2,1,0:T(8,128)S(1)}, u32[]{:S(2)}, u32[]{:S(2)}) %all-to-all-start) | async-done | bytes 786464 | tf_op jit(solution)/shard_map/all_to_all | solution.py:596
  32.4 0.0 copy-done.3
  32.4 0.0 copy-done.2
  32.4 0.0 copy-done.1
  32.4 0.0 copy-start.6
  32.4 0.0 copy-start.7
  32.4 6.3 %land_sums.1 = (f32[480,128]{1,0:T(8,128)S(1)}, f32[480,128]{1,0:T(8,128)S(1)}, f32[480,128]{1,0:T(8,128)S(1)}, f32[1024,128]{1,0:T(8,128)}) custom-call(s32[480]{0:T(512)S(1)} %copy-done.4, s32[480]{0:T(512)S(1)} %fusion.2.first_rows, f32[1536,128]{1,0:T(8,128)S(1)} %bitcast.10, s32[480,128]{1,0:T(8,128)S(1)} %copy-done, s32[480,128]{1,0:T(8,128)S(1)} %segment_plan.1.meta, ...), custom_call_target="tpu_custom_call" | custom-call | flops 100000000 | bytes 20971520 | tf_op jit(solution)/shard_map/land_sums/pallas_call | solution.py:411
  38.7 3.6 %all-to-all-start.1 = ((f32[32,32,128]{2,1,0:T(8,128)}), f32[32,32,128]{2,1,0:T(8,128)S(1)}, u32[]{:S(2)}, u32[]{:S(2)}) async-start(f32[32,32,128]{2,1,0:T(8,128)} %bitcast.5), calls=%async_computation.1 | async-start | bytes 1048576 | tf_op jit(solution)/shard_map/all_to_all | solution.py:596
  42.3 0.0 copy-done.6
  42.3 0.0 copy-done.7
  42.4 0.7 unpack_plan.1
  43.0 0.1 edge_columns.1
  43.1 2.2 %collective-permute-start.2 = (f32[8,128]{1,0:T(8,128)S(1)}, f32[8,128]{1,0:T(8,128)S(1)}, u32[]{:S(2)}, u32[]{:S(2)}) collective-permute-start(f32[8,128]{1,0:T(8,128)S(1)} %get-tuple-element.28), channel_id=1, source_target_pairs={{0,1},{1,2},{2,3},{3,4},{4,5},{5,6},{6,7},{8,9},{9,10},{10,11},{11... | collective-permute-start | bytes 12296 | tf_op jit(solution)/shard_map/ppermute | solution.py:643
  45.3 1.3 %collective-permute-start.3 = (f32[8,128]{1,0:T(8,128)S(1)}, f32[8,128]{1,0:T(8,128)S(1)}, u32[]{:S(2)}, u32[]{:S(2)}) collective-permute-start(f32[8,128]{1,0:T(8,128)S(1)} %get-tuple-element.29), channel_id=1, source_target_pairs={{1,0},{2,1},{3,2},{4,3},{5,4},{6,5},{7,6},{9,8},{10,9},{11,10},{12... | collective-permute-start | bytes 12296 | tf_op jit(solution)/shard_map/ppermute | solution.py:644
  46.6 0.0 copy-start.5
  46.6 5.1 %new_soil.2 = (f32[15,480,128]{2,1,0:T(8,128)}, f32[480,128]{1,0:T(8,128)}) custom-call(f32[480,128]{1,0:T(8,128)S(1)} %get-tuple-element.20.through, f32[480,128]{1,0:T(8,128)S(1)} %get-tuple-element.21.lost, f32[480,128]{1,0:T(8,128)S(1)} %get-tuple-element.22.canopy, f32[15,480,128]{2,1,0:T(8,128)} %soil.3, f32[15,480,128]{2,1,0:T(8,128)} %porosity.3, ...), custom_call_target="tpu_custom_call" | custom-call | flops 100000000 | bytes 9437184 | tf_op jit(solution)/shard_map/new_soil/pallas_call | solution.py:454
  51.7 0.0 collective-permute-done.2.before
  51.7 0.0 collective-permute-done.3.after
  51.7 0.1 static_halo.1._.fixed
  51.7 6.1 %all-to-all-done.1 = f32[32,32,128]{2,1,0:T(8,128)S(1)} async-done(((f32[32,32,128]{2,1,0:T(8,128)}), f32[32,32,128]{2,1,0:T(8,128)S(1)}, u32[]{:S(2)}, u32[]{:S(2)}) %all-to-all-start.1) | async-done | bytes 524320 | tf_op jit(solution)/shard_map/all_to_all | solution.py:596
  57.9 0.0 copy-done.5
  57.9 1.4 %unpack_runoff.1 = (f32[64,128]{1,0:T(8,128)}, f32[64,128]{1,0:T(8,128)S(1)}, f32[128,128]{1,0:T(8,128)}) custom-call(f32[1024,128]{1,0:T(8,128)S(1)} %bitcast.11, s32[1024,128]{1,0:T(8,128)S(1)} %get-tuple-element.26.code, bf16[64,1024]{1,0:T(8,128)(2,1)S(1)} %get-tuple-element.27.place, f32[64,128]{1,0:T(8,128)S(1)} %copy-done.5, ...), custom_call_target="tpu_custom_call" | custom-call | flops 1000000000 | bytes 1048576 | tf_op jit(solution)/shard_map/unpack_runoff/pallas_call | solution.py:261
  59.2 3.1 %all-to-all-start.2 = ((f32[32,4,128]{2,1,0:T(4,128)}), f32[32,4,128]{2,1,0:T(4,128)S(1)}, u32[]{:S(2)}, u32[]{:S(2)}) async-start(f32[32,4,128]{2,1,0:T(4,128)} %bitcast.7), calls=%async_computation.2 | async-start | bytes 131072 | tf_op jit(solution)/shard_map/all_to_all | solution.py:596
  62.3 3.3 %new_soil.3 = (f32[15,480,128]{2,1,0:T(8,128)}, f32[480,128]{1,0:T(8,128)}) custom-call(f32[480,128]{1,0:T(8,128)S(1)} %get-tuple-element.20.through, f32[480,128]{1,0:T(8,128)S(1)} %get-tuple-element.21.lost, f32[480,128]{1,0:T(8,128)S(1)} %get-tuple-element.22.canopy, f32[15,480,128]{2,1,0:T(8,128)} %soil.3, ...), custom_call_target="tpu_custom_call", output_to_operand_aliasing={{0}: (6, {}), {1}: (7, {})} | custom-call | flops 100000000 | bytes 6291456 | tf_op jit(solution)/shard_map/new_soil/pallas_call | solution.py:454
  65.6 1.2 %unpack_evap.1 = f32[64,128]{1,0:T(8,128)} custom-call(f32[1024,128]{1,0:T(8,128)S(1)} %bitcast.12, s32[1024,128]{1,0:T(8,128)S(1)} %get-tuple-element.26.code, bf16[64,1024]{1,0:T(8,128)(2,1)S(1)} %get-tuple-element.27.place), custom_call_target="tpu_custom_call" | custom-call | flops 1000000000 | bytes 1048576 | tf_op jit(solution)/shard_map/unpack_evap/pallas_call | solution.py:277
  66.8 2.9 %all-to-all-done.2 = f32[32,4,128]{2,1,0:T(4,128)S(1)} async-done(((f32[32,4,128]{2,1,0:T(4,128)}), f32[32,4,128]{2,1,0:T(4,128)S(1)}, u32[]{:S(2)}, u32[]{:S(2)}) %all-to-all-start.2) | async-done | bytes 65568 | tf_op jit(solution)/shard_map/all_to_all | solution.py:596
  69.7 1.2 %river_steps.1 = f32[64,128]{1,0:T(8,128)} custom-call(f32[64,128]{1,0:T(8,128)S(1)} %get-tuple-element.34.state, f32[128,128]{1,0:T(8,128)S(1)} %bitcast.13, f32[2,72,256]{2,1,0:T(8,128)S(1)} %static_halo.1._.fixed, f32[480,128]{1,0:T(8,128)} %get-tuple-element.16._), custom_call_target="tpu_custom_call" | custom-call | flops 10000000 | bytes 1048576 | tf_op jit(solution)/shard_map/river_steps/pallas_call | solution.py:585
  (4 shorter events, 0.0 us)
Async XLA Ops:
  0.6 11.1 %copy-start.9 = (s32[64,128]{1,0:T(8,128)S(1)}, s32[64,128]{1,0:T(8,128)}, u32[]{:S(2)}) copy-start(s32[64,128]{1,0:T(8,128)} %param.17) | copy-start | bytes 98308
  0.6 11.1 %copy-start.8 = (f32[64,128]{1,0:T(8,128)S(1)}, f32[64,128]{1,0:T(8,128)}, u32[]{:S(2)}) copy-start(f32[64,128]{1,0:T(8,128)} %param.16) | copy-start | bytes 98308
  0.7 17.0 %copy-start.4 = (s32[480]{0:T(512)S(1)}, s32[480]{0:T(512)}, u32[]{:S(2)}) copy-start(s32[480]{0:T(512)} %slots.1) | copy-start | bytes 5764
  0.7 17.1 %copy-start = (s32[480,128]{1,0:T(8,128)S(1)}, s32[480,128]{1,0:T(8,128)}, u32[]{:S(2)}) copy-start(s32[480,128]{1,0:T(8,128)} %cell.3) | copy-start | bytes 737284
  0.7 31.7 %copy-start.3 = (f32[480,128]{1,0:T(8,128)S(1)}, f32[480,128]{1,0:T(8,128)}, u32[]{:S(2)}) copy-start(f32[480,128]{1,0:T(8,128)} %cap.1) | copy-start | bytes 737284
  0.7 31.7 %copy-start.2 = (f32[480,128]{1,0:T(8,128)S(1)}, f32[480,128]{1,0:T(8,128)}, u32[]{:S(2)}) copy-start(f32[480,128]{1,0:T(8,128)} %water.1) | copy-start | bytes 737284
  0.7 31.7 %copy-start.1 = (f32[480,128]{1,0:T(8,128)S(1)}, f32[480,128]{1,0:T(8,128)}, u32[]{:S(2)}) copy-start(f32[480,128]{1,0:T(8,128)} %area.1) | copy-start | bytes 737284
  4.4 28.0 %all-to-all-start = ((f32[32,48,128]{2,1,0:T(8,128)}), f32[32,48,128]{2,1,0:T(8,128)S(1)}, u32[]{:S(2)}, u32[]{:S(2)}) async-start(f32[32,48,128]{2,1,0:T(8,128)} %bitcast), calls=%async_computation | async-start | bytes 1572864 | tf_op jit(solution)/shard_map/all_to_all | solution.py:596
  11.8 10.3 %collective-permute-start.1 = (f32[2,4,128]{2,1,0:T(4,128)S(1)}, f32[2,4,128]{2,1,0:T(4,128)S(1)}, u32[]{:S(2)}, u32[]{:S(2)}) collective-permute-start(f32[2,4,128]{2,1,0:T(4,128)S(1)} %get-tuple-element.35), channel_id=1, source_target_pairs={{8,0},{16,8},{24,16},{9,1},{17,9},{25,17},{10,2},{18,10},{26,18},{... | collective-permute-start | bytes 12296 | tf_op jit(solution)/shard_map/ppermute | solution.py:478
  13.1 12.1 %collective-permute-start = (f32[2,4,128]{2,1,0:T(4,128)S(1)}, f32[2,4,128]{2,1,0:T(4,128)S(1)}, u32[]{:S(2)}, u32[]{:S(2)}) collective-permute-start(f32[2,4,128]{2,1,0:T(4,128)S(1)} %get-tuple-element.36), channel_id=1, source_target_pairs={{0,8},{8,16},{16,24},{1,9},{9,17},{17,25},{2,10},{10,18},{18,26},{... | collective-permute-start | bytes 12296 | tf_op jit(solution)/shard_map/ppermute | solution.py:478
  32.4 9.9 %copy-start.6 = (s32[1,1024]{1,0:T(1,128)S(1)}, s32[1,1024]{1,0:T(1,128)}, u32[]{:S(2)}) copy-start(s32[1,1024]{1,0:T(1,128)} %slot.1) | copy-start | bytes 12292
  32.4 9.9 %copy-start.7 = (s32[1,1024]{1,0:T(1,128)S(1)}, s32[1,1024]{1,0:T(1,128)}, u32[]{:S(2)}) copy-start(s32[1,1024]{1,0:T(1,128)} %offset.1) | copy-start | bytes 12292
  38.7 19.2 %all-to-all-start.1 = ((f32[32,32,128]{2,1,0:T(8,128)}), f32[32,32,128]{2,1,0:T(8,128)S(1)}, u32[]{:S(2)}, u32[]{:S(2)}) async-start(f32[32,32,128]{2,1,0:T(8,128)} %bitcast.5), calls=%async_computation.1 | async-start | bytes 1048576 | tf_op jit(solution)/shard_map/all_to_all | solution.py:596
  43.1 8.5 %collective-permute-start.2 = (f32[8,128]{1,0:T(8,128)S(1)}, f32[8,128]{1,0:T(8,128)S(1)}, u32[]{:S(2)}, u32[]{:S(2)}) collective-permute-start(f32[8,128]{1,0:T(8,128)S(1)} %get-tuple-element.28), channel_id=1, source_target_pairs={{0,1},{1,2},{2,3},{3,4},{4,5},{5,6},{6,7},{8,9},{9,10},{10,11},{11... | collective-permute-start | bytes 12296 | tf_op jit(solution)/shard_map/ppermute | solution.py:643
  45.3 6.4 %collective-permute-start.3 = (f32[8,128]{1,0:T(8,128)S(1)}, f32[8,128]{1,0:T(8,128)S(1)}, u32[]{:S(2)}, u32[]{:S(2)}) collective-permute-start(f32[8,128]{1,0:T(8,128)S(1)} %get-tuple-element.29), channel_id=1, source_target_pairs={{1,0},{2,1},{3,2},{4,3},{5,4},{6,5},{7,6},{9,8},{10,9},{11,10},{12... | collective-permute-start | bytes 12296 | tf_op jit(solution)/shard_map/ppermute | solution.py:644
  46.6 11.3 %copy-start.5 = (f32[64,128]{1,0:T(8,128)S(1)}, f32[64,128]{1,0:T(8,128)}, u32[]{:S(2)}) copy-start(f32[64,128]{1,0:T(8,128)} %river.1) | copy-start | bytes 98308
  59.2 10.5 %all-to-all-start.2 = ((f32[32,4,128]{2,1,0:T(4,128)}), f32[32,4,128]{2,1,0:T(4,128)S(1)}, u32[]{:S(2)}, u32[]{:S(2)}) async-start(f32[32,4,128]{2,1,0:T(4,128)} %bitcast.7), calls=%async_computation.2 | async-start | bytes 131072 | tf_op jit(solution)/shard_map/all_to_all | solution.py:596

commit v3 on v2

--- a/solution.py
+++ b/solution.py
@@ -118,11 +118,12 @@
     copies[1].wait()
     places = slot_table(slot[...], offset[...], homes, capacity, True)
     copies[2].wait()
+    limit = pltpu.roll(forcing[2], WINDOW, 1)
+    above = jnp.concatenate([limit[lane_rows - 1 :], limit[: lane_rows - 1]], axis=0)
+    limit = jnp.where(iota(limit.shape, 1) < WINDOW, above, limit)
     parts = []
-    for var in range(3):
-        here = forcing[var]
-        following = jnp.concatenate([here[1:], here[:1]], axis=0)
-        parts += [here, following]
+    for own in (forcing[0], forcing[1], limit):
+        parts += [own, jnp.concatenate([own[1:], own[:1]], axis=0)]
     table = jnp.concatenate(thirds(jnp.concatenate(parts, axis=1)), axis=0)
     chunk = 128
     here = iota((chunk, LANES), 1)
@@ -144,9 +145,8 @@
         ]
         first = (here + lane) & 127
         second = (first + WINDOW) & 127
-        losses = jnp.where(
-            here < WINDOW, lane_pick(joined[1], first), lane_pick(joined[2], second)
-        )
+        demanded = ((here - lane) & 127) < WINDOW
+        losses = lane_pick(jnp.where(demanded, joined[1], joined[2]), first)
         base = start - slots // 2 if odd else start
         if odd:
             rains = jnp.where(
@@ -307,16 +307,46 @@
     )(cell, worker)
 
 
+def stage_kernel(soil_in, porosity_in, drainage_in, _, soil, porosity, drainage, ready):
+    part = pl.ds(0, soil.shape[1])
+    pairs = ((soil_in, soil), (porosity_in, porosity), (drainage_in, drainage))
+    copies = [
+        pltpu.make_async_copy(source.at[:, part, :], target, ready.at[i])
+        for i, (source, target) in enumerate(pairs)
+    ]
+    for copy in copies:
+        copy.start()
+    for copy in copies:
+        copy.wait()
+
+
+def stage(rows, soil, porosity, drainage, after):
+    far = pl.BlockSpec(memory_space=pltpu.HBM)
+    shape = (soil.shape[0], rows, LANES)
+    return pl.pallas_call(
+        stage_kernel,
+        in_specs=[far] * 3 + [pl.BlockSpec(memory_space=pl.ANY)],
+        out_specs=[pl.BlockSpec(memory_space=pltpu.VMEM)] * 3,
+        out_shape=[pltpu.VMEM(shape, jnp.float32)] * 3,
+        scratch_shapes=[pltpu.SemaphoreType.DMA((3,))],
+        compiler_params=pltpu.CompilerParams(vmem_limit_bytes=4 * MIB),
+        cost_estimate=pl.CostEstimate(flops=0, bytes_accessed=4 * MIB, transcendentals=0),
+        name="stage_soil",
+    )(in_hbm(soil), in_hbm(porosity), in_hbm(drainage), after)
+
+
 def land_sums_kernel(
-    pairs, slots, first_rows, arrived, cell, meta, area, water, cap, soil_in, porosity_in,
-    drainage_in, _, __, through, lost, canopy_new, sums_out, soil, porosity, drainage, fetched,
-    runoffs, evaps, ready,
+    pairs, slots, first_rows, arrived, cell, meta, area, water, cap, soil_first, porosity_first,
+    drainage_first, soil_in, porosity_in, drainage_in, _, __, through, lost, canopy_new,
+    sums_out, soil_rest, porosity_rest, drainage_rest, fetched, runoffs, evaps, ready,
 ):
-    layers, rows = soil.shape[:2]
-    steps = ready.shape[0]
-    block = rows // steps
+    layers, block = soil_first.shape[:2]
+    rows = cell.shape[0]
+    steps = rows // block
     chunk = block // 2
-    arrays = ((soil_in, soil), (porosity_in, porosity), (drainage_in, drainage))
+    staged = (soil_first, porosity_first, drainage_first)
+    rest = (soil_rest, porosity_rest, drainage_rest)
+    sources = (soil_in, porosity_in, drainage_in)
 
     def part_of(step):
         return pl.ds(step * block, block)
@@ -324,9 +354,11 @@
     def reads(step):
         return [
             pltpu.make_async_copy(
-                source.at[:, part_of(step), :], target.at[:, part_of(step), :], ready.at[step, i]
+                source.at[:, part_of(step), :],
+                target.at[:, part_of(step - 1), :],
+                ready.at[step - 1, i],
             )
-            for i, (source, target) in enumerate(arrays)
+            for i, (source, target) in enumerate(zip(sources, rest))
         ]
 
     def fetch(step):
@@ -350,12 +382,14 @@
         canopy_new[part, :] = retained - canopy_loss
         through[part, :] = flowing
         surface = jnp.zeros_like(flowing)
+        soil, porosity, drainage = staged if start < block else rest
+        local = pl.ds(start if start < block else start - block, chunk)
         for layer in range(layers):
-            filled = soil[layer, part, :] + flowing
-            excess = jnp.maximum(filled - porosity[layer, part, :], 0.0)
+            filled = soil[layer, local, :] + flowing
+            excess = jnp.maximum(filled - porosity[layer, local, :], 0.0)
             surface = surface + excess
             filled = filled - excess
-            flowing = drainage[layer, part, :] * filled
+            flowing = drainage[layer, local, :] * filled
             if layer == 0:
                 half = 0.5 * (filled - flowing)
                 soil_loss = jnp.minimum(jnp.minimum(limit, demand - canopy_loss), half)
@@ -382,7 +416,7 @@
         for i in range(step * block, (step + 1) * block):
             sums_out[pl.ds(slots[i], 1), :] = runoffs[pl.ds(i, 1), :]
 
-    for step in range(steps):
+    for step in range(1, steps):
         for copy in reads(step):
             copy.start()
     sums_out[...] = jnp.zeros_like(sums_out)
@@ -390,7 +424,7 @@
         fetch(step)
     for step in range(steps + 2):
         if step < steps:
-            for copy in reads(step):
+            for copy in reads(step) if step else ():
                 copy.wait()
             for start in range(step * block, (step + 1) * block, chunk):
                 cascade(start)
@@ -401,22 +435,23 @@
 
 
 def land_sums(
-    sums_shape, pairs, slots, first_rows, arrived, cell, meta, area, water, cap, soil, porosity,
-    drainage, after,
+    sums_shape, pairs, slots, first_rows, arrived, cell, meta, area, water, cap, staged, soil,
+    porosity, drainage, after,
 ):
     layers, rows = soil.shape[:2]
-    steps = 5
+    block = staged[0].shape[1]
+    steps = rows // block
     near = pl.BlockSpec(memory_space=pltpu.VMEM)
     far = pl.BlockSpec(memory_space=pltpu.HBM)
     return pl.pallas_call(
         functools.partial(land_sums_kernel, pairs),
-        in_specs=[pl.BlockSpec(memory_space=pltpu.SMEM)] * 2 + [near] * 6 + [far] * 3
+        in_specs=[pl.BlockSpec(memory_space=pltpu.SMEM)] * 2 + [near] * 9 + [far] * 3
         + [pl.BlockSpec(memory_space=pl.ANY)] * 2,
         out_specs=[near] * 4,
-        scratch_shapes=[pltpu.VMEM(soil.shape, jnp.float32)] * 3
+        scratch_shapes=[pltpu.VMEM((layers, rows - block, LANES), jnp.float32)] * 3
         + [pltpu.VMEM((2 * rows, LANES), jnp.float32)]
         + [pltpu.VMEM((rows, LANES), jnp.float32)] * 2
-        + [pltpu.SemaphoreType.DMA((steps, 3))],
+        + [pltpu.SemaphoreType.DMA((steps - 1, 3))],
         out_shape=[jax.ShapeDtypeStruct((rows, LANES), jnp.float32)] * 3
         + [jax.ShapeDtypeStruct(sums_shape, jnp.float32)],
         compiler_params=pltpu.CompilerParams(vmem_limit_bytes=VMEM_LIMIT),
@@ -424,6 +459,7 @@
         name="land_sums",
     )(
         slots, first_rows, arrived, cell, meta, area, water, cap,
+        *(pltpu.with_memory_space_constraint(value, pltpu.VMEM) for value in staged),
         in_hbm(soil), in_hbm(porosity), in_hbm(drainage), *after,
     )
 
@@ -627,9 +663,11 @@
     meta = segment_plan(patch_cell, worker_list[:, None])
     fixed = jnp.stack([river_rate, flow_code.astype(jnp.float32)])
     above, below = halo_parts(fixed, "region", 1, ITERS)
+    staged = stage(96, soil_water, porosity, drainage, meta)
     through, lost, canopy, sums = land_sums(
         (homes * capacity, LANES), pairs, worker_list, first_rows, arrived, patch_cell, meta,
-        patch_area, canopy_water, canopy_cap, soil_water, porosity, drainage, (above, below),
+        patch_area, canopy_water, canopy_cap, staged, soil_water, porosity, drainage,
+        (above, below),
     )
     returned = exchange(sums)
     layers_of = (through, lost, canopy, soil_water, porosity, drainage)

time: 71.4 us -> 74.9 us (1.049)
  local copies, waits for them, and re-layouts: 0.18 us -> 4.98 us
  waiting for transfers between devices: 21.7 us -> 19.2 us
  Pallas kernels: 24.8 us -> 25.7 us
    unnamed x20 -> x26, local copies, waits for them, and re-layouts: 0.05 us -> 4.85 us
    ppermute x2, waiting for transfers between devices: 5.45 us -> 2.99 us  [halo_parts(): return (lax.ppermute(last, axis, up), lax.ppermute(initial, axis, down))]
    pallas_call x0 -> x1, Pallas kernels: none -> 1.59 us  [stage(): pl.pallas_call(stage_kernel, in_specs=[far] * 3 + [pl.BlockSpec(memory_sp...]
  transfers between devices with their start and end apart: 7 -> 7, of which waited for: 5 -> 4; matrix products, arithmetic and copies ran while one was open for 0% -> 0% of each run, Pallas kernels for 17% -> 19%
where the time goes in v3:
time: 74.9 us; the launch traced here: 74.2 us
  Pallas kernels  25.7 us (34%)
  starting transfers between devices  23.3 us (31%)
  waiting for transfers between devices  19.2 us (26%)
  local copies, waits for them, and re-layouts  4.98 us (7%)
  between operations  0.9 us (1%)
    all_to_all x3, waiting for transfers between devices, exchange(): return lax.all_to_all(value, axes, split_axis=0, concat_axis=0, tiled=True)  16.2 us
    all_to_all x3, starting transfers between devices, exchange(): return lax.all_to_all(value, axes, split_axis=0, concat_axis=0, tiled=True)  14 us
    pallas_call x2, Pallas kernels, new_soil(): pl.pallas_call(new_soil_kernel, grid=(last - first,), in_specs=[flat, fla...  8.36 us
    ppermute x2, starting transfers between devices, halo_parts(): return (lax.ppermute(last, axis, up), lax.ppermute(initial, axis, down))  5.84 us
    pallas_call x1, Pallas kernels, land_sums(): pl.pallas_call(functools.partial(land_sums_kernel, pairs), in_specs=[pl.B...  5.72 us
    unnamed x26, local copies, waits for them, and re-layouts  4.85 us
    pallas_call x1, Pallas kernels, pack(): pl.pallas_call(functools.partial(pack_kernel, homes, capacity), in_specs=...  3.59 us
    ppermute x2, waiting for transfers between devices, halo_parts(): return (lax.ppermute(last, axis, up), lax.ppermute(initial, axis, down))  2.99 us
  transfers between devices with their start and end apart: 7, of which 4 were waited for; matrix products, arithmetic and copies ran while one was open for 0% of the time, Pallas kernels for 19%

profile of v3, /device:TPU:0, one launch (start us, length us, event | category | flops | bytes accessed | tf_op | source)
XLA Modules:
  0.0 74.2 jit_solution(14244836822532123335)
XLA Ops:
  0.6 0.0 copy-start.12
  0.6 0.0 copy-start.10
  0.7 0.0 copy-start.6
  0.7 0.0 copy-start
  0.7 3.6 %pack_forcing.1 = f32[1536,128]{1,0:T(8,128)} custom-call(s32[1,1024]{1,0:T(1,128)} %slot.1, s32[1,1024]{1,0:T(1,128)} %offset.1, f32[3,64,128]{2,1,0:T(8,128)} %forcing_in.1), custom_call_target="tpu_custom_call" | custom-call | flops 1000000000 | bytes 2097152 | tf_op jit(solution)/shard_map/pack_forcing/pallas_call | solution.py:168
  4.3 7.3 %all-to-all-start = ((f32[32,48,128]{2,1,0:T(8,128)}), f32[32,48,128]{2,1,0:T(8,128)S(1)}, u32[]{:S(2)}, u32[]{:S(2)}) async-start(f32[32,48,128]{2,1,0:T(8,128)} %bitcast), calls=%async_computation | async-start | bytes 1572864 | tf_op jit(solution)/shard_map/all_to_all | solution.py:632
  11.6 0.0 copy-done.12
  11.6 0.0 copy-done.10
  11.6 1.3 %collective-permute-start.1 = (f32[2,4,128]{2,1,0:T(4,128)S(1)}, f32[2,4,128]{2,1,0:T(4,128)S(1)}, u32[]{:S(2)}, u32[]{:S(2)}) collective-permute-start(f32[2,4,128]{2,1,0:T(4,128)S(1)} %get-tuple-element.41), channel_id=1, source_target_pairs={{8,0},{16,8},{24,16},{9,1},{17,9},{25,17},{10,2},{18,10},{26,18},{... | collective-permute-start | bytes 12296 | tf_op jit(solution)/shard_map/ppermute | solution.py:514
  12.9 4.5 %collective-permute-start = (f32[2,4,128]{2,1,0:T(4,128)S(1)}, f32[2,4,128]{2,1,0:T(4,128)S(1)}, u32[]{:S(2)}, u32[]{:S(2)}) collective-permute-start(f32[2,4,128]{2,1,0:T(4,128)S(1)} %get-tuple-element.42), channel_id=1, source_target_pairs={{0,8},{8,16},{16,24},{1,9},{9,17},{17,25},{2,10},{10,18},{18,26},{... | collective-permute-start | bytes 12296 | tf_op jit(solution)/shard_map/ppermute | solution.py:514
  17.5 0.0 copy-done.6
  17.5 0.1 copy.21.worker
  17.7 0.0 copy-done
  17.7 1.9 %segment_plan.1._.meta = s32[480,128]{1,0:T(8,128)S(1)} custom-call(s32[480,128]{1,0:T(8,128)S(1)} %copy-done, s32[480,1]{1,0:T(8,128)S(1)} %copy.21.worker), custom_call_target="tpu_custom_call" | custom-call | flops 100000000 | bytes 1048576 | tf_op jit(solution)/shard_map/segment_plan/pallas_call | solution.py:301
  19.6 1.6 %stage_soil.1 = (f32[15,96,128]{2,1,0:T(8,128)S(1)}, f32[15,96,128]{2,1,0:T(8,128)S(1)}, f32[15,96,128]{2,1,0:T(8,128)S(1)}) custom-call(f32[15,480,128]{2,1,0:T(8,128)} %soil.3, f32[15,480,128]{2,1,0:T(8,128)} %porosity.3, f32[15,480,128]{2,1,0:T(8,128)} %drainage.3, s32[480,128]{1,0:T(8,128)S(1)} %segment_plan.1._.meta), custom_call_target="tpu_custom_call" | custom-call | bytes 4194304 | tf_op jit(solution)/shard_map/stage_soil/pallas_call | solution.py:326
  21.2 0.0 copy-start.1
  21.2 0.9 %copy-done.1 = f32[15,96,128]{2,1,0:T(8,128)} copy-done((f32[15,96,128]{2,1,0:T(8,128)}, f32[15,96,128]{2,1,0:T(8,128)S(1)}, u32[]{:S(2)}) %copy-start.1) | copy-done | bytes 737304
  22.1 0.0 collective-permute-done.1.__
  22.1 3.0 %collective-permute-done._ = f32[2,4,128]{2,1,0:T(4,128)S(1)} collective-permute-done((f32[2,4,128]{2,1,0:T(4,128)S(1)}, f32[2,4,128]{2,1,0:T(4,128)S(1)}, u32[]{:S(2)}, u32[]{:S(2)}) %collective-permute-start) | collective-permute-done | bytes 4128 | tf_op jit(solution)/shard_map/ppermute | solution.py:514
  25.1 7.2 %all-to-all-done = f32[32,48,128]{2,1,0:T(8,128)S(1)} async-done(((f32[32,48,128]{2,1,0:T(8,128)}), f32[32,48,128]{2,1,0:T(8,128)S(1)}, u32[]{:S(2)}, u32[]{:S(2)}) %all-to-all-start) | async-done | bytes 786464 | tf_op jit(solution)/shard_map/all_to_all | solution.py:632
  32.3 0.0 copy-start.2
  32.3 1.1 %copy-done.2 = f32[15,96,128]{2,1,0:T(8,128)S(1)} copy-done((f32[15,96,128]{2,1,0:T(8,128)S(1)}, f32[15,96,128]{2,1,0:T(8,128)}, u32[]{:S(2)}) %copy-start.2) | copy-done | bytes 737304
  33.4 0.0 copy-start.3
  33.4 0.9 %copy-done.3 = f32[480,128]{1,0:T(8,128)S(1)} copy-done((f32[480,128]{1,0:T(8,128)S(1)}, f32[480,128]{1,0:T(8,128)}, u32[]{:S(2)}) %copy-start.3) | copy-done | bytes 245784
  34.3 0.0 copy-start.4
  34.3 0.9 %copy-done.4 = f32[480,128]{1,0:T(8,128)S(1)} copy-done((f32[480,128]{1,0:T(8,128)S(1)}, f32[480,128]{1,0:T(8,128)}, u32[]{:S(2)}) %copy-start.4) | copy-done | bytes 245784
  35.3 0.0 copy-start.5
  35.3 0.9 %copy-done.5 = f32[480,128]{1,0:T(8,128)S(1)} copy-done((f32[480,128]{1,0:T(8,128)S(1)}, f32[480,128]{1,0:T(8,128)}, u32[]{:S(2)}) %copy-start.5) | copy-done | bytes 245784
  36.2 0.0 copy-start.8
  36.2 0.0 copy-start.9
  36.2 5.7 %land_sums.1 = (f32[480,128]{1,0:T(8,128)S(1)}, f32[480,128]{1,0:T(8,128)S(1)}, f32[480,128]{1,0:T(8,128)S(1)}, f32[1024,128]{1,0:T(8,128)}) custom-call(s32[480]{0:T(512)S(1)} %copy-done.6, s32[480]{0:T(512)S(1)} %fusion.2.first_rows, f32[1536,128]{1,0:T(8,128)S(1)} %bitcast.10, s32[480,128]{1,0:T(8,128)S(1)} %copy-done, ...), custom_call_target="tpu_custom_call" | custom-call | flops 100000000 | bytes 20971520 | tf_op jit(solution)/shard_map/land_sums/pallas_call | solution.py:446
  41.9 0.0 copy-start.11
  41.9 3.6 %all-to-all-start.1 = ((f32[32,32,128]{2,1,0:T(8,128)}), f32[32,32,128]{2,1,0:T(8,128)S(1)}, u32[]{:S(2)}, u32[]{:S(2)}) async-start(f32[32,32,128]{2,1,0:T(8,128)} %bitcast.5), calls=%async_computation.1 | async-start | bytes 1048576 | tf_op jit(solution)/shard_map/all_to_all | solution.py:632
  45.6 0.0 copy-done.8
  45.6 0.0 copy-done.9
  45.6 0.7 unpack_plan.1
  46.3 0.0 copy-done.11
  46.3 0.1 edge_columns.1
  46.4 2.2 %collective-permute-start.2 = (f32[8,128]{1,0:T(8,128)S(1)}, f32[8,128]{1,0:T(8,128)S(1)}, u32[]{:S(2)}, u32[]{:S(2)}) collective-permute-start(f32[8,128]{1,0:T(8,128)S(1)} %get-tuple-element.34), channel_id=1, source_target_pairs={{0,1},{1,2},{2,3},{3,4},{4,5},{5,6},{6,7},{8,9},{9,10},{10,11},{11... | collective-permute-start | bytes 12296 | tf_op jit(solution)/shard_map/ppermute | solution.py:681
  48.5 1.3 %collective-permute-start.3 = (f32[8,128]{1,0:T(8,128)S(1)}, f32[8,128]{1,0:T(8,128)S(1)}, u32[]{:S(2)}, u32[]{:S(2)}) collective-permute-start(f32[8,128]{1,0:T(8,128)S(1)} %get-tuple-element.35), channel_id=1, source_target_pairs={{1,0},{2,1},{3,2},{4,3},{5,4},{6,5},{7,6},{9,8},{10,9},{11,10},{12... | collective-permute-start | bytes 12296 | tf_op jit(solution)/shard_map/ppermute | solution.py:682
  49.8 0.0 copy-start.7
  49.9 5.1 %new_soil.2 = (f32[15,480,128]{2,1,0:T(8,128)}, f32[480,128]{1,0:T(8,128)}) custom-call(f32[480,128]{1,0:T(8,128)S(1)} %get-tuple-element.26.through, f32[480,128]{1,0:T(8,128)S(1)} %get-tuple-element.27.lost, f32[480,128]{1,0:T(8,128)S(1)} %get-tuple-element.28.canopy, f32[15,480,128]{2,1,0:T(8,128)} %soil.3, f32[15,480,128]{2,1,0:T(8,128)} %porosity.3, ...), custom_call_target="tpu_custom_call" | custom-call | flops 100000000 | bytes 9437184 | tf_op jit(solution)/shard_map/new_soil/pallas_call | solution.py:490
  54.9 0.0 collective-permute-done.2.before
  54.9 0.0 collective-permute-done.3.after
  54.9 0.1 static_halo.1._.fixed
  55.0 6.1 %all-to-all-done.1 = f32[32,32,128]{2,1,0:T(8,128)S(1)} async-done(((f32[32,32,128]{2,1,0:T(8,128)}), f32[32,32,128]{2,1,0:T(8,128)S(1)}, u32[]{:S(2)}, u32[]{:S(2)}) %all-to-all-start.1) | async-done | bytes 524320 | tf_op jit(solution)/shard_map/all_to_all | solution.py:632
  61.1 0.0 copy-done.7
  61.1 1.3 %unpack_runoff.1 = (f32[64,128]{1,0:T(8,128)}, f32[64,128]{1,0:T(8,128)S(1)}, f32[128,128]{1,0:T(8,128)}) custom-call(f32[1024,128]{1,0:T(8,128)S(1)} %bitcast.11, s32[1024,128]{1,0:T(8,128)S(1)} %get-tuple-element.32.code, bf16[64,1024]{1,0:T(8,128)(2,1)S(1)} %get-tuple-element.33.place, f32[64,128]{1,0:T(8,128)S(1)} %copy-done.7, ...), custom_call_target="tpu_custom_call" | custom-call | flops 1000000000 | bytes 1048576 | tf_op jit(solution)/shard_map/unpack_runoff/pallas_call | solution.py:261
  62.5 3.1 %all-to-all-start.2 = ((f32[32,4,128]{2,1,0:T(4,128)}), f32[32,4,128]{2,1,0:T(4,128)S(1)}, u32[]{:S(2)}, u32[]{:S(2)}) async-start(f32[32,4,128]{2,1,0:T(4,128)} %bitcast.7), calls=%async_computation.2 | async-start | bytes 131072 | tf_op jit(solution)/shard_map/all_to_all | solution.py:632
  65.6 3.3 %new_soil.3 = (f32[15,480,128]{2,1,0:T(8,128)}, f32[480,128]{1,0:T(8,128)}) custom-call(f32[480,128]{1,0:T(8,128)S(1)} %get-tuple-element.26.through, f32[480,128]{1,0:T(8,128)S(1)} %get-tuple-element.27.lost, f32[480,128]{1,0:T(8,128)S(1)} %get-tuple-element.28.canopy, f32[15,480,128]{2,1,0:T(8,128)} %soil.3, ...), custom_call_target="tpu_custom_call", output_to_operand_aliasing={{0}: (6, {}), {1}: (7, {})} | custom-call | flops 100000000 | bytes 6291456 | tf_op jit(solution)/shard_map/new_soil/pallas_call | solution.py:490
  68.9 1.2 %unpack_evap.1 = f32[64,128]{1,0:T(8,128)} custom-call(f32[1024,128]{1,0:T(8,128)S(1)} %bitcast.12, s32[1024,128]{1,0:T(8,128)S(1)} %get-tuple-element.32.code, bf16[64,1024]{1,0:T(8,128)(2,1)S(1)} %get-tuple-element.33.place), custom_call_target="tpu_custom_call" | custom-call | flops 1000000000 | bytes 1048576 | tf_op jit(solution)/shard_map/unpack_evap/pallas_call | solution.py:277
  70.1 2.9 %all-to-all-done.2 = f32[32,4,128]{2,1,0:T(4,128)S(1)} async-done(((f32[32,4,128]{2,1,0:T(4,128)}), f32[32,4,128]{2,1,0:T(4,128)S(1)}, u32[]{:S(2)}, u32[]{:S(2)}) %all-to-all-start.2) | async-done | bytes 65568 | tf_op jit(solution)/shard_map/all_to_all | solution.py:632
  73.0 1.2 %river_steps.1 = f32[64,128]{1,0:T(8,128)} custom-call(f32[64,128]{1,0:T(8,128)S(1)} %get-tuple-element.40.state, f32[128,128]{1,0:T(8,128)S(1)} %bitcast.13, f32[2,72,256]{2,1,0:T(8,128)S(1)} %static_halo.1._.fixed, f32[480,128]{1,0:T(8,128)} %get-tuple-element.19._), custom_call_target="tpu_custom_call" | custom-call | flops 10000000 | bytes 1048576 | tf_op jit(solution)/shard_map/river_steps/pallas_call | solution.py:621
  (4 shorter events, 0.0 us)
Async XLA Ops:
  0.6 11.0 %copy-start.12 = (s32[64,128]{1,0:T(8,128)S(1)}, s32[64,128]{1,0:T(8,128)}, u32[]{:S(2)}) copy-start(s32[64,128]{1,0:T(8,128)} %param.17) | copy-start | bytes 98308
  0.6 11.0 %copy-start.10 = (f32[64,128]{1,0:T(8,128)S(1)}, f32[64,128]{1,0:T(8,128)}, u32[]{:S(2)}) copy-start(f32[64,128]{1,0:T(8,128)} %param.16) | copy-start | bytes 98308
  0.7 16.8 %copy-start.6 = (s32[480]{0:T(512)S(1)}, s32[480]{0:T(512)}, u32[]{:S(2)}) copy-start(s32[480]{0:T(512)} %slots.1) | copy-start | bytes 5764
  0.7 17.0 %copy-start = (s32[480,128]{1,0:T(8,128)S(1)}, s32[480,128]{1,0:T(8,128)}, u32[]{:S(2)}) copy-start(s32[480,128]{1,0:T(8,128)} %cell.3) | copy-start | bytes 737284
  4.3 28.0 %all-to-all-start = ((f32[32,48,128]{2,1,0:T(8,128)}), f32[32,48,128]{2,1,0:T(8,128)S(1)}, u32[]{:S(2)}, u32[]{:S(2)}) async-start(f32[32,48,128]{2,1,0:T(8,128)} %bitcast), calls=%async_computation | async-start | bytes 1572864 | tf_op jit(solution)/shard_map/all_to_all | solution.py:632
  11.6 10.4 %collective-permute-start.1 = (f32[2,4,128]{2,1,0:T(4,128)S(1)}, f32[2,4,128]{2,1,0:T(4,128)S(1)}, u32[]{:S(2)}, u32[]{:S(2)}) collective-permute-start(f32[2,4,128]{2,1,0:T(4,128)S(1)} %get-tuple-element.41), channel_id=1, source_target_pairs={{8,0},{16,8},{24,16},{9,1},{17,9},{25,17},{10,2},{18,10},{26,18},{... | collective-permute-start | bytes 12296 | tf_op jit(solution)/shard_map/ppermute | solution.py:514
  12.9 12.1 %collective-permute-start = (f32[2,4,128]{2,1,0:T(4,128)S(1)}, f32[2,4,128]{2,1,0:T(4,128)S(1)}, u32[]{:S(2)}, u32[]{:S(2)}) collective-permute-start(f32[2,4,128]{2,1,0:T(4,128)S(1)} %get-tuple-element.42), channel_id=1, source_target_pairs={{0,8},{8,16},{16,24},{1,9},{9,17},{17,25},{2,10},{10,18},{18,26},{... | collective-permute-start | bytes 12296 | tf_op jit(solution)/shard_map/ppermute | solution.py:514
  21.2 0.9 %copy-start.1 = (f32[15,96,128]{2,1,0:T(8,128)}, f32[15,96,128]{2,1,0:T(8,128)S(1)}, u32[]{:S(2)}) copy-start(f32[15,96,128]{2,1,0:T(8,128)S(1)} %get-tuple-element.25.drainage_first) | copy-start | bytes 2211844
  32.3 1.1 %copy-start.2 = (f32[15,96,128]{2,1,0:T(8,128)S(1)}, f32[15,96,128]{2,1,0:T(8,128)}, u32[]{:S(2)}) copy-start(f32[15,96,128]{2,1,0:T(8,128)} %copy-done.1) | copy-start | bytes 2211844
  33.4 0.9 %copy-start.3 = (f32[480,128]{1,0:T(8,128)S(1)}, f32[480,128]{1,0:T(8,128)}, u32[]{:S(2)}) copy-start(f32[480,128]{1,0:T(8,128)} %area.1) | copy-start | bytes 737284
  34.3 0.9 %copy-start.4 = (f32[480,128]{1,0:T(8,128)S(1)}, f32[480,128]{1,0:T(8,128)}, u32[]{:S(2)}) copy-start(f32[480,128]{1,0:T(8,128)} %water.1) | copy-start | bytes 737284
  35.3 0.9 %copy-start.5 = (f32[480,128]{1,0:T(8,128)S(1)}, f32[480,128]{1,0:T(8,128)}, u32[]{:S(2)}) copy-start(f32[480,128]{1,0:T(8,128)} %cap.1) | copy-start | bytes 737284
  36.2 9.4 %copy-start.8 = (s32[1,1024]{1,0:T(1,128)S(1)}, s32[1,1024]{1,0:T(1,128)}, u32[]{:S(2)}) copy-start(s32[1,1024]{1,0:T(1,128)} %slot.1) | copy-start | bytes 12292
  36.2 9.4 %copy-start.9 = (s32[1,1024]{1,0:T(1,128)S(1)}, s32[1,1024]{1,0:T(1,128)}, u32[]{:S(2)}) copy-start(s32[1,1024]{1,0:T(1,128)} %offset.1) | copy-start | bytes 12292
  41.9 4.3 %copy-start.11 = (f32[64,128]{1,0:T(8,128)S(1)}, f32[64,128]{1,0:T(8,128)}, u32[]{:S(2)}) copy-start(f32[64,128]{1,0:T(8,128)} %param.16) | copy-start | bytes 98308
  41.9 19.2 %all-to-all-start.1 = ((f32[32,32,128]{2,1,0:T(8,128)}), f32[32,32,128]{2,1,0:T(8,128)S(1)}, u32[]{:S(2)}, u32[]{:S(2)}) async-start(f32[32,32,128]{2,1,0:T(8,128)} %bitcast.5), calls=%async_computation.1 | async-start | bytes 1048576 | tf_op jit(solution)/shard_map/all_to_all | solution.py:632
  46.4 8.5 %collective-permute-start.2 = (f32[8,128]{1,0:T(8,128)S(1)}, f32[8,128]{1,0:T(8,128)S(1)}, u32[]{:S(2)}, u32[]{:S(2)}) collective-permute-start(f32[8,128]{1,0:T(8,128)S(1)} %get-tuple-element.34), channel_id=1, source_target_pairs={{0,1},{1,2},{2,3},{3,4},{4,5},{5,6},{6,7},{8,9},{9,10},{10,11},{11... | collective-permute-start | bytes 12296 | tf_op jit(solution)/shard_map/ppermute | solution.py:681
  48.5 6.4 %collective-permute-start.3 = (f32[8,128]{1,0:T(8,128)S(1)}, f32[8,128]{1,0:T(8,128)S(1)}, u32[]{:S(2)}, u32[]{:S(2)}) collective-permute-start(f32[8,128]{1,0:T(8,128)S(1)} %get-tuple-element.35), channel_id=1, source_target_pairs={{1,0},{2,1},{3,2},{4,3},{5,4},{6,5},{7,6},{9,8},{10,9},{11,10},{12... | collective-permute-start | bytes 12296 | tf_op jit(solution)/shard_map/ppermute | solution.py:682
  49.8 11.3 %copy-start.7 = (f32[64,128]{1,0:T(8,128)S(1)}, f32[64,128]{1,0:T(8,128)}, u32[]{:S(2)}) copy-start(f32[64,128]{1,0:T(8,128)} %river.1) | copy-start | bytes 98308
  62.5 10.5 %all-to-all-start.2 = ((f32[32,4,128]{2,1,0:T(4,128)}), f32[32,4,128]{2,1,0:T(4,128)S(1)}, u32[]{:S(2)}, u32[]{:S(2)}) async-start(f32[32,4,128]{2,1,0:T(4,128)} %bitcast.7), calls=%async_computation.2 | async-start | bytes 131072 | tf_op jit(solution)/shard_map/all_to_all | solution.py:632

commit v4 on v2

--- a/solution.py
+++ b/solution.py
@@ -118,11 +118,12 @@
     copies[1].wait()
     places = slot_table(slot[...], offset[...], homes, capacity, True)
     copies[2].wait()
+    limit = pltpu.roll(forcing[2], WINDOW, 1)
+    above = jnp.concatenate([limit[lane_rows - 1 :], limit[: lane_rows - 1]], axis=0)
+    limit = jnp.where(iota(limit.shape, 1) < WINDOW, above, limit)
     parts = []
-    for var in range(3):
-        here = forcing[var]
-        following = jnp.concatenate([here[1:], here[:1]], axis=0)
-        parts += [here, following]
+    for own in (forcing[0], forcing[1], limit):
+        parts += [own, jnp.concatenate([own[1:], own[:1]], axis=0)]
     table = jnp.concatenate(thirds(jnp.concatenate(parts, axis=1)), axis=0)
     chunk = 128
     here = iota((chunk, LANES), 1)
@@ -144,9 +145,8 @@
         ]
         first = (here + lane) & 127
         second = (first + WINDOW) & 127
-        losses = jnp.where(
-            here < WINDOW, lane_pick(joined[1], first), lane_pick(joined[2], second)
-        )
+        demanded = ((here - lane) & 127) < WINDOW
+        losses = lane_pick(jnp.where(demanded, joined[1], joined[2]), first)
         base = start - slots // 2 if odd else start
         if odd:
             rains = jnp.where(
@@ -307,16 +307,51 @@
     )(cell, worker)
 
 
+def layer_terms_kernel(soil, porosity, drainage, _, out):
+    layers, block = soil.shape[:2]
+    chunk = 48
+    for start in range(0, block, chunk):
+        part = pl.ds(start, chunk)
+        share = inverse = None
+        total = jnp.zeros((chunk, LANES), jnp.float32)
+        for layer in range(layers):
+            content, room = soil[layer, part, :], porosity[layer, part, :]
+            if layer:
+                content, room = content * inverse, room * inverse
+            total = total + content
+            out[0, layer, part, :] = room - total
+            rate = drainage[layer, part, :]
+            share = rate if layer == 0 else share * rate
+            inverse = 1.0 / share
+            out[0, layers + layer, part, :] = share
+        out[0, 2 * layers, part, :] = total
+        out[0, 2 * layers + 1, part, :] = soil[0, part, :]
+
+
+def layer_terms(soil, porosity, drainage, after):
+    layers, rows = soil.shape[:2]
+    block = 96
+    deep = pl.BlockSpec((layers, block, LANES), lambda i: (0, i, 0))
+    shape = (rows // block, 2 * layers + 2, block, LANES)
+    return pl.pallas_call(
+        layer_terms_kernel,
+        grid=(rows // block,),
+        in_specs=[deep] * 3 + [pl.BlockSpec(memory_space=pl.ANY)],
+        out_specs=pl.BlockSpec((1,) + shape[1:], lambda i: (i, 0, 0, 0)),
+        out_shape=pltpu.HBM(shape, jnp.float32),
+        compiler_params=pltpu.CompilerParams(vmem_limit_bytes=VMEM_LIMIT),
+        cost_estimate=pl.CostEstimate(flops=10**8, bytes_accessed=19 * MIB, transcendentals=0),
+        name="layer_terms",
+    )(in_hbm(soil), in_hbm(porosity), in_hbm(drainage), after)
+
+
 def land_sums_kernel(
-    pairs, slots, first_rows, arrived, cell, meta, area, water, cap, soil_in, porosity_in,
-    drainage_in, _, __, through, lost, canopy_new, sums_out, soil, porosity, drainage, fetched,
-    runoffs, evaps, ready,
+    pairs, slots, first_rows, arrived, cell, meta, area, water, cap, terms_in, _, __, through,
+    lost, canopy_new, sums_out, terms, fetched, runoffs, evaps, ready,
 ):
-    layers, rows = soil.shape[:2]
-    steps = ready.shape[0]
-    block = rows // steps
+    steps, count, block = terms.shape[:3]
+    layers = count // 2 - 1
     chunk = block // 2
-    arrays = ((soil_in, soil), (porosity_in, porosity), (drainage_in, drainage))
 
     def part_of(step):
         return pl.ds(step * block, block)
@@ -324,9 +359,9 @@
     def reads(step):
         return [
             pltpu.make_async_copy(
-                source.at[:, part_of(step), :], target.at[:, part_of(step), :], ready.at[step, i]
+                terms_in.at[step, part], terms.at[step, part], ready.at[step, i]
             )
-            for i, (source, target) in enumerate(arrays)
+            for i, part in enumerate((pl.ds(0, count // 2), pl.ds(count // 2, count // 2)))
         ]
 
     def fetch(step):
@@ -349,19 +384,25 @@
         canopy_loss = jnp.minimum(demand, retained)
         canopy_new[part, :] = retained - canopy_loss
         through[part, :] = flowing
-        surface = jnp.zeros_like(flowing)
+        step, local = start // block, pl.ds(start % block, chunk)
+        surface = None
         for layer in range(layers):
-            filled = soil[layer, part, :] + flowing
-            excess = jnp.maximum(filled - porosity[layer, part, :], 0.0)
-            surface = surface + excess
-            filled = filled - excess
-            flowing = drainage[layer, part, :] * filled
+            room = terms[step, layer, local, :]
+            excess = jnp.maximum(flowing - room, 0.0)
+            flowing = jnp.minimum(flowing, room)
             if layer == 0:
-                half = 0.5 * (filled - flowing)
+                surface = excess
+                content = flowing + terms[step, 2 * layers + 1, local, :]
+                half = 0.5 * (content - terms[step, layers, local, :] * content)
                 soil_loss = jnp.minimum(jnp.minimum(limit, demand - canopy_loss), half)
                 lost[part, :] = soil_loss
                 evaps[part, :] = area[part, :] * (canopy_loss + soil_loss)
-        runoffs[part, :] = area[part, :] * (surface + flowing)
+            else:
+                surface = surface + terms[step, layers + layer - 1, local, :] * excess
+        bottom = terms[step, 2 * layers - 1, local, :] * (
+            flowing + terms[step, 2 * layers, local, :]
+        )
+        runoffs[part, :] = area[part, :] * (surface + bottom)
 
     def scan(step):
         part = part_of(step)
@@ -401,22 +442,22 @@
 
 
 def land_sums(
-    sums_shape, pairs, slots, first_rows, arrived, cell, meta, area, water, cap, soil, porosity,
-    drainage, after,
+    sums_shape, pairs, slots, first_rows, arrived, cell, meta, area, water, cap, terms, after
 ):
-    layers, rows = soil.shape[:2]
-    steps = 5
+    rows = cell.shape[0]
     near = pl.BlockSpec(memory_space=pltpu.VMEM)
-    far = pl.BlockSpec(memory_space=pltpu.HBM)
     return pl.pallas_call(
         functools.partial(land_sums_kernel, pairs),
-        in_specs=[pl.BlockSpec(memory_space=pltpu.SMEM)] * 2 + [near] * 6 + [far] * 3
-        + [pl.BlockSpec(memory_space=pl.ANY)] * 2,
+        in_specs=[pl.BlockSpec(memory_space=pltpu.SMEM)] * 2 + [near] * 6
+        + [pl.BlockSpec(memory_space=pltpu.HBM)] + [pl.BlockSpec(memory_space=pl.ANY)] * 2,
         out_specs=[near] * 4,
-        scratch_shapes=[pltpu.VMEM(soil.shape, jnp.float32)] * 3
-        + [pltpu.VMEM((2 * rows, LANES), jnp.float32)]
-        + [pltpu.VMEM((rows, LANES), jnp.float32)] * 2
-        + [pltpu.SemaphoreType.DMA((steps, 3))],
+        scratch_shapes=[
+            pltpu.VMEM(terms.shape, jnp.float32),
+            pltpu.VMEM((2 * rows, LANES), jnp.float32),
+            pltpu.VMEM((rows, LANES), jnp.float32),
+            pltpu.VMEM((rows, LANES), jnp.float32),
+            pltpu.SemaphoreType.DMA((terms.shape[0], 2)),
+        ],
         out_shape=[jax.ShapeDtypeStruct((rows, LANES), jnp.float32)] * 3
         + [jax.ShapeDtypeStruct(sums_shape, jnp.float32)],
         compiler_params=pltpu.CompilerParams(vmem_limit_bytes=VMEM_LIMIT),
@@ -424,7 +465,7 @@
         name="land_sums",
     )(
         slots, first_rows, arrived, cell, meta, area, water, cap,
-        in_hbm(soil), in_hbm(porosity), in_hbm(drainage), *after,
+        in_hbm(terms), *after,
     )
 
 
@@ -627,9 +668,10 @@
     meta = segment_plan(patch_cell, worker_list[:, None])
     fixed = jnp.stack([river_rate, flow_code.astype(jnp.float32)])
     above, below = halo_parts(fixed, "region", 1, ITERS)
+    terms = layer_terms(soil_water, porosity, drainage, meta)
     through, lost, canopy, sums = land_sums(
         (homes * capacity, LANES), pairs, worker_list, first_rows, arrived, patch_cell, meta,
-        patch_area, canopy_water, canopy_cap, soil_water, porosity, drainage, (above, below),
+        patch_area, canopy_water, canopy_cap, terms, (above, below),
     )
     returned = exchange(sums)
     layers_of = (through, lost, canopy, soil_water, porosity, drainage)

time: 71.4 us -> 70.4 us (0.986)
  waiting for transfers between devices: 21.7 us -> 13.6 us
  Pallas kernels: 24.8 us -> 32.7 us
  starting transfers between devices: 23.3 us -> 22.4 us
    pallas_call x0 -> x1, Pallas kernels: none -> 8.9 us  [layer_terms(): pl.pallas_call(layer_terms_kernel, grid=(rows // block,), in_specs=[deep]...]
    ppermute x2, waiting for transfers between devices: 5.45 us -> 0.01 us  [halo_parts(): return (lax.ppermute(last, axis, up), lax.ppermute(initial, axis, down))]
    all_to_all x3, waiting for transfers between devices: 16.2 us -> 13.6 us  [exchange(): return lax.all_to_all(value, axes, split_axis=0, concat_axis=0, tiled=True)]
    pallas_call x1, Pallas kernels: 6.27 us -> 5.36 us  [land_sums(): pl.pallas_call(functools.partial(land_sums_kernel, pairs), in_specs=[pl.B...]
    ppermute x2, starting transfers between devices: 5.84 us -> 4.97 us  [halo_parts(): return (lax.ppermute(last, axis, up), lax.ppermute(initial, axis, down))]
  transfers between devices with their start and end apart: 7 -> 7, of which waited for: 5 -> 3; matrix products, arithmetic and copies ran while one was open for 0% -> 0% of each run, Pallas kernels for 17% -> 30%
where the time goes in v4:
time: 70.4 us; the launch traced here: 69.9 us
  Pallas kernels  32.7 us (46%)
  starting transfers between devices  22.4 us (32%)
  waiting for transfers between devices  13.6 us (19%)
  between operations  0.9 us (1%)
    all_to_all x3, starting transfers between devices, exchange(): return lax.all_to_all(value, axes, split_axis=0, concat_axis=0, tiled=True)  14 us
    all_to_all x3, waiting for transfers between devices, exchange(): return lax.all_to_all(value, axes, split_axis=0, concat_axis=0, tiled=True)  13.6 us
    pallas_call x1, Pallas kernels, layer_terms(): pl.pallas_call(layer_terms_kernel, grid=(rows // block,), in_specs=[deep]...  8.9 us
    pallas_call x2, Pallas kernels, new_soil(): pl.pallas_call(new_soil_kernel, grid=(last - first,), in_specs=[flat, fla...  8.36 us
    pallas_call x1, Pallas kernels, land_sums(): pl.pallas_call(functools.partial(land_sums_kernel, pairs), in_specs=[pl.B...  5.36 us
    ppermute x2, starting transfers between devices, halo_parts(): return (lax.ppermute(last, axis, up), lax.ppermute(initial, axis, down))  4.97 us
    pallas_call x1, Pallas kernels, pack(): pl.pallas_call(functools.partial(pack_kernel, homes, capacity), in_specs=...  3.59 us
    ppermute x1, starting transfers between devices, shards(): before = lax.ppermute(last, 'col', [(i, i + 1) for i in range(count - 1)])  2.18 us
  transfers between devices with their start and end apart: 7, of which 3 were waited for; matrix products, arithmetic and copies ran while one was open for 0% of the time, Pallas kernels for 30%

profile of v4, /device:TPU:0, one launch (start us, length us, event | category | flops | bytes accessed | tf_op | source)
XLA Modules:
  0.0 69.9 jit_solution(7294831798311208244)
XLA Ops:
  0.6 0.0 copy-start.9
  0.6 0.0 copy-start.8
  0.7 0.0 copy-start.4
  0.7 0.0 copy-start
  0.7 3.6 %pack_forcing.1 = f32[1536,128]{1,0:T(8,128)} custom-call(s32[1,1024]{1,0:T(1,128)} %slot.1, s32[1,1024]{1,0:T(1,128)} %offset.1, f32[3,64,128]{2,1,0:T(8,128)} %forcing_in.1), custom_call_target="tpu_custom_call" | custom-call | flops 1000000000 | bytes 2097152 | tf_op jit(solution)/shard_map/pack_forcing/pallas_call | solution.py:168
  4.3 7.3 %all-to-all-start = ((f32[32,48,128]{2,1,0:T(8,128)}), f32[32,48,128]{2,1,0:T(8,128)S(1)}, u32[]{:S(2)}, u32[]{:S(2)}) async-start(f32[32,48,128]{2,1,0:T(8,128)} %bitcast), calls=%async_computation | async-start | bytes 1572864 | tf_op jit(solution)/shard_map/all_to_all | solution.py:637
  11.6 0.0 copy-done.9
  11.6 0.0 copy-done.8
  11.6 3.7 %collective-permute-start = (f32[2,4,128]{2,1,0:T(4,128)S(1)}, f32[2,4,128]{2,1,0:T(4,128)S(1)}, u32[]{:S(2)}, u32[]{:S(2)}) collective-permute-start(f32[2,4,128]{2,1,0:T(4,128)S(1)} %get-tuple-element.36), channel_id=1, source_target_pairs={{0,8},{8,16},{16,24},{1,9},{9,17},{17,25},{2,10},{10,18},{18,26},{... | collective-permute-start | bytes 12296 | tf_op jit(solution)/shard_map/ppermute | solution.py:519
  15.3 1.3 %collective-permute-start.1 = (f32[2,4,128]{2,1,0:T(4,128)S(1)}, f32[2,4,128]{2,1,0:T(4,128)S(1)}, u32[]{:S(2)}, u32[]{:S(2)}) collective-permute-start(f32[2,4,128]{2,1,0:T(4,128)S(1)} %get-tuple-element.35), channel_id=1, source_target_pairs={{8,0},{16,8},{24,16},{9,1},{17,9},{25,17},{10,2},{18,10},{26,18},{... | collective-permute-start | bytes 12296 | tf_op jit(solution)/shard_map/ppermute | solution.py:519
  16.6 0.0 copy-done.4
  16.6 0.1 copy.21.worker
  16.8 0.0 copy-done
  16.8 1.9 %segment_plan.1._.meta = s32[480,128]{1,0:T(8,128)S(1)} custom-call(s32[480,128]{1,0:T(8,128)S(1)} %copy-done, s32[480,1]{1,0:T(8,128)S(1)} %copy.21.worker), custom_call_target="tpu_custom_call" | custom-call | flops 100000000 | bytes 1048576 | tf_op jit(solution)/shard_map/segment_plan/pallas_call | solution.py:301
  18.7 0.0 copy-start.1
  18.7 0.0 copy-start.2
  18.7 0.0 copy-start.3
  18.8 8.9 %layer_terms.1.terms_in = f32[5,32,96,128]{3,2,1,0:T(8,128)} custom-call(f32[15,480,128]{2,1,0:T(8,128)} %soil.5, f32[15,480,128]{2,1,0:T(8,128)} %porosity.5, f32[15,480,128]{2,1,0:T(8,128)} %drainage.5, s32[480,128]{1,0:T(8,128)S(1)} %segment_plan.1._.meta), custom_call_target="tpu_custom_call" | custom-call | flops 100000000 | bytes 19922944 | tf_op jit(solution)/shard_map/layer_terms/pallas_call | solution.py:336
  27.7 0.0 collective-permute-done._
  27.7 0.0 collective-permute-done.1.__
  27.7 4.6 %all-to-all-done = f32[32,48,128]{2,1,0:T(8,128)S(1)} async-done(((f32[32,48,128]{2,1,0:T(8,128)}), f32[32,48,128]{2,1,0:T(8,128)S(1)}, u32[]{:S(2)}, u32[]{:S(2)}) %all-to-all-start) | async-done | bytes 786464 | tf_op jit(solution)/shard_map/all_to_all | solution.py:637
  32.3 0.0 copy-done.1
  32.3 0.0 copy-done.2
  32.3 0.0 copy-done.3
  32.3 0.0 copy-start.6
  32.3 0.0 copy-start.7
  32.3 5.4 %land_sums.1 = (f32[480,128]{1,0:T(8,128)S(1)}, f32[480,128]{1,0:T(8,128)S(1)}, f32[480,128]{1,0:T(8,128)S(1)}, f32[1024,128]{1,0:T(8,128)}) custom-call(s32[480]{0:T(512)S(1)} %copy-done.4, s32[480]{0:T(512)S(1)} %fusion.2.first_rows, f32[1536,128]{1,0:T(8,128)S(1)} %bitcast.10, s32[480,128]{1,0:T(8,128)S(1)} %copy-done, ...), custom_call_target="tpu_custom_call" | custom-call | flops 100000000 | bytes 20971520 | tf_op jit(solution)/shard_map/land_sums/pallas_call | solution.py:449
  37.7 3.6 %all-to-all-start.1 = ((f32[32,32,128]{2,1,0:T(8,128)}), f32[32,32,128]{2,1,0:T(8,128)S(1)}, u32[]{:S(2)}, u32[]{:S(2)}) async-start(f32[32,32,128]{2,1,0:T(8,128)} %bitcast.5), calls=%async_computation.1 | async-start | bytes 1048576 | tf_op jit(solution)/shard_map/all_to_all | solution.py:637
  41.3 0.0 copy-done.6
  41.3 0.0 copy-done.7
  41.3 0.7 unpack_plan.1
  42.0 0.1 edge_columns.1
  42.1 2.2 %collective-permute-start.2 = (f32[8,128]{1,0:T(8,128)S(1)}, f32[8,128]{1,0:T(8,128)S(1)}, u32[]{:S(2)}, u32[]{:S(2)}) collective-permute-start(f32[8,128]{1,0:T(8,128)S(1)} %get-tuple-element.28), channel_id=1, source_target_pairs={{0,1},{1,2},{2,3},{3,4},{4,5},{5,6},{6,7},{8,9},{9,10},{10,11},{11... | collective-permute-start | bytes 12296 | tf_op jit(solution)/shard_map/ppermute | solution.py:685
  44.3 1.3 %collective-permute-start.3 = (f32[8,128]{1,0:T(8,128)S(1)}, f32[8,128]{1,0:T(8,128)S(1)}, u32[]{:S(2)}, u32[]{:S(2)}) collective-permute-start(f32[8,128]{1,0:T(8,128)S(1)} %get-tuple-element.29), channel_id=1, source_target_pairs={{1,0},{2,1},{3,2},{4,3},{5,4},{6,5},{7,6},{9,8},{10,9},{11,10},{12... | collective-permute-start | bytes 12296 | tf_op jit(solution)/shard_map/ppermute | solution.py:686
  45.6 0.0 copy-start.5
  45.6 5.1 %new_soil.2 = (f32[15,480,128]{2,1,0:T(8,128)}, f32[480,128]{1,0:T(8,128)}) custom-call(f32[480,128]{1,0:T(8,128)S(1)} %get-tuple-element.20.through, f32[480,128]{1,0:T(8,128)S(1)} %get-tuple-element.21.lost, f32[480,128]{1,0:T(8,128)S(1)} %get-tuple-element.22.canopy, f32[15,480,128]{2,1,0:T(8,128)} %soil.5, f32[15,480,128]{2,1,0:T(8,128)} %porosity.5, ...), custom_call_target="tpu_custom_call" | custom-call | flops 100000000 | bytes 9437184 | tf_op jit(solution)/shard_map/new_soil/pallas_call | solution.py:495
  50.6 0.0 collective-permute-done.2.before
  50.6 0.0 collective-permute-done.3.after
  50.6 0.1 static_halo.1._.fixed
  50.7 6.1 %all-to-all-done.1 = f32[32,32,128]{2,1,0:T(8,128)S(1)} async-done(((f32[32,32,128]{2,1,0:T(8,128)}), f32[32,32,128]{2,1,0:T(8,128)S(1)}, u32[]{:S(2)}, u32[]{:S(2)}) %all-to-all-start.1) | async-done | bytes 524320 | tf_op jit(solution)/shard_map/all_to_all | solution.py:637
  56.8 0.0 copy-done.5
  56.8 1.4 %unpack_runoff.1 = (f32[64,128]{1,0:T(8,128)}, f32[64,128]{1,0:T(8,128)S(1)}, f32[128,128]{1,0:T(8,128)}) custom-call(f32[1024,128]{1,0:T(8,128)S(1)} %bitcast.11, s32[1024,128]{1,0:T(8,128)S(1)} %get-tuple-element.26.code, bf16[64,1024]{1,0:T(8,128)(2,1)S(1)} %get-tuple-element.27.place, f32[64,128]{1,0:T(8,128)S(1)} %copy-done.5, ...), custom_call_target="tpu_custom_call" | custom-call | flops 1000000000 | bytes 1048576 | tf_op jit(solution)/shard_map/unpack_runoff/pallas_call | solution.py:261
  58.2 3.1 %all-to-all-start.2 = ((f32[32,4,128]{2,1,0:T(4,128)}), f32[32,4,128]{2,1,0:T(4,128)S(1)}, u32[]{:S(2)}, u32[]{:S(2)}) async-start(f32[32,4,128]{2,1,0:T(4,128)} %bitcast.7), calls=%async_computation.2 | async-start | bytes 131072 | tf_op jit(solution)/shard_map/all_to_all | solution.py:637
  61.3 3.3 %new_soil.3 = (f32[15,480,128]{2,1,0:T(8,128)}, f32[480,128]{1,0:T(8,128)}) custom-call(f32[480,128]{1,0:T(8,128)S(1)} %get-tuple-element.20.through, f32[480,128]{1,0:T(8,128)S(1)} %get-tuple-element.21.lost, f32[480,128]{1,0:T(8,128)S(1)} %get-tuple-element.22.canopy, f32[15,480,128]{2,1,0:T(8,128)} %soil.5, ...), custom_call_target="tpu_custom_call", output_to_operand_aliasing={{0}: (6, {}), {1}: (7, {})} | custom-call | flops 100000000 | bytes 6291456 | tf_op jit(solution)/shard_map/new_soil/pallas_call | solution.py:495
  64.6 1.2 %unpack_evap.1 = f32[64,128]{1,0:T(8,128)} custom-call(f32[1024,128]{1,0:T(8,128)S(1)} %bitcast.12, s32[1024,128]{1,0:T(8,128)S(1)} %get-tuple-element.26.code, bf16[64,1024]{1,0:T(8,128)(2,1)S(1)} %get-tuple-element.27.place), custom_call_target="tpu_custom_call" | custom-call | flops 1000000000 | bytes 1048576 | tf_op jit(solution)/shard_map/unpack_evap/pallas_call | solution.py:277
  65.8 2.9 %all-to-all-done.2 = f32[32,4,128]{2,1,0:T(4,128)S(1)} async-done(((f32[32,4,128]{2,1,0:T(4,128)}), f32[32,4,128]{2,1,0:T(4,128)S(1)}, u32[]{:S(2)}, u32[]{:S(2)}) %all-to-all-start.2) | async-done | bytes 65568 | tf_op jit(solution)/shard_map/all_to_all | solution.py:637
  68.7 1.2 %river_steps.1 = f32[64,128]{1,0:T(8,128)} custom-call(f32[64,128]{1,0:T(8,128)S(1)} %get-tuple-element.34.state, f32[128,128]{1,0:T(8,128)S(1)} %bitcast.13, f32[2,72,256]{2,1,0:T(8,128)S(1)} %static_halo.1._.fixed, f32[480,128]{1,0:T(8,128)} %get-tuple-element.16._), custom_call_target="tpu_custom_call" | custom-call | flops 10000000 | bytes 1048576 | tf_op jit(solution)/shard_map/river_steps/pallas_call | solution.py:626
  (4 shorter events, 0.0 us)
Async XLA Ops:
  0.6 11.0 %copy-start.9 = (s32[64,128]{1,0:T(8,128)S(1)}, s32[64,128]{1,0:T(8,128)}, u32[]{:S(2)}) copy-start(s32[64,128]{1,0:T(8,128)} %param.17) | copy-start | bytes 98308
  0.6 11.0 %copy-start.8 = (f32[64,128]{1,0:T(8,128)S(1)}, f32[64,128]{1,0:T(8,128)}, u32[]{:S(2)}) copy-start(f32[64,128]{1,0:T(8,128)} %param.16) | copy-start | bytes 98308
  0.7 16.0 %copy-start.4 = (s32[480]{0:T(512)S(1)}, s32[480]{0:T(512)}, u32[]{:S(2)}) copy-start(s32[480]{0:T(512)} %slots.1) | copy-start | bytes 5764
  0.7 16.1 %copy-start = (s32[480,128]{1,0:T(8,128)S(1)}, s32[480,128]{1,0:T(8,128)}, u32[]{:S(2)}) copy-start(s32[480,128]{1,0:T(8,128)} %cell.3) | copy-start | bytes 737284
  4.3 28.0 %all-to-all-start = ((f32[32,48,128]{2,1,0:T(8,128)}), f32[32,48,128]{2,1,0:T(8,128)S(1)}, u32[]{:S(2)}, u32[]{:S(2)}) async-start(f32[32,48,128]{2,1,0:T(8,128)} %bitcast), calls=%async_computation | async-start | bytes 1572864 | tf_op jit(solution)/shard_map/all_to_all | solution.py:637
  11.6 16.0 %collective-permute-start = (f32[2,4,128]{2,1,0:T(4,128)S(1)}, f32[2,4,128]{2,1,0:T(4,128)S(1)}, u32[]{:S(2)}, u32[]{:S(2)}) collective-permute-start(f32[2,4,128]{2,1,0:T(4,128)S(1)} %get-tuple-element.36), channel_id=1, source_target_pairs={{0,8},{8,16},{16,24},{1,9},{9,17},{17,25},{2,10},{10,18},{18,26},{... | collective-permute-start | bytes 12296 | tf_op jit(solution)/shard_map/ppermute | solution.py:519
  15.3 12.4 %collective-permute-start.1 = (f32[2,4,128]{2,1,0:T(4,128)S(1)}, f32[2,4,128]{2,1,0:T(4,128)S(1)}, u32[]{:S(2)}, u32[]{:S(2)}) collective-permute-start(f32[2,4,128]{2,1,0:T(4,128)S(1)} %get-tuple-element.35), channel_id=1, source_target_pairs={{8,0},{16,8},{24,16},{9,1},{17,9},{25,17},{10,2},{18,10},{26,18},{... | collective-permute-start | bytes 12296 | tf_op jit(solution)/shard_map/ppermute | solution.py:519
  18.7 13.5 %copy-start.1 = (f32[480,128]{1,0:T(8,128)S(1)}, f32[480,128]{1,0:T(8,128)}, u32[]{:S(2)}) copy-start(f32[480,128]{1,0:T(8,128)} %area.1) | copy-start | bytes 737284
  18.7 13.5 %copy-start.2 = (f32[480,128]{1,0:T(8,128)S(1)}, f32[480,128]{1,0:T(8,128)}, u32[]{:S(2)}) copy-start(f32[480,128]{1,0:T(8,128)} %water.1) | copy-start | bytes 737284
  18.7 13.5 %copy-start.3 = (f32[480,128]{1,0:T(8,128)S(1)}, f32[480,128]{1,0:T(8,128)}, u32[]{:S(2)}) copy-start(f32[480,128]{1,0:T(8,128)} %cap.1) | copy-start | bytes 737284
  32.3 9.0 %copy-start.6 = (s32[1,1024]{1,0:T(1,128)S(1)}, s32[1,1024]{1,0:T(1,128)}, u32[]{:S(2)}) copy-start(s32[1,1024]{1,0:T(1,128)} %slot.1) | copy-start | bytes 12292
  32.3 9.0 %copy-start.7 = (s32[1,1024]{1,0:T(1,128)S(1)}, s32[1,1024]{1,0:T(1,128)}, u32[]{:S(2)}) copy-start(s32[1,1024]{1,0:T(1,128)} %offset.1) | copy-start | bytes 12292
  37.7 19.2 %all-to-all-start.1 = ((f32[32,32,128]{2,1,0:T(8,128)}), f32[32,32,128]{2,1,0:T(8,128)S(1)}, u32[]{:S(2)}, u32[]{:S(2)}) async-start(f32[32,32,128]{2,1,0:T(8,128)} %bitcast.5), calls=%async_computation.1 | async-start | bytes 1048576 | tf_op jit(solution)/shard_map/all_to_all | solution.py:637
  42.1 8.6 %collective-permute-start.2 = (f32[8,128]{1,0:T(8,128)S(1)}, f32[8,128]{1,0:T(8,128)S(1)}, u32[]{:S(2)}, u32[]{:S(2)}) collective-permute-start(f32[8,128]{1,0:T(8,128)S(1)} %get-tuple-element.28), channel_id=1, source_target_pairs={{0,1},{1,2},{2,3},{3,4},{4,5},{5,6},{6,7},{8,9},{9,10},{10,11},{11... | collective-permute-start | bytes 12296 | tf_op jit(solution)/shard_map/ppermute | solution.py:685
  44.3 6.4 %collective-permute-start.3 = (f32[8,128]{1,0:T(8,128)S(1)}, f32[8,128]{1,0:T(8,128)S(1)}, u32[]{:S(2)}, u32[]{:S(2)}) collective-permute-start(f32[8,128]{1,0:T(8,128)S(1)} %get-tuple-element.29), channel_id=1, source_target_pairs={{1,0},{2,1},{3,2},{4,3},{5,4},{6,5},{7,6},{9,8},{10,9},{11,10},{12... | collective-permute-start | bytes 12296 | tf_op jit(solution)/shard_map/ppermute | solution.py:686
  45.6 11.3 %copy-start.5 = (f32[64,128]{1,0:T(8,128)S(1)}, f32[64,128]{1,0:T(8,128)}, u32[]{:S(2)}) copy-start(f32[64,128]{1,0:T(8,128)} %river.1) | copy-start | bytes 98308
  58.2 10.5 %all-to-all-start.2 = ((f32[32,4,128]{2,1,0:T(4,128)}), f32[32,4,128]{2,1,0:T(4,128)S(1)}, u32[]{:S(2)}, u32[]{:S(2)}) async-start(f32[32,4,128]{2,1,0:T(4,128)} %bitcast.7), calls=%async_computation.2 | async-start | bytes 131072 | tf_op jit(solution)/shard_map/all_to_all | solution.py:637

commit v5 on v2

--- a/solution.py
+++ b/solution.py
@@ -14,7 +14,8 @@
 VMEM_LIMIT = 24 * MIB
 
 directions = ((0, 1), (1, 1), (1, 0), (1, -1), (0, -1), (-1, -1), (-1, 0), (-1, 1))
-axes = ("region", "col")
+region = ("half", "near")
+axes = ("half", "near", "col")
 
 
 def iota(shape, dim):
@@ -52,20 +53,20 @@
     )
 
 
-def slot_factors(slot, offset, homes, capacity):
+def slot_factors(slot, offset, homes, capacity, first=0):
     slots = slot.shape[1]
     worker = slot // capacity if capacity & (capacity - 1) else slot >> (capacity.bit_length() - 1)
     position = slot - worker * capacity
-    by_worker = onehot(iota((homes, slots), 0) == worker)
+    by_worker = onehot(iota((homes, slots), 0) + first == worker)
     at_position = iota((capacity, slots), 0) == position
     row = jnp.where(at_position, ((offset >> 7) + 1).astype(jnp.float32), 0.0)
     lane = jnp.where(at_position, (offset & 127).astype(jnp.float32), 0.0)
     return by_worker, row.astype(jnp.bfloat16), lane.astype(jnp.bfloat16)
 
 
-def slot_table(slot, offset, homes, capacity, split=False):
-    slots = slot.shape[1]
-    by_worker, row, lane = slot_factors(slot, offset, homes, capacity)
+def slot_table(slot, offset, homes, capacity, first=0, split=False):
+    slots = homes * capacity
+    by_worker, row, lane = slot_factors(slot, offset, homes, capacity, first)
     table = matmul(by_worker, jnp.concatenate([row, lane], axis=0), 1, 1)
     groups = 2 if split else 1
     spread = jnp.broadcast_to(
@@ -100,34 +101,23 @@
     return rows.astype(jnp.int32) - 1, lanes.astype(jnp.int32)
 
 
-def pack_kernel(
-    homes, capacity, slot_in, offset_in, forcing_in, out, slot, offset, forcing, rain, ready
-):
-    copies = [
-        pltpu.make_async_copy(source, target, ready.at[i])
-        for i, (source, target) in enumerate(
-            ((slot_in, slot), (offset_in, offset), (forcing_in, forcing))
-        )
-    ]
-    for copy in copies:
-        copy.start()
-    slots = slot.shape[1]
+def put_windows(homes, capacity, stride, shift, out, rain, slots, offsets, values):
+    first_home = lax.axis_index("half") * homes
     pairs = capacity // 2
-    lane_rows = forcing.shape[1]
-    copies[0].wait()
-    copies[1].wait()
-    places = slot_table(slot[...], offset[...], homes, capacity, True)
-    copies[2].wait()
-    parts = []
-    for var in range(3):
-        here = forcing[var]
-        following = jnp.concatenate([here[1:], here[:1]], axis=0)
-        parts += [here, following]
-    table = jnp.concatenate(thirds(jnp.concatenate(parts, axis=1)), axis=0)
+    half = homes * pairs
+    lane_rows = values.shape[1]
     chunk = 128
     here = iota((chunk, LANES), 1)
-    for start in range(0, slots, chunk):
-        odd = start >= slots // 2
+    places = slot_table(slots, offsets, homes, capacity, first_home, True)
+    limit = pltpu.roll(values[2], WINDOW, 1)
+    above = jnp.concatenate([limit[lane_rows - 1 :], limit[: lane_rows - 1]], axis=0)
+    limit = jnp.where(iota(limit.shape, 1) < WINDOW, above, limit)
+    parts = []
+    for own in (values[0], values[1], limit):
+        parts += [own, jnp.concatenate([own[1:], own[:1]], axis=0)]
+    table = jnp.concatenate(thirds(jnp.concatenate(parts, axis=1)), axis=0)
+    for start in range(0, 2 * half, chunk):
+        odd = start >= half
         row, lane = slot_columns(places[start : start + chunk])
         shape = (chunk, 3 * lane_rows)
         wide = jnp.concatenate([row, row], axis=1)[:, : 3 * lane_rows]
@@ -144,10 +134,9 @@
         ]
         first = (here + lane) & 127
         second = (first + WINDOW) & 127
-        losses = jnp.where(
-            here < WINDOW, lane_pick(joined[1], first), lane_pick(joined[2], second)
-        )
-        base = start - slots // 2 if odd else start
+        demanded = ((here - lane) & 127) < WINDOW
+        losses = lane_pick(jnp.where(demanded, joined[1], joined[2]), first)
+        base = start - half if odd else start
         if odd:
             rains = jnp.where(
                 here < WINDOW, rain[pl.ds(base, chunk), :], lane_pick(joined[0], second)
@@ -155,7 +144,7 @@
         else:
             rain[pl.ds(base, chunk), :] = lane_pick(joined[0], first)
         for part in range(0, chunk, pairs):
-            place = (base + part) * 3
+            place = (base + part) * stride + shift
             if odd:
                 out[pl.ds(place + pairs, pairs), :] = rains[part : part + pairs]
                 out[pl.ds(place + 2 * pairs, pairs), :] = losses[part : part + pairs]
@@ -163,23 +152,58 @@
                 out[pl.ds(place, pairs), :] = losses[part : part + pairs]
 
 
-def pack(homes, capacity, slot, offset, forcing):
-    slots = slot.shape[1]
-    return pl.pallas_call(
-        functools.partial(pack_kernel, homes, capacity),
+def pack_own_kernel(
+    homes, capacity, slot_in, offset_in, forcing_in, out, slot, offset, forcing, rain, ready
+):
+    copies = [
+        pltpu.make_async_copy(source, target, ready.at[i])
+        for i, (source, target) in enumerate(
+            ((slot_in, slot), (offset_in, offset), (forcing_in, forcing))
+        )
+    ]
+    for copy in copies:
+        copy.start()
+    for copy in copies:
+        copy.wait()
+    put_windows(homes, capacity, 3, 0, out, rain, slot[...], offset[...], forcing)
+
+
+def pack_own(homes, capacity, slot, offset, forcing):
+    rows = homes * capacity // 2
+    return pl.pallas_call(
+        functools.partial(pack_own_kernel, homes, capacity),
         in_specs=[pl.BlockSpec(memory_space=pltpu.HBM)] * 3,
-        out_shape=jax.ShapeDtypeStruct((slots + slots // 2, LANES), jnp.float32),
+        out_shape=jax.ShapeDtypeStruct((3 * rows, LANES), jnp.float32),
         scratch_shapes=[
             pltpu.VMEM(slot.shape, jnp.int32),
             pltpu.VMEM(offset.shape, jnp.int32),
             pltpu.VMEM(forcing.shape, jnp.float32),
-            pltpu.VMEM((slots // 2, LANES), jnp.float32),
+            pltpu.VMEM((rows, LANES), jnp.float32),
             pltpu.SemaphoreType.DMA((3,)),
         ],
         compiler_params=pltpu.CompilerParams(vmem_limit_bytes=VMEM_LIMIT),
         cost_estimate=pl.CostEstimate(flops=10**9, bytes_accessed=2 * MIB, transcendentals=0),
-        name="pack_forcing",
+        name="pack_own",
     )(in_hbm(slot), in_hbm(offset), in_hbm(forcing))
+
+
+def pack_both_kernel(homes, capacity, own, far_slots, far_forcing, out, rain):
+    size = own.shape[0] // homes
+    for home in range(homes):
+        out[pl.ds(2 * size * home, size), :] = own[pl.ds(size * home, size), :]
+    slots, offsets = far_slots[pl.ds(0, 1), :], far_slots[pl.ds(1, 1), :]
+    put_windows(homes, capacity, 6, size, out, rain, slots, offsets, far_forcing)
+
+
+def pack_both(homes, capacity, own, far_slots, far_forcing):
+    return pl.pallas_call(
+        functools.partial(pack_both_kernel, homes, capacity),
+        out_shape=jax.ShapeDtypeStruct((2 * own.shape[0], LANES), jnp.float32),
+        scratch_shapes=[pltpu.VMEM((homes * capacity // 2, LANES), jnp.float32)],
+        compiler_params=pltpu.CompilerParams(vmem_limit_bytes=VMEM_LIMIT),
+        cost_estimate=pl.CostEstimate(flops=10**9, bytes_accessed=2 * MIB, transcendentals=0),
+        name="pack_both",
+    )(own, far_slots, far_forcing)
 
 
 def unpack_plan_kernel(homes, capacity, lane_rows, slot, offset, code, place):
@@ -209,7 +233,7 @@
 
 def strips_for_neighbours(state, rows):
     device = iota((rows, LANES), 0) // ITERS
-    down = device // lax.axis_size("col") - lax.axis_index("region")
+    down = device // lax.axis_size("col") - lax.axis_index(region)
     right = device % lax.axis_size("col") - lax.axis_index("col")
     height, width = state.shape
     columns = jnp.transpose(state)
@@ -478,6 +502,22 @@
     return lax.ppermute(last, axis, up), lax.ppermute(initial, axis, down)
 
 
+def rate_and_code_kernel(rate, code, _, out):
+    out[0] = rate[...]
+    out[1] = code[...].astype(jnp.float32)
+
+
+def rate_and_code(rate, code, after):
+    return pl.pallas_call(
+        rate_and_code_kernel,
+        in_specs=[pl.BlockSpec(memory_space=pltpu.VMEM)] * 2 + [pl.BlockSpec(memory_space=pl.ANY)],
+        out_shape=jax.ShapeDtypeStruct((2,) + rate.shape, jnp.float32),
+        compiler_params=pltpu.CompilerParams(vmem_limit_bytes=VMEM_LIMIT),
+        cost_estimate=pl.CostEstimate(flops=10**5, bytes_accessed=10**5, transcendentals=0),
+        name="rate_and_code",
+    )(rate, code, after)
+
+
 def edge_columns_kernel(tall, _, first, last):
     arrays, height, width = tall.shape
     for number in range(arrays):
@@ -524,8 +564,8 @@
 
 
 def neighbour(down, right):
-    row, column = lax.axis_index("region") + down, lax.axis_index("col") + right
-    there = (row >= 0) & (row < lax.axis_size("region"))
+    row, column = lax.axis_index(region) + down, lax.axis_index("col") + right
+    there = (row >= 0) & (row < lax.axis_size(region))
     there &= (column >= 0) & (column < lax.axis_size("col"))
     return jnp.where(there, row * lax.axis_size("col") + column, 0), jnp.where(there, 1.0, 0.0)
 
@@ -592,8 +632,8 @@
     )(state, strips, fixed, in_hbm(after))
 
 
-def exchange(value):
-    return lax.all_to_all(value, axes, split_axis=0, concat_axis=0, tiled=True)
+def exchange(value, over=axes):
+    return lax.all_to_all(value, over, split_axis=0, concat_axis=0, tiled=True)
 
 
 def shards(
@@ -612,21 +652,26 @@
     porosity,
     drainage,
 ):
-    homes = lax.axis_size("region") * lax.axis_size("col")
+    homes = lax.axis_size(region) * lax.axis_size("col")
     capacity = home_slot.shape[1] // homes
     grid_rows, grid_cols = river_storage.shape
     lane_rows = grid_rows * grid_cols // LANES
-    outgoing = pack(
-        homes, capacity, home_slot, home_offset, forcing.reshape(3, lane_rows, LANES)
-    )
-    arrived = exchange(outgoing)
+    forcing = forcing.reshape(3, lane_rows, LANES)
+    swap = [(0, 1), (1, 0)]
+    far_slots = lax.ppermute(jnp.concatenate([home_slot, home_offset], axis=0), "half", swap)
+    far_forcing = lax.ppermute(forcing, "half", swap)
+    own = pack_own(homes // 2, capacity, home_slot, home_offset, forcing)
+    outgoing = pack_both(homes // 2, capacity, own, far_slots, far_forcing)
+    arrived = exchange(outgoing, ("near", "col"))
     home = worker_list // capacity
     position = worker_list - home * capacity
     pairs = capacity // 2
-    first_rows = home * (3 * pairs) + position // 2 + position % 2 * pairs
+    own_half = home // (homes // 2) == lax.axis_index("half")
+    first_rows = home % (homes // 2) * (6 * pairs) + jnp.where(own_half, 0, 3 * pairs)
+    first_rows = first_rows + position // 2 + position % 2 * pairs
     meta = segment_plan(patch_cell, worker_list[:, None])
-    fixed = jnp.stack([river_rate, flow_code.astype(jnp.float32)])
-    above, below = halo_parts(fixed, "region", 1, ITERS)
+    fixed = rate_and_code(river_rate, flow_code, outgoing)
+    above, below = halo_parts(fixed, region, 1, ITERS)
     through, lost, canopy, sums = land_sums(
         (homes * capacity, LANES), pairs, worker_list, first_rows, arrived, patch_cell, meta,
         patch_area, canopy_water, canopy_cap, soil_water, porosity, drainage, (above, below),
@@ -662,32 +707,34 @@
 
 
 def solution(mesh):
+    rows, cols = mesh.devices.shape
+    mesh = jax.sharding.Mesh(mesh.devices.reshape(2, rows // 2, cols), axes)
     placed = (
-        P(None, "region", "col"),
-        P("region", "col"),
-        P("region", "col"),
-        P("region", "col"),
-        P(("region", "col"), None),
-        P(("region", "col"), None),
-        P(("region", "col")),
-        P(("region", "col"), None),
-        P(("region", "col"), None),
-        P(("region", "col"), None),
-        P(("region", "col"), None),
-        P(None, ("region", "col"), None),
-        P(None, ("region", "col"), None),
-        P(None, ("region", "col"), None),
+        P(None, region, "col"),
+        P(region, "col"),
+        P(region, "col"),
+        P(region, "col"),
+        P(axes, None),
+        P(axes, None),
+        P(axes),
+        P(axes, None),
+        P(axes, None),
+        P(axes, None),
+        P(axes, None),
+        P(None, axes, None),
+        P(None, axes, None),
+        P(None, axes, None),
     )
     return jax.shard_map(
         shards,
         mesh=mesh,
         in_specs=placed,
         out_specs=(
-            P(None, ("region", "col"), None),
-            P(("region", "col"), None),
-            P("region", "col"),
-            P("region", "col"),
-            P("region", "col"),
+            P(None, axes, None),
+            P(axes, None),
+            P(region, "col"),
+            P(region, "col"),
+            P(region, "col"),
         ),
         check_vma=False,
     )

time: 71.4 us -> 69.4 us (0.972)
  waiting for transfers between devices: 21.7 us -> 16.8 us
  starting transfers between devices: 23.3 us -> 25 us
    all_to_all x3, waiting for transfers between devices: 16.2 us -> 10.8 us  [exchange(): return lax.all_to_all(value, over, split_axis=0, concat_axis=0, tiled=True)]
    ppermute x0 -> x2, starting transfers between devices: none -> 4.19 us  [the longest x1 4.1 us: shards(): far_forcing = lax.ppermute(forcing, 'half', swap)]
    all_to_all x3, starting transfers between devices: 14 us -> 11.5 us  [exchange(): return lax.all_to_all(value, over, split_axis=0, concat_axis=0, tiled=True)]
    ppermute x0 -> x2, waiting for transfers between devices: none -> 2.38 us  [the longest x1 2.37 us: shards(): lax.ppermute(jnp.concatenate([home_slot, home_offset], axis=0), 'half', s...]
    ppermute x2, waiting for transfers between devices: 5.45 us -> 3.62 us  [halo_parts(): return (lax.ppermute(last, axis, up), lax.ppermute(initial, axis, down))]
    pallas_call x1 -> x3, Pallas kernels: 3.7 us -> 4.16 us  [the longest x1 2.11 us: pack_own(): pl.pallas_call(functools.partial(pack_own_kernel, homes, capacity), in_sp...]
  transfers between devices with their start and end apart: 7 -> 9, of which waited for: 5 -> 5; matrix products, arithmetic and copies ran while one was open for 0% -> 1% of each run, Pallas kernels for 17% -> 21%
where the time goes in v5:
time: 69.4 us; the launch traced here: 68.9 us
  Pallas kernels  25.3 us (36%)
  starting transfers between devices  25 us (36%)
  waiting for transfers between devices  16.8 us (24%)
  between operations  0.91 us (1%)
  other arithmetic  0.75 us (1%)
    all_to_all x3, starting transfers between devices, exchange(): return lax.all_to_all(value, over, split_axis=0, concat_axis=0, tiled=True)  11.5 us
    all_to_all x3, waiting for transfers between devices, exchange(): return lax.all_to_all(value, over, split_axis=0, concat_axis=0, tiled=True)  10.8 us
    pallas_call x2, Pallas kernels, new_soil(): pl.pallas_call(new_soil_kernel, grid=(last - first,), in_specs=[flat, fla...  8.36 us
    pallas_call x1, Pallas kernels, land_sums(): pl.pallas_call(functools.partial(land_sums_kernel, pairs), in_specs=[pl.B...  6.28 us
    ppermute x2, starting transfers between devices, halo_parts(): return (lax.ppermute(last, axis, up), lax.ppermute(initial, axis, down))  5.84 us
    ppermute x1, starting transfers between devices, shards(): far_forcing = lax.ppermute(forcing, 'half', swap)  4.1 us
    ppermute x2, waiting for transfers between devices, halo_parts(): return (lax.ppermute(last, axis, up), lax.ppermute(initial, axis, down))  3.62 us
    ppermute x1, waiting for transfers between devices, shards(): lax.ppermute(jnp.concatenate([home_slot, home_offset], axis=0), 'half', s...  2.37 us
  transfers between devices with their start and end apart: 9, of which 5 were waited for; matrix products, arithmetic and copies ran while one was open for 1% of the time, Pallas kernels for 21%

profile of v5, /device:TPU:0, one launch (start us, length us, event | category | flops | bytes accessed | tf_op | source)
XLA Modules:
  0.0 68.9 jit_solution(14634266516859535823)
XLA Ops:
  0.6 4.1 %collective-permute-start.1 = (f32[3,64,128]{2,1,0:T(8,128)}, f32[3,64,128]{2,1,0:T(8,128)S(1)}, u32[]{:S(2)}, u32[]{:S(2)}) collective-permute-start(f32[3,64,128]{2,1,0:T(8,128)} %forcing_in.1), channel_id=1, source_target_pairs={{0,16},{16,0},{1,17},{17,1},{2,18},{18,2},{3,19},{19,3},{4,20},{20... | collective-permute-start | bytes 294920 | tf_op jit(solution)/shard_map/ppermute | solution.py:662
  4.7 0.7 %pad_add_fusion = s32[2,1024]{1,0:T(2,128)S(1)} fusion(s32[1,1024]{1,0:T(1,128)} %offset.1, s32[1,1024]{1,0:T(1,128)} %slot.1), kind=kLoop, calls=%fused_computation.1 | loop fusion | flops 2048 | bytes 16384 | tf_op jit(solution)/shard_map/concatenate | solution.py:661
  5.4 0.0 copy-start.6
  5.5 0.1 collective-permute-start
  5.5 2.1 %pack_own.1.own = f32[768,128]{1,0:T(8,128)S(1)} custom-call(s32[1,1024]{1,0:T(1,128)} %slot.1, s32[1,1024]{1,0:T(1,128)} %offset.1, f32[3,64,128]{2,1,0:T(8,128)} %forcing_in.1), custom_call_target="tpu_custom_call" | custom-call | flops 1000000000 | bytes 2097152 | tf_op jit(solution)/shard_map/pack_own/pallas_call | solution.py:173
  7.7 0.0 copy-start.4
  7.7 0.0 copy-start.5
  7.7 0.0 copy-start
  7.7 0.0 copy-start.1
  7.7 0.0 copy-start.2
  7.7 0.0 copy-start.3
  7.7 2.4 %collective-permute-done.far_slots = s32[2,1024]{1,0:T(2,128)S(1)} collective-permute-done((s32[2,1024]{1,0:T(2,128)S(1)}, s32[2,1024]{1,0:T(2,128)S(1)}, u32[]{:S(2)}, u32[]{:S(2)}) %collective-permute-start) | collective-permute-done | bytes 8224 | tf_op jit(solution)/shard_map/ppermute | solution.py:661
  10.1 0.0 collective-permute-done.1.far_forcing
  10.1 2.0 %pack_both.1._ = f32[1536,128]{1,0:T(8,128)} custom-call(f32[768,128]{1,0:T(8,128)S(1)} %pack_own.1.own, s32[2,1024]{1,0:T(2,128)S(1)} %collective-permute-done.far_slots, f32[3,64,128]{2,1,0:T(8,128)S(1)} %collective-permute-done.1.far_forcing), custom_call_target="tpu_custom_call" | custom-call | flops 1000000000 | bytes 2097152 | tf_op jit(solution)/shard_map/pack_both/pallas_call | solution.py:199
  12.2 4.8 %all-to-all-start = ((f32[16,96,128]{2,1,0:T(8,128)}), f32[16,96,128]{2,1,0:T(8,128)S(1)}, u32[]{:S(2)}, u32[]{:S(2)}) async-start(f32[16,96,128]{2,1,0:T(8,128)} %bitcast), calls=%async_computation | async-start | bytes 1572864 | tf_op jit(solution)/shard_map/all_to_all | solution.py:636
  17.0 0.0 copy-done.6
  17.0 0.1 copy.21.worker
  17.2 0.0 copy-done.4
  17.2 0.0 copy-done.5
  17.2 1.3 %collective-permute-start.3 = (f32[2,4,128]{2,1,0:T(4,128)S(1)}, f32[2,4,128]{2,1,0:T(4,128)S(1)}, u32[]{:S(2)}, u32[]{:S(2)}) collective-permute-start(f32[2,4,128]{2,1,0:T(4,128)S(1)} %get-tuple-element.35), channel_id=1, source_target_pairs={{8,0},{16,8},{24,16},{9,1},{17,9},{25,17},{10,2},{18,10},{26,18},{... | collective-permute-start | bytes 12296 | tf_op jit(solution)/shard_map/ppermute | solution.py:502
  18.5 4.5 %collective-permute-start.2 = (f32[2,4,128]{2,1,0:T(4,128)S(1)}, f32[2,4,128]{2,1,0:T(4,128)S(1)}, u32[]{:S(2)}, u32[]{:S(2)}) collective-permute-start(f32[2,4,128]{2,1,0:T(4,128)S(1)} %get-tuple-element.36), channel_id=1, source_target_pairs={{0,8},{8,16},{16,24},{1,9},{9,17},{17,25},{2,10},{10,18},{18,26},{... | collective-permute-start | bytes 12296 | tf_op jit(solution)/shard_map/ppermute | solution.py:502
  23.1 0.0 copy-done
  23.1 1.9 %segment_plan.1.meta = s32[480,128]{1,0:T(8,128)S(1)} custom-call(s32[480,128]{1,0:T(8,128)S(1)} %copy-done, s32[480,1]{1,0:T(8,128)S(1)} %copy.21.worker), custom_call_target="tpu_custom_call" | custom-call | flops 100000000 | bytes 1048576 | tf_op jit(solution)/shard_map/segment_plan/pallas_call | solution.py:325
  25.0 3.6 %collective-permute-done.3.__ = f32[2,4,128]{2,1,0:T(4,128)S(1)} collective-permute-done((f32[2,4,128]{2,1,0:T(4,128)S(1)}, f32[2,4,128]{2,1,0:T(4,128)S(1)}, u32[]{:S(2)}, u32[]{:S(2)}) %collective-permute-start.3) | collective-permute-done | bytes 4128 | tf_op jit(solution)/shard_map/ppermute | solution.py:502
  28.6 0.0 collective-permute-done.2._
  28.6 1.8 %all-to-all-done = f32[16,96,128]{2,1,0:T(8,128)S(1)} async-done(((f32[16,96,128]{2,1,0:T(8,128)}), f32[16,96,128]{2,1,0:T(8,128)S(1)}, u32[]{:S(2)}, u32[]{:S(2)}) %all-to-all-start) | async-done | bytes 786464 | tf_op jit(solution)/shard_map/all_to_all | solution.py:636
  30.4 0.0 copy-done.1
  30.4 0.0 copy-done.2
  30.4 0.0 copy-done.3
  30.4 0.0 copy-start.7
  30.4 0.0 copy-start.8
  30.4 6.3 %land_sums.1 = (f32[480,128]{1,0:T(8,128)S(1)}, f32[480,128]{1,0:T(8,128)S(1)}, f32[480,128]{1,0:T(8,128)S(1)}, f32[1024,128]{1,0:T(8,128)}) custom-call(s32[480]{0:T(512)S(1)} %copy-done.6, s32[480]{0:T(512)S(1)} %fusion.4.first_rows, f32[1536,128]{1,0:T(8,128)S(1)} %bitcast.7, s32[480,128]{1,0:T(8,128)S(1)} %copy-done, s32[480,128]{1,0:T(8,128)S(1)} %segment_plan.1.meta, ...), custom_call_target="tpu_custom_call" | custom-call | flops 100000000 | bytes 20971520 | tf_op jit(solution)/shard_map/land_sums/pallas_call | solution.py:435
  36.7 3.6 %all-to-all-start.1 = ((f32[32,32,128]{2,1,0:T(8,128)}), f32[32,32,128]{2,1,0:T(8,128)S(1)}, u32[]{:S(2)}, u32[]{:S(2)}) async-start(f32[32,32,128]{2,1,0:T(8,128)} %bitcast.3), calls=%async_computation.1 | async-start | bytes 1048576 | tf_op jit(solution)/shard_map/all_to_all | solution.py:636
  40.3 0.0 copy-done.7
  40.3 0.0 copy-done.8
  40.3 0.7 unpack_plan.1
  41.0 0.1 edge_columns.1
  41.1 2.2 %collective-permute-start.4 = (f32[8,128]{1,0:T(8,128)S(1)}, f32[8,128]{1,0:T(8,128)S(1)}, u32[]{:S(2)}, u32[]{:S(2)}) collective-permute-start(f32[8,128]{1,0:T(8,128)S(1)} %get-tuple-element.28), channel_id=1, source_target_pairs={{0,1},{1,2},{2,3},{3,4},{4,5},{5,6},{6,7},{8,9},{9,10},{10,11},{11... | collective-permute-start | bytes 12296 | tf_op jit(solution)/shard_map/ppermute | solution.py:688
  43.3 1.3 %collective-permute-start.5 = (f32[8,128]{1,0:T(8,128)S(1)}, f32[8,128]{1,0:T(8,128)S(1)}, u32[]{:S(2)}, u32[]{:S(2)}) collective-permute-start(f32[8,128]{1,0:T(8,128)S(1)} %get-tuple-element.29), channel_id=1, source_target_pairs={{1,0},{2,1},{3,2},{4,3},{5,4},{6,5},{7,6},{9,8},{10,9},{11,10},{12... | collective-permute-start | bytes 12296 | tf_op jit(solution)/shard_map/ppermute | solution.py:689
  44.6 0.0 copy-start.9
  44.6 5.1 %new_soil.2 = (f32[15,480,128]{2,1,0:T(8,128)}, f32[480,128]{1,0:T(8,128)}) custom-call(f32[480,128]{1,0:T(8,128)S(1)} %get-tuple-element.20.through, f32[480,128]{1,0:T(8,128)S(1)} %get-tuple-element.21.lost, f32[480,128]{1,0:T(8,128)S(1)} %get-tuple-element.22.canopy, f32[15,480,128]{2,1,0:T(8,128)} %soil.3, f32[15,480,128]{2,1,0:T(8,128)} %porosity.3, ...), custom_call_target="tpu_custom_call" | custom-call | flops 100000000 | bytes 9437184 | tf_op jit(solution)/shard_map/new_soil/pallas_call | solution.py:478
  49.6 0.0 collective-permute-done.4.before
  49.6 0.0 collective-permute-done.5.after
  49.6 0.1 static_halo.1._.fixed
  49.7 6.1 %all-to-all-done.1 = f32[32,32,128]{2,1,0:T(8,128)S(1)} async-done(((f32[32,32,128]{2,1,0:T(8,128)}), f32[32,32,128]{2,1,0:T(8,128)S(1)}, u32[]{:S(2)}, u32[]{:S(2)}) %all-to-all-start.1) | async-done | bytes 524320 | tf_op jit(solution)/shard_map/all_to_all | solution.py:636
  55.9 0.0 copy-done.9
  55.9 1.3 %unpack_runoff.1 = (f32[64,128]{1,0:T(8,128)}, f32[64,128]{1,0:T(8,128)S(1)}, f32[128,128]{1,0:T(8,128)}) custom-call(f32[1024,128]{1,0:T(8,128)S(1)} %bitcast.8, s32[1024,128]{1,0:T(8,128)S(1)} %get-tuple-element.26.code, bf16[64,1024]{1,0:T(8,128)(2,1)S(1)} %get-tuple-element.27.place, f32[64,128]{1,0:T(8,128)S(1)} %copy-done.9, ...), custom_call_target="tpu_custom_call" | custom-call | flops 1000000000 | bytes 1048576 | tf_op jit(solution)/shard_map/unpack_runoff/pallas_call | solution.py:285
  57.2 3.1 %all-to-all-start.2 = ((f32[32,4,128]{2,1,0:T(4,128)}), f32[32,4,128]{2,1,0:T(4,128)S(1)}, u32[]{:S(2)}, u32[]{:S(2)}) async-start(f32[32,4,128]{2,1,0:T(4,128)} %bitcast.5), calls=%async_computation.2 | async-start | bytes 131072 | tf_op jit(solution)/shard_map/all_to_all | solution.py:636
  60.3 3.3 %new_soil.3 = (f32[15,480,128]{2,1,0:T(8,128)}, f32[480,128]{1,0:T(8,128)}) custom-call(f32[480,128]{1,0:T(8,128)S(1)} %get-tuple-element.20.through, f32[480,128]{1,0:T(8,128)S(1)} %get-tuple-element.21.lost, f32[480,128]{1,0:T(8,128)S(1)} %get-tuple-element.22.canopy, f32[15,480,128]{2,1,0:T(8,128)} %soil.3, ...), custom_call_target="tpu_custom_call", output_to_operand_aliasing={{0}: (6, {}), {1}: (7, {})} | custom-call | flops 100000000 | bytes 6291456 | tf_op jit(solution)/shard_map/new_soil/pallas_call | solution.py:478
  63.6 1.2 %unpack_evap.1 = f32[64,128]{1,0:T(8,128)} custom-call(f32[1024,128]{1,0:T(8,128)S(1)} %bitcast.9, s32[1024,128]{1,0:T(8,128)S(1)} %get-tuple-element.26.code, bf16[64,1024]{1,0:T(8,128)(2,1)S(1)} %get-tuple-element.27.place), custom_call_target="tpu_custom_call" | custom-call | flops 1000000000 | bytes 1048576 | tf_op jit(solution)/shard_map/unpack_evap/pallas_call | solution.py:301
  64.8 2.9 %all-to-all-done.2 = f32[32,4,128]{2,1,0:T(4,128)S(1)} async-done(((f32[32,4,128]{2,1,0:T(4,128)}), f32[32,4,128]{2,1,0:T(4,128)S(1)}, u32[]{:S(2)}, u32[]{:S(2)}) %all-to-all-start.2) | async-done | bytes 65568 | tf_op jit(solution)/shard_map/all_to_all | solution.py:636
  67.7 1.2 %river_steps.1 = f32[64,128]{1,0:T(8,128)} custom-call(f32[64,128]{1,0:T(8,128)S(1)} %get-tuple-element.34.state, f32[128,128]{1,0:T(8,128)S(1)} %bitcast.10, f32[2,72,256]{2,1,0:T(8,128)S(1)} %static_halo.1._.fixed, f32[480,128]{1,0:T(8,128)} %get-tuple-element.16._), custom_call_target="tpu_custom_call" | custom-call | flops 10000000 | bytes 1048576 | tf_op jit(solution)/shard_map/river_steps/pallas_call | solution.py:625
  (4 shorter events, 0.0 us)
Async XLA Ops:
  0.6 9.5 %collective-permute-start.1 = (f32[3,64,128]{2,1,0:T(8,128)}, f32[3,64,128]{2,1,0:T(8,128)S(1)}, u32[]{:S(2)}, u32[]{:S(2)}) collective-permute-start(f32[3,64,128]{2,1,0:T(8,128)} %forcing_in.1), channel_id=1, source_target_pairs={{0,16},{16,0},{1,17},{17,1},{2,18},{18,2},{3,19},{19,3},{4,20},{20... | collective-permute-start | bytes 294920 | tf_op jit(solution)/shard_map/ppermute | solution.py:662
  5.4 11.5 %copy-start.6 = (s32[480]{0:T(512)S(1)}, s32[480]{0:T(512)}, u32[]{:S(2)}) copy-start(s32[480]{0:T(512)} %slots.1) | copy-start | bytes 5764
  5.5 4.6 %collective-permute-start = (s32[2,1024]{1,0:T(2,128)S(1)}, s32[2,1024]{1,0:T(2,128)S(1)}, u32[]{:S(2)}, u32[]{:S(2)}) collective-permute-start(s32[2,1024]{1,0:T(2,128)S(1)} %pad_add_fusion), channel_id=1, source_target_pairs={{0,16},{16,0},{1,17},{17,1},{2,18},{18,2},{3,19},{19,3},{4,20},{20... | collective-permute-start | bytes 24584 | tf_op jit(solution)/shard_map/ppermute | solution.py:661
  7.7 9.5 %copy-start.4 = (f32[64,128]{1,0:T(8,128)S(1)}, f32[64,128]{1,0:T(8,128)}, u32[]{:S(2)}) copy-start(f32[64,128]{1,0:T(8,128)} %rate.1) | copy-start | bytes 98308
  7.7 9.5 %copy-start.5 = (s32[64,128]{1,0:T(8,128)S(1)}, s32[64,128]{1,0:T(8,128)}, u32[]{:S(2)}) copy-start(s32[64,128]{1,0:T(8,128)} %code.1) | copy-start | bytes 98308
  7.7 15.4 %copy-start = (s32[480,128]{1,0:T(8,128)S(1)}, s32[480,128]{1,0:T(8,128)}, u32[]{:S(2)}) copy-start(s32[480,128]{1,0:T(8,128)} %cell.3) | copy-start | bytes 737284
  7.7 22.7 %copy-start.1 = (f32[480,128]{1,0:T(8,128)S(1)}, f32[480,128]{1,0:T(8,128)}, u32[]{:S(2)}) copy-start(f32[480,128]{1,0:T(8,128)} %area.1) | copy-start | bytes 737284
  7.7 22.7 %copy-start.2 = (f32[480,128]{1,0:T(8,128)S(1)}, f32[480,128]{1,0:T(8,128)}, u32[]{:S(2)}) copy-start(f32[480,128]{1,0:T(8,128)} %water.1) | copy-start | bytes 737284
  7.7 22.7 %copy-start.3 = (f32[480,128]{1,0:T(8,128)S(1)}, f32[480,128]{1,0:T(8,128)}, u32[]{:S(2)}) copy-start(f32[480,128]{1,0:T(8,128)} %cap.1) | copy-start | bytes 737284
  12.2 18.2 %all-to-all-start = ((f32[16,96,128]{2,1,0:T(8,128)}), f32[16,96,128]{2,1,0:T(8,128)S(1)}, u32[]{:S(2)}, u32[]{:S(2)}) async-start(f32[16,96,128]{2,1,0:T(8,128)} %bitcast), calls=%async_computation | async-start | bytes 1572864 | tf_op jit(solution)/shard_map/all_to_all | solution.py:636
  17.2 11.4 %collective-permute-start.3 = (f32[2,4,128]{2,1,0:T(4,128)S(1)}, f32[2,4,128]{2,1,0:T(4,128)S(1)}, u32[]{:S(2)}, u32[]{:S(2)}) collective-permute-start(f32[2,4,128]{2,1,0:T(4,128)S(1)} %get-tuple-element.35), channel_id=1, source_target_pairs={{8,0},{16,8},{24,16},{9,1},{17,9},{25,17},{10,2},{18,10},{26,18},{... | collective-permute-start | bytes 12296 | tf_op jit(solution)/shard_map/ppermute | solution.py:502
  18.5 10.1 %collective-permute-start.2 = (f32[2,4,128]{2,1,0:T(4,128)S(1)}, f32[2,4,128]{2,1,0:T(4,128)S(1)}, u32[]{:S(2)}, u32[]{:S(2)}) collective-permute-start(f32[2,4,128]{2,1,0:T(4,128)S(1)} %get-tuple-element.36), channel_id=1, source_target_pairs={{0,8},{8,16},{16,24},{1,9},{9,17},{17,25},{2,10},{10,18},{18,26},{... | collective-permute-start | bytes 12296 | tf_op jit(solution)/shard_map/ppermute | solution.py:502
  30.4 9.9 %copy-start.7 = (s32[1,1024]{1,0:T(1,128)S(1)}, s32[1,1024]{1,0:T(1,128)}, u32[]{:S(2)}) copy-start(s32[1,1024]{1,0:T(1,128)} %slot.1) | copy-start | bytes 12292
  30.4 9.9 %copy-start.8 = (s32[1,1024]{1,0:T(1,128)S(1)}, s32[1,1024]{1,0:T(1,128)}, u32[]{:S(2)}) copy-start(s32[1,1024]{1,0:T(1,128)} %offset.1) | copy-start | bytes 12292
  36.7 19.2 %all-to-all-start.1 = ((f32[32,32,128]{2,1,0:T(8,128)}), f32[32,32,128]{2,1,0:T(8,128)S(1)}, u32[]{:S(2)}, u32[]{:S(2)}) async-start(f32[32,32,128]{2,1,0:T(8,128)} %bitcast.3), calls=%async_computation.1 | async-start | bytes 1048576 | tf_op jit(solution)/shard_map/all_to_all | solution.py:636
  41.1 8.6 %collective-permute-start.4 = (f32[8,128]{1,0:T(8,128)S(1)}, f32[8,128]{1,0:T(8,128)S(1)}, u32[]{:S(2)}, u32[]{:S(2)}) collective-permute-start(f32[8,128]{1,0:T(8,128)S(1)} %get-tuple-element.28), channel_id=1, source_target_pairs={{0,1},{1,2},{2,3},{3,4},{4,5},{5,6},{6,7},{8,9},{9,10},{10,11},{11... | collective-permute-start | bytes 12296 | tf_op jit(solution)/shard_map/ppermute | solution.py:688
  43.3 6.4 %collective-permute-start.5 = (f32[8,128]{1,0:T(8,128)S(1)}, f32[8,128]{1,0:T(8,128)S(1)}, u32[]{:S(2)}, u32[]{:S(2)}) collective-permute-start(f32[8,128]{1,0:T(8,128)S(1)} %get-tuple-element.29), channel_id=1, source_target_pairs={{1,0},{2,1},{3,2},{4,3},{5,4},{6,5},{7,6},{9,8},{10,9},{11,10},{12... | collective-permute-start | bytes 12296 | tf_op jit(solution)/shard_map/ppermute | solution.py:689
  44.6 11.3 %copy-start.9 = (f32[64,128]{1,0:T(8,128)S(1)}, f32[64,128]{1,0:T(8,128)}, u32[]{:S(2)}) copy-start(f32[64,128]{1,0:T(8,128)} %river.1) | copy-start | bytes 98308
  57.2 10.5 %all-to-all-start.2 = ((f32[32,4,128]{2,1,0:T(4,128)}), f32[32,4,128]{2,1,0:T(4,128)S(1)}, u32[]{:S(2)}, u32[]{:S(2)}) async-start(f32[32,4,128]{2,1,0:T(4,128)} %bitcast.5), calls=%async_computation.2 | async-start | bytes 131072 | tf_op jit(solution)/shard_map/all_to_all | solution.py:636

commit v6 on v5

--- a/solution.py
+++ b/solution.py
@@ -187,15 +187,16 @@
     )(in_hbm(slot), in_hbm(offset), in_hbm(forcing))
 
 
-def pack_both_kernel(homes, capacity, own, far_slots, far_forcing, out, rain):
+def pack_both_kernel(homes, capacity, own, far_slot, far_offset, far_forcing, out, rain):
     size = own.shape[0] // homes
     for home in range(homes):
         out[pl.ds(2 * size * home, size), :] = own[pl.ds(size * home, size), :]
-    slots, offsets = far_slots[pl.ds(0, 1), :], far_slots[pl.ds(1, 1), :]
-    put_windows(homes, capacity, 6, size, out, rain, slots, offsets, far_forcing)
-
-
-def pack_both(homes, capacity, own, far_slots, far_forcing):
+    put_windows(
+        homes, capacity, 6, size, out, rain, far_slot[...], far_offset[...], far_forcing
+    )
+
+
+def pack_both(homes, capacity, own, far_slot, far_offset, far_forcing):
     return pl.pallas_call(
         functools.partial(pack_both_kernel, homes, capacity),
         out_shape=jax.ShapeDtypeStruct((2 * own.shape[0], LANES), jnp.float32),
@@ -203,7 +204,7 @@
         compiler_params=pltpu.CompilerParams(vmem_limit_bytes=VMEM_LIMIT),
         cost_estimate=pl.CostEstimate(flops=10**9, bytes_accessed=2 * MIB, transcendentals=0),
         name="pack_both",
-    )(own, far_slots, far_forcing)
+    )(own, far_slot, far_offset, far_forcing)
 
 
 def unpack_plan_kernel(homes, capacity, lane_rows, slot, offset, code, place):
@@ -658,10 +659,11 @@
     lane_rows = grid_rows * grid_cols // LANES
     forcing = forcing.reshape(3, lane_rows, LANES)
     swap = [(0, 1), (1, 0)]
-    far_slots = lax.ppermute(jnp.concatenate([home_slot, home_offset], axis=0), "half", swap)
+    far_slot = lax.ppermute(home_slot, "half", swap)
+    far_offset = lax.ppermute(home_offset, "half", swap)
     far_forcing = lax.ppermute(forcing, "half", swap)
     own = pack_own(homes // 2, capacity, home_slot, home_offset, forcing)
-    outgoing = pack_both(homes // 2, capacity, own, far_slots, far_forcing)
+    outgoing = pack_both(homes // 2, capacity, own, far_slot, far_offset, far_forcing)
     arrived = exchange(outgoing, ("near", "col"))
     home = worker_list // capacity
     position = worker_list - home * capacity

time: 69.4 us -> 69.4 us (level)
  starting transfers between devices: 25 us -> 27.8 us
  waiting for transfers between devices: 16.8 us -> 14.7 us
  other arithmetic: 0.75 us -> 0.04 us
    ppermute x1 -> x2, starting transfers between devices: 0.08 us -> 2.92 us  [the longest x1 2.85 us: shards(): far_offset = lax.ppermute(home_offset, 'half', swap)]
    ppermute x1 -> x2, waiting for transfers between devices: 2.37 us -> 0.26 us  [the longest x1 0.22 us: shards(): far_slot = lax.ppermute(home_slot, 'half', swap)]
    concatenate x1 -> x0, other arithmetic: 0.71 us -> none  [shards(): jnp.concatenate([home_slot, home_offset], axis=0)]
  transfers between devices with their start and end apart: 9 -> 10, of which waited for: 5 -> 5; matrix products, arithmetic and copies ran while one was open for 1% -> 0% of each run, Pallas kernels for 21% -> 21%
where the time goes in v6:
time: 69.4 us; the launch traced here: 68.9 us
  starting transfers between devices  27.8 us (40%)
  Pallas kernels  25.3 us (36%)
  waiting for transfers between devices  14.7 us (21%)
  between operations  0.91 us (1%)
    all_to_all x3, starting transfers between devices, exchange(): return lax.all_to_all(value, over, split_axis=0, concat_axis=0, tiled=True)  11.5 us
    all_to_all x3, waiting for transfers between devices, exchange(): return lax.all_to_all(value, over, split_axis=0, concat_axis=0, tiled=True)  10.8 us
    pallas_call x2, Pallas kernels, new_soil(): pl.pallas_call(new_soil_kernel, grid=(last - first,), in_specs=[flat, fla...  8.36 us
    pallas_call x1, Pallas kernels, land_sums(): pl.pallas_call(functools.partial(land_sums_kernel, pairs), in_specs=[pl.B...  6.28 us
    ppermute x2, starting transfers between devices, halo_parts(): return (lax.ppermute(last, axis, up), lax.ppermute(initial, axis, down))  5.84 us
    ppermute x1, starting transfers between devices, shards(): far_forcing = lax.ppermute(forcing, 'half', swap)  4.1 us
    ppermute x2, waiting for transfers between devices, halo_parts(): return (lax.ppermute(last, axis, up), lax.ppermute(initial, axis, down))  3.62 us
    ppermute x1, starting transfers between devices, shards(): far_offset = lax.ppermute(home_offset, 'half', swap)  2.85 us
  transfers between devices with their start and end apart: 10, of which 5 were waited for; matrix products, arithmetic and copies ran while one was open for 0% of the time, Pallas kernels for 21%

profile of v6, /device:TPU:0, one launch (start us, length us, event | category | flops | bytes accessed | tf_op | source)
XLA Modules:
  0.0 68.9 jit_solution(6296899426382390624)
XLA Ops:
  0.6 0.0 copy-start.6
  0.6 4.1 %collective-permute-start.2 = (f32[3,64,128]{2,1,0:T(8,128)}, f32[3,64,128]{2,1,0:T(8,128)S(1)}, u32[]{:S(2)}, u32[]{:S(2)}) collective-permute-start(f32[3,64,128]{2,1,0:T(8,128)} %forcing_in.1), channel_id=1, source_target_pairs={{0,16},{16,0},{1,17},{17,1},{2,18},{18,2},{3,19},{19,3},{4,20},{20... | collective-permute-start | bytes 294920 | tf_op jit(solution)/shard_map/ppermute | solution.py:664
  4.7 0.1 collective-permute-start
  4.8 2.8 %collective-permute-start.1 = (s32[1,1024]{1,0:T(1,128)}, s32[1,1024]{1,0:T(1,128)S(1)}, u32[]{:S(2)}, u32[]{:S(2)}) collective-permute-start(s32[1,1024]{1,0:T(1,128)} %offset.1), channel_id=1, source_target_pairs={{0,16},{16,0},{1,17},{17,1},{2,18},{18,2},{3,19},{19,3},{4,20},{20... | collective-permute-start | bytes 12296 | tf_op jit(solution)/shard_map/ppermute | solution.py:663
  7.7 2.1 %pack_own.1.own = f32[768,128]{1,0:T(8,128)S(1)} custom-call(s32[1,1024]{1,0:T(1,128)} %slot.1, s32[1,1024]{1,0:T(1,128)} %offset.1, f32[3,64,128]{2,1,0:T(8,128)} %forcing_in.1), custom_call_target="tpu_custom_call" | custom-call | flops 1000000000 | bytes 2097152 | tf_op jit(solution)/shard_map/pack_own/pallas_call | solution.py:173
  9.8 0.0 copy-start.4
  9.8 0.0 copy-start.5
  9.8 0.0 copy-start
  9.8 0.0 copy-start.1
  9.8 0.0 copy-start.2
  9.8 0.0 copy-start.3
  9.9 0.2 collective-permute-done.far_slot
  10.1 0.0 collective-permute-done.1.far_offset
  10.1 0.0 collective-permute-done.2.far_forcing
  10.1 2.0 %pack_both.1._ = f32[1536,128]{1,0:T(8,128)} custom-call(f32[768,128]{1,0:T(8,128)S(1)} %pack_own.1.own, s32[1,1024]{1,0:T(1,128)S(1)} %collective-permute-done.far_slot, s32[1,1024]{1,0:T(1,128)S(1)} %collective-permute-done.1.far_offset, f32[3,64,128]{2,1,0:T(8,128)S(1)} %collective-permute-done.2.far_forcing), custom_call_target="tpu_custom_call" | custom-call | flops 1000000000 | bytes 2097152 | tf_op jit(solution)/shard_map/pack_both/pallas_call | solution.py:200
  12.2 4.6 %all-to-all-start = ((f32[16,96,128]{2,1,0:T(8,128)}), f32[16,96,128]{2,1,0:T(8,128)S(1)}, u32[]{:S(2)}, u32[]{:S(2)}) async-start(f32[16,96,128]{2,1,0:T(8,128)} %bitcast), calls=%async_computation | async-start | bytes 1572864 | tf_op jit(solution)/shard_map/all_to_all | solution.py:637
  16.8 0.0 copy-done.6
  16.8 0.1 copy.21.worker
  17.0 0.0 copy-done.4
  17.0 0.0 copy-done.5
  17.0 1.3 %collective-permute-start.4 = (f32[2,4,128]{2,1,0:T(4,128)S(1)}, f32[2,4,128]{2,1,0:T(4,128)S(1)}, u32[]{:S(2)}, u32[]{:S(2)}) collective-permute-start(f32[2,4,128]{2,1,0:T(4,128)S(1)} %get-tuple-element.35), channel_id=1, source_target_pairs={{8,0},{16,8},{24,16},{9,1},{17,9},{25,17},{10,2},{18,10},{26,18},{... | collective-permute-start | bytes 12296 | tf_op jit(solution)/shard_map/ppermute | solution.py:503
  18.3 4.5 %collective-permute-start.3 = (f32[2,4,128]{2,1,0:T(4,128)S(1)}, f32[2,4,128]{2,1,0:T(4,128)S(1)}, u32[]{:S(2)}, u32[]{:S(2)}) collective-permute-start(f32[2,4,128]{2,1,0:T(4,128)S(1)} %get-tuple-element.36), channel_id=1, source_target_pairs={{0,8},{8,16},{16,24},{1,9},{9,17},{17,25},{2,10},{10,18},{18,26},{... | collective-permute-start | bytes 12296 | tf_op jit(solution)/shard_map/ppermute | solution.py:503
  22.9 0.0 copy-done
  22.9 1.9 %segment_plan.1.meta = s32[480,128]{1,0:T(8,128)S(1)} custom-call(s32[480,128]{1,0:T(8,128)S(1)} %copy-done, s32[480,1]{1,0:T(8,128)S(1)} %copy.21.worker), custom_call_target="tpu_custom_call" | custom-call | flops 100000000 | bytes 1048576 | tf_op jit(solution)/shard_map/segment_plan/pallas_call | solution.py:326
  24.8 3.6 %collective-permute-done.4.__ = f32[2,4,128]{2,1,0:T(4,128)S(1)} collective-permute-done((f32[2,4,128]{2,1,0:T(4,128)S(1)}, f32[2,4,128]{2,1,0:T(4,128)S(1)}, u32[]{:S(2)}, u32[]{:S(2)}) %collective-permute-start.4) | collective-permute-done | bytes 4128 | tf_op jit(solution)/shard_map/ppermute | solution.py:503
  28.4 0.0 collective-permute-done.3._
  28.4 1.8 %all-to-all-done = f32[16,96,128]{2,1,0:T(8,128)S(1)} async-done(((f32[16,96,128]{2,1,0:T(8,128)}), f32[16,96,128]{2,1,0:T(8,128)S(1)}, u32[]{:S(2)}, u32[]{:S(2)}) %all-to-all-start) | async-done | bytes 786464 | tf_op jit(solution)/shard_map/all_to_all | solution.py:637
  30.2 0.0 copy-done.1
  30.2 0.0 copy-done.2
  30.2 0.0 copy-done.3
  30.2 0.0 copy-start.8
  30.2 0.0 copy-start.9
  30.2 6.3 %land_sums.1 = (f32[480,128]{1,0:T(8,128)S(1)}, f32[480,128]{1,0:T(8,128)S(1)}, f32[480,128]{1,0:T(8,128)S(1)}, f32[1024,128]{1,0:T(8,128)}) custom-call(s32[480]{0:T(512)S(1)} %copy-done.6, s32[480]{0:T(512)S(1)} %fusion.4.first_rows, f32[1536,128]{1,0:T(8,128)S(1)} %bitcast.7, s32[480,128]{1,0:T(8,128)S(1)} %copy-done, s32[480,128]{1,0:T(8,128)S(1)} %segment_plan.1.meta, ...), custom_call_target="tpu_custom_call" | custom-call | flops 100000000 | bytes 20971520 | tf_op jit(solution)/shard_map/land_sums/pallas_call | solution.py:436
  36.5 3.8 %all-to-all-start.1 = ((f32[32,32,128]{2,1,0:T(8,128)}), f32[32,32,128]{2,1,0:T(8,128)S(1)}, u32[]{:S(2)}, u32[]{:S(2)}) async-start(f32[32,32,128]{2,1,0:T(8,128)} %bitcast.3), calls=%async_computation.1 | async-start | bytes 1048576 | tf_op jit(solution)/shard_map/all_to_all | solution.py:637
  40.3 0.0 copy-done.8
  40.3 0.0 copy-done.9
  40.3 0.7 unpack_plan.1
  41.0 0.1 edge_columns.1
  41.1 2.2 %collective-permute-start.5 = (f32[8,128]{1,0:T(8,128)S(1)}, f32[8,128]{1,0:T(8,128)S(1)}, u32[]{:S(2)}, u32[]{:S(2)}) collective-permute-start(f32[8,128]{1,0:T(8,128)S(1)} %get-tuple-element.28), channel_id=1, source_target_pairs={{0,1},{1,2},{2,3},{3,4},{4,5},{5,6},{6,7},{8,9},{9,10},{10,11},{11... | collective-permute-start | bytes 12296 | tf_op jit(solution)/shard_map/ppermute | solution.py:690
  43.3 1.3 %collective-permute-start.6 = (f32[8,128]{1,0:T(8,128)S(1)}, f32[8,128]{1,0:T(8,128)S(1)}, u32[]{:S(2)}, u32[]{:S(2)}) collective-permute-start(f32[8,128]{1,0:T(8,128)S(1)} %get-tuple-element.29), channel_id=1, source_target_pairs={{1,0},{2,1},{3,2},{4,3},{5,4},{6,5},{7,6},{9,8},{10,9},{11,10},{12... | collective-permute-start | bytes 12296 | tf_op jit(solution)/shard_map/ppermute | solution.py:691
  44.6 0.0 copy-start.7
  44.6 5.1 %new_soil.2 = (f32[15,480,128]{2,1,0:T(8,128)}, f32[480,128]{1,0:T(8,128)}) custom-call(f32[480,128]{1,0:T(8,128)S(1)} %get-tuple-element.20.through, f32[480,128]{1,0:T(8,128)S(1)} %get-tuple-element.21.lost, f32[480,128]{1,0:T(8,128)S(1)} %get-tuple-element.22.canopy, f32[15,480,128]{2,1,0:T(8,128)} %soil.3, f32[15,480,128]{2,1,0:T(8,128)} %porosity.3, ...), custom_call_target="tpu_custom_call" | custom-call | flops 100000000 | bytes 9437184 | tf_op jit(solution)/shard_map/new_soil/pallas_call | solution.py:479
  49.6 0.0 collective-permute-done.5.before
  49.6 0.0 collective-permute-done.6.after
  49.7 0.1 static_halo.1._.fixed
  49.7 6.1 %all-to-all-done.1 = f32[32,32,128]{2,1,0:T(8,128)S(1)} async-done(((f32[32,32,128]{2,1,0:T(8,128)}), f32[32,32,128]{2,1,0:T(8,128)S(1)}, u32[]{:S(2)}, u32[]{:S(2)}) %all-to-all-start.1) | async-done | bytes 524320 | tf_op jit(solution)/shard_map/all_to_all | solution.py:637
  55.9 0.0 copy-done.7
  55.9 1.3 %unpack_runoff.1 = (f32[64,128]{1,0:T(8,128)}, f32[64,128]{1,0:T(8,128)S(1)}, f32[128,128]{1,0:T(8,128)}) custom-call(f32[1024,128]{1,0:T(8,128)S(1)} %bitcast.8, s32[1024,128]{1,0:T(8,128)S(1)} %get-tuple-element.26.code, bf16[64,1024]{1,0:T(8,128)(2,1)S(1)} %get-tuple-element.27.place, f32[64,128]{1,0:T(8,128)S(1)} %copy-done.7, ...), custom_call_target="tpu_custom_call" | custom-call | flops 1000000000 | bytes 1048576 | tf_op jit(solution)/shard_map/unpack_runoff/pallas_call | solution.py:286
  57.2 3.1 %all-to-all-start.2 = ((f32[32,4,128]{2,1,0:T(4,128)}), f32[32,4,128]{2,1,0:T(4,128)S(1)}, u32[]{:S(2)}, u32[]{:S(2)}) async-start(f32[32,4,128]{2,1,0:T(4,128)} %bitcast.5), calls=%async_computation.2 | async-start | bytes 131072 | tf_op jit(solution)/shard_map/all_to_all | solution.py:637
  60.3 3.3 %new_soil.3 = (f32[15,480,128]{2,1,0:T(8,128)}, f32[480,128]{1,0:T(8,128)}) custom-call(f32[480,128]{1,0:T(8,128)S(1)} %get-tuple-element.20.through, f32[480,128]{1,0:T(8,128)S(1)} %get-tuple-element.21.lost, f32[480,128]{1,0:T(8,128)S(1)} %get-tuple-element.22.canopy, f32[15,480,128]{2,1,0:T(8,128)} %soil.3, ...), custom_call_target="tpu_custom_call", output_to_operand_aliasing={{0}: (6, {}), {1}: (7, {})} | custom-call | flops 100000000 | bytes 6291456 | tf_op jit(solution)/shard_map/new_soil/pallas_call | solution.py:479
  63.6 1.2 %unpack_evap.1 = f32[64,128]{1,0:T(8,128)} custom-call(f32[1024,128]{1,0:T(8,128)S(1)} %bitcast.9, s32[1024,128]{1,0:T(8,128)S(1)} %get-tuple-element.26.code, bf16[64,1024]{1,0:T(8,128)(2,1)S(1)} %get-tuple-element.27.place), custom_call_target="tpu_custom_call" | custom-call | flops 1000000000 | bytes 1048576 | tf_op jit(solution)/shard_map/unpack_evap/pallas_call | solution.py:302
  64.8 2.9 %all-to-all-done.2 = f32[32,4,128]{2,1,0:T(4,128)S(1)} async-done(((f32[32,4,128]{2,1,0:T(4,128)}), f32[32,4,128]{2,1,0:T(4,128)S(1)}, u32[]{:S(2)}, u32[]{:S(2)}) %all-to-all-start.2) | async-done | bytes 65568 | tf_op jit(solution)/shard_map/all_to_all | solution.py:637
  67.7 1.2 %river_steps.1 = f32[64,128]{1,0:T(8,128)} custom-call(f32[64,128]{1,0:T(8,128)S(1)} %get-tuple-element.34.state, f32[128,128]{1,0:T(8,128)S(1)} %bitcast.10, f32[2,72,256]{2,1,0:T(8,128)S(1)} %static_halo.1._.fixed, f32[480,128]{1,0:T(8,128)} %get-tuple-element.16._), custom_call_target="tpu_custom_call" | custom-call | flops 10000000 | bytes 1048576 | tf_op jit(solution)/shard_map/river_steps/pallas_call | solution.py:626
  (4 shorter events, 0.1 us)
Async XLA Ops:
  0.6 16.2 %copy-start.6 = (s32[480]{0:T(512)S(1)}, s32[480]{0:T(512)}, u32[]{:S(2)}) copy-start(s32[480]{0:T(512)} %slots.1) | copy-start | bytes 5764
  0.6 9.5 %collective-permute-start.2 = (f32[3,64,128]{2,1,0:T(8,128)}, f32[3,64,128]{2,1,0:T(8,128)S(1)}, u32[]{:S(2)}, u32[]{:S(2)}) collective-permute-start(f32[3,64,128]{2,1,0:T(8,128)} %forcing_in.1), channel_id=1, source_target_pairs={{0,16},{16,0},{1,17},{17,1},{2,18},{18,2},{3,19},{19,3},{4,20},{20... | collective-permute-start | bytes 294920 | tf_op jit(solution)/shard_map/ppermute | solution.py:664
  4.7 5.3 %collective-permute-start = (s32[1,1024]{1,0:T(1,128)}, s32[1,1024]{1,0:T(1,128)S(1)}, u32[]{:S(2)}, u32[]{:S(2)}) collective-permute-start(s32[1,1024]{1,0:T(1,128)} %slot.1), channel_id=1, source_target_pairs={{0,16},{16,0},{1,17},{17,1},{2,18},{18,2},{3,19},{19,3},{4,20},{20... | collective-permute-start | bytes 12296 | tf_op jit(solution)/shard_map/ppermute | solution.py:662
  4.8 5.3 %collective-permute-start.1 = (s32[1,1024]{1,0:T(1,128)}, s32[1,1024]{1,0:T(1,128)S(1)}, u32[]{:S(2)}, u32[]{:S(2)}) collective-permute-start(s32[1,1024]{1,0:T(1,128)} %offset.1), channel_id=1, source_target_pairs={{0,16},{16,0},{1,17},{17,1},{2,18},{18,2},{3,19},{19,3},{4,20},{20... | collective-permute-start | bytes 12296 | tf_op jit(solution)/shard_map/ppermute | solution.py:663
  9.8 7.2 %copy-start.4 = (f32[64,128]{1,0:T(8,128)S(1)}, f32[64,128]{1,0:T(8,128)}, u32[]{:S(2)}) copy-start(f32[64,128]{1,0:T(8,128)} %rate.1) | copy-start | bytes 98308
  9.8 7.2 %copy-start.5 = (s32[64,128]{1,0:T(8,128)S(1)}, s32[64,128]{1,0:T(8,128)}, u32[]{:S(2)}) copy-start(s32[64,128]{1,0:T(8,128)} %code.1) | copy-start | bytes 98308
  9.8 13.1 %copy-start = (s32[480,128]{1,0:T(8,128)S(1)}, s32[480,128]{1,0:T(8,128)}, u32[]{:S(2)}) copy-start(s32[480,128]{1,0:T(8,128)} %cell.3) | copy-start | bytes 737284
  9.8 20.4 %copy-start.1 = (f32[480,128]{1,0:T(8,128)S(1)}, f32[480,128]{1,0:T(8,128)}, u32[]{:S(2)}) copy-start(f32[480,128]{1,0:T(8,128)} %area.1) | copy-start | bytes 737284
  9.8 20.3 %copy-start.2 = (f32[480,128]{1,0:T(8,128)S(1)}, f32[480,128]{1,0:T(8,128)}, u32[]{:S(2)}) copy-start(f32[480,128]{1,0:T(8,128)} %water.1) | copy-start | bytes 737284
  9.8 20.3 %copy-start.3 = (f32[480,128]{1,0:T(8,128)S(1)}, f32[480,128]{1,0:T(8,128)}, u32[]{:S(2)}) copy-start(f32[480,128]{1,0:T(8,128)} %cap.1) | copy-start | bytes 737284
  12.2 18.0 %all-to-all-start = ((f32[16,96,128]{2,1,0:T(8,128)}), f32[16,96,128]{2,1,0:T(8,128)S(1)}, u32[]{:S(2)}, u32[]{:S(2)}) async-start(f32[16,96,128]{2,1,0:T(8,128)} %bitcast), calls=%async_computation | async-start | bytes 1572864 | tf_op jit(solution)/shard_map/all_to_all | solution.py:637
  17.0 11.4 %collective-permute-start.4 = (f32[2,4,128]{2,1,0:T(4,128)S(1)}, f32[2,4,128]{2,1,0:T(4,128)S(1)}, u32[]{:S(2)}, u32[]{:S(2)}) collective-permute-start(f32[2,4,128]{2,1,0:T(4,128)S(1)} %get-tuple-element.35), channel_id=1, source_target_pairs={{8,0},{16,8},{24,16},{9,1},{17,9},{25,17},{10,2},{18,10},{26,18},{... | collective-permute-start | bytes 12296 | tf_op jit(solution)/shard_map/ppermute | solution.py:503
  18.3 10.1 %collective-permute-start.3 = (f32[2,4,128]{2,1,0:T(4,128)S(1)}, f32[2,4,128]{2,1,0:T(4,128)S(1)}, u32[]{:S(2)}, u32[]{:S(2)}) collective-permute-start(f32[2,4,128]{2,1,0:T(4,128)S(1)} %get-tuple-element.36), channel_id=1, source_target_pairs={{0,8},{8,16},{16,24},{1,9},{9,17},{17,25},{2,10},{10,18},{18,26},{... | collective-permute-start | bytes 12296 | tf_op jit(solution)/shard_map/ppermute | solution.py:503
  30.2 10.1 %copy-start.8 = (s32[1,1024]{1,0:T(1,128)S(1)}, s32[1,1024]{1,0:T(1,128)}, u32[]{:S(2)}) copy-start(s32[1,1024]{1,0:T(1,128)} %slot.1) | copy-start | bytes 12292
  30.2 10.1 %copy-start.9 = (s32[1,1024]{1,0:T(1,128)S(1)}, s32[1,1024]{1,0:T(1,128)}, u32[]{:S(2)}) copy-start(s32[1,1024]{1,0:T(1,128)} %offset.1) | copy-start | bytes 12292
  36.5 19.4 %all-to-all-start.1 = ((f32[32,32,128]{2,1,0:T(8,128)}), f32[32,32,128]{2,1,0:T(8,128)S(1)}, u32[]{:S(2)}, u32[]{:S(2)}) async-start(f32[32,32,128]{2,1,0:T(8,128)} %bitcast.3), calls=%async_computation.1 | async-start | bytes 1048576 | tf_op jit(solution)/shard_map/all_to_all | solution.py:637
  41.1 8.5 %collective-permute-start.5 = (f32[8,128]{1,0:T(8,128)S(1)}, f32[8,128]{1,0:T(8,128)S(1)}, u32[]{:S(2)}, u32[]{:S(2)}) collective-permute-start(f32[8,128]{1,0:T(8,128)S(1)} %get-tuple-element.28), channel_id=1, source_target_pairs={{0,1},{1,2},{2,3},{3,4},{4,5},{5,6},{6,7},{8,9},{9,10},{10,11},{11... | collective-permute-start | bytes 12296 | tf_op jit(solution)/shard_map/ppermute | solution.py:690
  43.3 6.4 %collective-permute-start.6 = (f32[8,128]{1,0:T(8,128)S(1)}, f32[8,128]{1,0:T(8,128)S(1)}, u32[]{:S(2)}, u32[]{:S(2)}) collective-permute-start(f32[8,128]{1,0:T(8,128)S(1)} %get-tuple-element.29), channel_id=1, source_target_pairs={{1,0},{2,1},{3,2},{4,3},{5,4},{6,5},{7,6},{9,8},{10,9},{11,10},{12... | collective-permute-start | bytes 12296 | tf_op jit(solution)/shard_map/ppermute | solution.py:691
  44.6 11.3 %copy-start.7 = (f32[64,128]{1,0:T(8,128)S(1)}, f32[64,128]{1,0:T(8,128)}, u32[]{:S(2)}) copy-start(f32[64,128]{1,0:T(8,128)} %river.1) | copy-start | bytes 98308
  57.2 10.5 %all-to-all-start.2 = ((f32[32,4,128]{2,1,0:T(4,128)}), f32[32,4,128]{2,1,0:T(4,128)S(1)}, u32[]{:S(2)}, u32[]{:S(2)}) async-start(f32[32,4,128]{2,1,0:T(4,128)} %bitcast.5), calls=%async_computation.2 | async-start | bytes 131072 | tf_op jit(solution)/shard_map/all_to_all | solution.py:637
